TPU v7x, 32 devices: a whole 2x2x4 slice. The times are simulated.
32 devices in a mesh: dp: 4 (over x, core), ctx: 8 (over z, y).
Axes of the slice: x: 2, y: 2, z: 4, core: 2. Of those that a mesh axis runs over, the one named last changes fastest.
Arguments:
- features: bfloat16 [4, 1024, 6144], P('dp', 'ctx'), may hold values from -6 to 6
- upstream: bfloat16 [4, 1024, 2048], P('dp', 'ctx'), may hold values from -6 to 6
- lengths: int32 [4, 8], P('dp'), may hold values from 1 to 512, 1024 in all within a row
- conv_taps: float32 [3, 6144], replicated, may hold values from -3 to 3
- residues: float32 [16, 2048], P(None, 'ctx'), may hold values from -0.12 to 0.12
- log_rate: float32 [16, 2048], P(None, 'ctx'), may hold values from -13.2 to -3.5
- skip_gain: float32 [2048], P('ctx'), may hold values from -4 to 4
Outputs:
- grad_features: bfloat16 [4, 1024, 6144], P('dp', 'ctx')
- grad_taps: float32 [3, 6144], replicated
- grad_residues: float32 [16, 2048], P(None, 'ctx')
- grad_skip: float32 [2048], P('ctx')
All inputs are finite; a program needn't handle non-finite values.
Results may differ from a plain program's by a relative error of at most 0.0095.
Values may be sent and summed in bfloat16 or wider, within the bound.
No kernel may reach another device: no remote copies, remote signals or barrier semaphores. Data moves between devices by JAX's collectives and lax.ppermute only.
A program may use at most 192 MiB of HBM per device.

v0:
```python
import math

import jax
import jax.numpy as jnp
from jax import lax
from jax.sharding import PartitionSpec as P

BLOCK_ROWS = 128


def from_behind(block, axis, distance):
    devices = range(lax.axis_size(axis))
    route = [(i - distance, i) for i in devices if i - distance in devices]
    return lax.ppermute(block, axis, route)


def segment_of(positions, bounds):
    return jnp.sum((positions[:, None] >= bounds[None, :]).astype(jnp.int32), axis=1)


def segment_masks(positions, bounds, window_len):
    seg_ids = segment_of(positions, bounds)
    keep_one = ((positions >= 1) & (segment_of(positions - 1, bounds) == seg_ids)).astype(
        jnp.float32
    )
    keep_two = ((positions >= 2) & (segment_of(positions - 2, bounds) == seg_ids)).astype(
        jnp.float32
    )
    next_one = (
        (positions + 1 < window_len) & (segment_of(positions + 1, bounds) == seg_ids)
    ).astype(jnp.float32)
    next_two = (
        (positions + 2 < window_len) & (segment_of(positions + 2, bounds) == seg_ids)
    ).astype(jnp.float32)
    return (seg_ids, keep_one, keep_two, next_one, next_two)


def causal_taps(current, before, tap_rows, keep_one, keep_two):
    extended = jnp.concatenate([before, current], axis=0)
    return (
        tap_rows[0] * current
        + tap_rows[1] * (keep_one[:, None] * extended[1:-1])
        + tap_rows[2] * (keep_two[:, None] * extended[:-2])
    )


def transposed_taps(current, after, tap_rows, next_one, next_two):
    extended = jnp.concatenate([current, after], axis=0)
    return (
        tap_rows[0] * current
        + tap_rows[1] * (next_one[:, None] * extended[1:-1])
        + tap_rows[2] * (next_two[:, None] * extended[2:])
    )


def tap_terms(gradient, current, before, keep_one, keep_two):
    extended = jnp.concatenate([before, current], axis=0)
    first = jnp.sum(gradient * current, axis=0)
    second = jnp.sum(gradient * (keep_one[:, None] * extended[1:-1]), axis=0)
    third = jnp.sum(gradient * (keep_two[:, None] * extended[:-2]), axis=0)
    return jnp.stack([first, second, third])


def combine_states(earlier, later):
    return (earlier[0] * later[0], later[0] * earlier[1] + later[1])


def modal_sweep(source, segment_ids, decay_rate, coeff, other):
    length, chan_count = source.shape
    pole_count = decay_rate.shape[0]
    blocks = length // BLOCK_ROWS
    per_step = 4
    groups = blocks // per_step
    offsets = jnp.arange(BLOCK_ROWS, dtype=jnp.float32)
    rising = jnp.exp(decay_rate[None] * offsets[:, None, None])
    falling = jnp.exp(-decay_rate[None] * offsets[:, None, None])
    causal = offsets[:, None] >= offsets[None, :]

    def group_fn(inputs):
        src_blk, seg_blk, other_blk = inputs
        joined_mask = ((seg_blk[:, :, None] == seg_blk[:, None, :]) & causal[None]).astype(
            source.dtype
        )
        lifted = (src_blk[:, :, None, :] * rising[None]).reshape(
            per_step, BLOCK_ROWS, pole_count * chan_count
        )
        inner_state = jnp.einsum(
            "pij,pjk->pik", joined_mask, lifted, precision=lax.Precision.HIGHEST
        )
        inner_state = (
            inner_state.reshape(per_step, BLOCK_ROWS, pole_count, chan_count) * falling[None]
        )
        block_out = jnp.einsum("pimc,mc->pic", inner_state, coeff, precision=lax.Precision.HIGHEST)
        last_row = inner_state[:, -1]
        start_same = (seg_blk == seg_blk[:, :1]).astype(source.dtype)
        partial_sum = jnp.einsum(
            "pic,pimc->mc", other_blk, inner_state, precision=lax.Precision.HIGHEST
        )
        weights = jnp.einsum(
            "pic,imc->pmc",
            other_blk * start_same[:, :, None],
            falling,
            precision=lax.Precision.HIGHEST,
        )
        return (block_out, last_row, partial_sum, weights)

    src_groups = source.reshape(groups, per_step, BLOCK_ROWS, chan_count)
    seg_groups = segment_ids.reshape(groups, per_step, BLOCK_ROWS)
    other_groups = other.reshape(groups, per_step, BLOCK_ROWS, chan_count)
    block_out, last_row, partial_sum, weights = lax.map(
        group_fn, (src_groups, seg_groups, other_groups)
    )
    block_out = block_out.reshape(blocks, BLOCK_ROWS, chan_count)
    last_row = last_row.reshape(blocks, pole_count, chan_count)
    weights = weights.reshape(blocks, pole_count, chan_count)
    seg_rows = segment_ids.reshape(blocks, BLOCK_ROWS)
    starts = seg_rows[:, 0]
    finals = seg_rows[:, -1]
    joined = (starts[1:] == finals[:-1]).astype(source.dtype)
    through = (starts[:-1] == finals[:-1]).astype(source.dtype)
    one_step = jnp.exp(-decay_rate)
    block_decay = jnp.exp(-decay_rate * BLOCK_ROWS)
    factors = (joined * through)[:, None, None] * block_decay[None]
    inputs_in = joined[:, None, None] * one_step[None] * last_row[:-1]
    unused, states = lax.associative_scan(combine_states, (factors, inputs_in))
    carried = jnp.concatenate(
        [jnp.zeros((1, pole_count, chan_count), source.dtype), states], axis=0
    )
    start_rows = (seg_rows == starts[:, None]).astype(source.dtype)
    carry_out = (
        jnp.einsum("kmc,imc->kic", carried * coeff[None], falling, precision=lax.Precision.HIGHEST)
        * start_rows[:, :, None]
    )
    result = (block_out + carry_out).reshape(length, chan_count)
    grad_part = jnp.sum(partial_sum, axis=0) + jnp.einsum(
        "kmc,kmc->mc", weights, carried, precision=lax.Precision.HIGHEST
    )
    return (result, grad_part)


def per_device(features, upstream, lengths, conv_taps, residues, log_rate, skip_gain):
    feats = features[0]
    upf = upstream[0].astype(jnp.float32)
    tok_rows = feats.shape[0]
    channels = upstream.shape[2]
    ctx_count = lax.axis_size("ctx")
    shard_index = lax.axis_index("ctx")
    per_shard = channels // ctx_count
    window_len = tok_rows * ctx_count
    grad_scale = 1.0 / math.sqrt(window_len * lax.axis_size("dp"))
    bounds = jnp.cumsum(lengths[0])[:-1]
    local_pos = shard_index * tok_rows + jnp.arange(tok_rows, dtype=jnp.int32)
    seg_local, keep_one, keep_two, next_one, next_two = segment_masks(local_pos, bounds, window_len)
    whole_pos = jnp.arange(window_len, dtype=jnp.int32)
    seg_all, wkeep_one, wkeep_two, wnext_one, wnext_two = segment_masks(
        whole_pos, bounds, window_len
    )
    decay_rate = jnp.exp(log_rate)
    zero_rows = jnp.zeros((2, per_shard), jnp.float32)
    edge_rows = feats[-2:, :channels]
    before = from_behind(edge_rows, "ctx", 1).astype(jnp.float32)
    src_seq = feats[:, :channels].astype(jnp.float32)
    query_seq = causal_taps(src_seq, before, conv_taps[:, :channels], keep_one, keep_two)
    outgoing = feats[:, channels:].reshape(tok_rows, 2, channels)
    grad_out = (upf * query_seq).astype(jnp.bfloat16)[:, None, :]
    arrived = lax.all_to_all(outgoing, "ctx", split_axis=2, concat_axis=0, tiled=True)
    arrived_grad = lax.all_to_all(grad_out, "ctx", split_axis=2, concat_axis=0, tiled=True)
    tap_cols = lax.dynamic_slice(
        conv_taps.reshape(3, 3, channels), (0, 1, shard_index * per_shard), (3, 2, per_shard)
    )
    key_src = arrived[:, 0].astype(jnp.float32)
    val_src = arrived[:, 1].astype(jnp.float32)
    key_ch = causal_taps(key_src, zero_rows, tap_cols[:, 0], wkeep_one, wkeep_two)
    val_ch = causal_taps(val_src, zero_rows, tap_cols[:, 1], wkeep_one, wkeep_two)
    mixed_ch = (key_ch * val_ch).astype(jnp.bfloat16)
    mixedf = mixed_ch.astype(jnp.float32)
    conv_out, unused = modal_sweep(mixedf, seg_all, decay_rate, residues, jnp.zeros_like(mixedf))
    output_ch = (conv_out + skip_gain * mixedf).astype(jnp.bfloat16)
    gradf = arrived_grad[:, 0].astype(jnp.float32)
    adjoint, grad_resid = modal_sweep(
        gradf[::-1], seg_all[::-1], decay_rate, residues, mixedf[::-1]
    )
    grad_mixed = (adjoint[::-1] + skip_gain * gradf).astype(jnp.bfloat16)
    skip_part = jnp.sum(mixedf * gradf, axis=0)
    dmixf = grad_mixed.astype(jnp.float32)
    grad_key = dmixf * val_ch
    grad_val = dmixf * key_ch
    key_back = transposed_taps(grad_key, zero_rows, tap_cols[:, 0], wnext_one, wnext_two)
    val_back = transposed_taps(grad_val, zero_rows, tap_cols[:, 1], wnext_one, wnext_two)
    second = jnp.stack([key_back, val_back], axis=1).astype(jnp.bfloat16)
    kv_taps = jnp.stack(
        [
            tap_terms(grad_key, key_src, zero_rows, wkeep_one, wkeep_two),
            tap_terms(grad_val, val_src, zero_rows, wkeep_one, wkeep_two),
        ],
        axis=1,
    )
    first = output_ch[:, None, :]
    first_back = lax.all_to_all(first, "ctx", split_axis=0, concat_axis=2, tiled=True)
    second_back = lax.all_to_all(second, "ctx", split_axis=0, concat_axis=2, tiled=True)
    grad_query = upf * first_back[:, 0].astype(jnp.float32)
    rows_next = from_behind(grad_query[:2], "ctx", -1)
    grad_query_feats = transposed_taps(
        grad_query, rows_next, conv_taps[:, :channels], next_one, next_two
    ).astype(jnp.bfloat16)
    grad_feats = jnp.concatenate(
        [grad_query_feats, second_back.reshape(tok_rows, 2 * channels)], axis=1
    )
    placed = (
        jnp.zeros((3, 3, channels), jnp.float32)
        .at[:, 0, :]
        .set(tap_terms(grad_query, src_seq, before, keep_one, keep_two))
    )
    placed = lax.dynamic_update_slice(placed, kv_taps, (0, 1, shard_index * per_shard))
    tap_sum = placed.reshape(3, 3 * channels)
    grad_taps = lax.psum(tap_sum, ("dp", "ctx")) * grad_scale
    resid_sum, skip_sum = lax.psum((grad_resid, skip_part), "dp")
    return (grad_feats[None], grad_taps, resid_sum * grad_scale, skip_sum * grad_scale)


def solution(mesh):
    return jax.shard_map(
        per_device,
        mesh=mesh,
        in_specs=(
            P("dp", "ctx", None),
            P("dp", "ctx", None),
            P("dp", None),
            P(),
            P(None, "ctx"),
            P(None, "ctx"),
            P("ctx"),
        ),
        out_specs=(P("dp", "ctx", None), P(), P(None, "ctx"), P("ctx")),
        check_vma=False,
    )
```

profile of v0, /device:TPU:0, one launch (start us, length us, event | category | flops | bytes accessed | tf_op | source)
XLA Modules:
  0.0 501.0 jit_solution(13167381440553042326)
XLA Ops:
  10.3 5.7 %collective-permute-start.1 = (bf16[2,2048]{0,1:T(8,128)(2,1)}, bf16[2,2048]{0,1:T(8,128)(2,1)}, u32[]{:S(2)}, u32[]{:S(2)}) collective-permute-start(bf16[2,2048]{0,1:T(8,128)(2,1)} %slice.369), channel_id=1, source_target_pairs={{0,1},{1,2},{2,3},{3,4},{4,5},{5,6},{6,7},{8,9},{9,10},{10,11},{11... | collective-permute-start | bytes 24584 | tf_op jit(solution)/shard_map/ppermute | solution.py:14
  18.4 8.3 %collective-permute-done.1 = bf16[2,2048]{0,1:T(8,128)(2,1)} collective-permute-done((bf16[2,2048]{0,1:T(8,128)(2,1)}, bf16[2,2048]{0,1:T(8,128)(2,1)}, u32[]{:S(2)}, u32[]{:S(2)}) %collective-permute-start.1) | collective-permute-done | bytes 8224 | tf_op jit(solution)/shard_map/ppermute | solution.py:14
  29.8 8.9 %copy.385 = bf16[128,1,2048]{0,1,2:T(2,128)(2,1)} copy(bf16[128,1,2048]{0,2,1:T(8,128)(2,1)S(1)} %fusion.55) | data formatting | bytes 1048576 | tf_op jit(solution)/shard_map/broadcast_in_dim | solution.py:165
  39.3 12.6 %reduce.24 = bf16[2048,128]{1,0:T(8,128)(2,1)S(1)} reduce(bf16[2048,1,128]{2,1,0:T(2,128)(2,1)} %bitcast.281, bf16[]{:T(256)} %broadcast.315), dimensions={1}, to_apply=%bitcast.200.reduce_sub_computation | reduce | bytes 1048578
  52.9 7.1 %all-to-all-start.2 = ((bf16[8,2,16384]{2,1,0:T(2,128)(2,1)}), bf16[8,2,16384]{2,1,0:T(2,128)(2,1)S(1)}, u32[]{:S(2)}, u32[]{:S(2)}) async-start(bf16[8,2,16384]{2,1,0:T(2,128)(2,1)} %reshape.465), calls=%async_computation.2 | async-start | bytes 1048576 | tf_op jit(solution)/shard_map/all_to_all | solution.py:167
  60.2 9.5 %copy.271 = bf16[128,2,2048]{0,1,2:T(2,128)(2,1)} copy(bf16[128,2,2048]{0,2,1:T(8,128)(2,1)S(1)} %bitcast.278) | data formatting | bytes 2097152 | tf_op jit(solution)/shard_map/reshape | solution.py:164
  73.6 4.7 all-to-all-start
  83.8 19.0 %all-to-all-done = bf16[128,2,2048]{0,1,2:T(2,128)(2,1)S(1)} async-done(((bf16[128,2,2048]{0,1,2:T(2,128)(2,1)}), bf16[128,2,2048]{0,1,2:T(2,128)(2,1)S(1)}, u32[]{:S(2)}, u32[]{:S(2)}) %all-to-all-start) | async-done | bytes 1048608 | tf_op jit(solution)/shard_map/all_to_all | solution.py:166
  106.5 2.9 multiply_reduce_fusion.3
  111.7 119.2 %while.32 = (s32[]{:T(128)}, f32[2,4,128,256]{2,1,0,3:T(4,128)}, f32[2,4,16,256]{3,2,1,0:T(8,128)}, f32[2,16,256]{2,1,0:T(8,128)S(1)}, f32[2,4,16,256]{3,2,1,0:T...) while((s32[]{:T(128)}, f32[2,4,128,256]{2,1,0,3:T(4,128)}, ...), condition=%wide.region_12.13_spmd.clone, body=%wide.region_11.12_spmd.clone.sunk | while | flops 3260691456 | bytes 128545648 | solution.py:110
  124.3 3.9 mul.1141
  128.2 9.4 %mul.1142 = f32[4,128,4096]{2,1,0:T(8,128)} reshape(f32[4,128,16,256]{3,2,1,0:T(8,128)} %mul.1141) | data formatting | bytes 16777216 | tf_op jit(solution)/shard_map/while/body/eval_jaxpr/mul | solution.py:84
  139.6 7.6 %fusion.88 = f32[4,128,4096]{2,1,0:T(8,128)S(1)} fusion(f32[4,128,4096]{2,1,0:T(8,128)} %mul.1142, f32[128,4096]{1,0:T(8,128)S(1)} %bitcast.259, s32[4,128]{1,0:T(4,128)S(1)} %dynamic-slice_bitcast_fusion.11, pred[128,128]{1,0:T(8,128)(4,1)S(1)} %iota_compare_fusion.8), kind=kOutput, calls=%fused_computation.28.clone.1 | convolution fusion | flops 3223453696 | bytes 18892800 | tf_op jit(solution)/shard_map/while/body/eval_jaxpr/pij,pjk->pik/dot_general | solution.py:87
  147.2 7.1 %copy.406 = f32[64,8,16,256]{3,2,1,0:T(8,128)} copy(f32[64,8,16,256]{3,1,2,0:T(8,128)S(1)} %bitcast.257) | data formatting | bytes 16777216 | tf_op jit(solution)/shard_map/while
  157.4 6.9 %multiply_reduce_fusion.17 = (f32[256,16]{0,1:T(8,128)S(1)}, f32[4,128,16,256]{3,2,0,1:T(8,128)}) fusion(f32[256,128,4]{0,2,1:T(4,128)S(1)} %bitcast.262, f32[128,16,256]{2,1,0:T(8,128)} %copy.404, f32[4,128,16,256]{3,2,1,0:T(8,128)} %bitcast.254), kind=kLoop, calls=%fused_computation.25.clone.1 | loop fusion | flops 6287360 | bytes 19415040 | tf_op jit(solution)/shard_map/while/body/eval_jaxpr/pic,pimc->mc/dot_general | solution.py:96
  164.8 3.5 convolution_bitcast_fusion.2
  169.9 5.7 %multiply_reduce_fusion.18 = f32[256,4,128]{0,1,2:T(4,128)S(1)} fusion(f32[4,128,16,256]{3,2,0,1:T(8,128)} %get-tuple-element.635, f32[256,16]{0,1:T(8,128)S(1)} %bitcast.288), kind=kLoop, calls=%fused_computation.26.clone.1 | loop fusion | flops 4063232 | bytes 8929280 | tf_op jit(solution)/shard_map/while
  177.4 3.9 mul.1141
  181.3 9.4 %mul.1142 = f32[4,128,4096]{2,1,0:T(8,128)} reshape(f32[4,128,16,256]{3,2,1,0:T(8,128)} %mul.1141) | data formatting | bytes 16777216 | tf_op jit(solution)/shard_map/while/body/eval_jaxpr/mul | solution.py:84
  192.7 7.6 %fusion.88 = f32[4,128,4096]{2,1,0:T(8,128)S(1)} fusion(f32[4,128,4096]{2,1,0:T(8,128)} %mul.1142, f32[128,4096]{1,0:T(8,128)S(1)} %bitcast.259, s32[4,128]{1,0:T(4,128)S(1)} %dynamic-slice_bitcast_fusion.11, pred[128,128]{1,0:T(8,128)(4,1)S(1)} %iota_compare_fusion.8), kind=kOutput, calls=%fused_computation.28.clone.1 | convolution fusion | flops 3223453696 | bytes 18892800 | tf_op jit(solution)/shard_map/while/body/eval_jaxpr/pij,pjk->pik/dot_general | solution.py:87
  200.3 7.1 %copy.406 = f32[64,8,16,256]{3,2,1,0:T(8,128)} copy(f32[64,8,16,256]{3,1,2,0:T(8,128)S(1)} %bitcast.257) | data formatting | bytes 16777216 | tf_op jit(solution)/shard_map/while
  210.6 6.9 %multiply_reduce_fusion.17 = (f32[256,16]{0,1:T(8,128)S(1)}, f32[4,128,16,256]{3,2,0,1:T(8,128)}) fusion(f32[256,128,4]{0,2,1:T(4,128)S(1)} %bitcast.262, f32[128,16,256]{2,1,0:T(8,128)} %copy.404, f32[4,128,16,256]{3,2,1,0:T(8,128)} %bitcast.254), kind=kLoop, calls=%fused_computation.25.clone.1 | loop fusion | flops 6287360 | bytes 19415040 | tf_op jit(solution)/shard_map/while/body/eval_jaxpr/pic,pimc->mc/dot_general | solution.py:96
  217.9 3.5 convolution_bitcast_fusion.2
  223.1 5.7 %multiply_reduce_fusion.18 = f32[256,4,128]{0,1,2:T(4,128)S(1)} fusion(f32[4,128,16,256]{3,2,0,1:T(8,128)} %get-tuple-element.635, f32[256,16]{0,1:T(8,128)S(1)} %bitcast.288), kind=kLoop, calls=%fused_computation.26.clone.1 | loop fusion | flops 4063232 | bytes 8929280 | tf_op jit(solution)/shard_map/while
  231.6 68.6 %while.31 = (s32[]{:T(128)}, f32[2,4,128,256]{2,1,0,3:T(4,128)S(1)}, f32[2,4,16,256]{3,2,1,0:T(8,128)S(1)}, s32[2,4,128]{2,1,0:T(4,128)S(1)}, f32[2,4,128,256]{3...) while((s32[]{:T(128)}, ...), condition=%wide.region_5.6_spmd.clone, body=%wide.region_4.5_spmd.clone.sunk | while | flops 3230679040 | bytes 127096960 | solution.py:110
  232.6 3.9 mul.1126
  236.5 9.4 %mul.1127 = f32[4,128,4096]{2,1,0:T(8,128)} reshape(f32[4,128,16,256]{3,2,1,0:T(8,128)} %mul.1126) | data formatting | bytes 16777216 | tf_op jit(solution)/shard_map/while/body/eval_jaxpr/mul | solution.py:84
  249.3 5.4 %fusion.84 = f32[4,128,4096]{2,1,0:T(8,128)S(1)} fusion(f32[4,128,4096]{2,1,0:T(8,128)S(1)} %copy-done, f32[128,4096]{1,0:T(8,128)S(1)} %bitcast.258, s32[4,128]{1,0:T(4,128)S(1)} %dynamic-slice_bitcast_fusion.9, pred[128,128]{1,0:T(8,128)(4,1)S(1)} %iota_compare_fusion.7), kind=kOutput, calls=%fused_computation.8.clone.1 | convolution fusion | flops 3223453696 | bytes 18892800 | tf_op jit(solution)/shard_map/while/body/eval_jaxpr/pij,pjk->pik/dot_general | solution.py:87
  254.8 3.9 copy.400
  258.7 5.8 %multiply_reduce_fusion.16 = (f32[256,4,128]{0,1,2:T(4,128)S(1)}, f32[4,128,16,256]{3,2,0,1:T(8,128)}) fusion(f32[256,16]{0,1:T(8,128)S(1)} %bitcast.289, f32[128,16,256]{2,1,0:T(8,128)S(1)} %get-tuple-element.620, f32[4,128,16,256]{3,2,1,0:T(8,128)S(1)} %bitcast.255), kind=kLoop, calls=%fused_computation.6.clone.1 | loop fusion | flops 6160384 | bytes 19415040 | tf_op jit(solution)/shard_map/while
  266.9 3.9 mul.1126
  270.7 9.4 %mul.1127 = f32[4,128,4096]{2,1,0:T(8,128)} reshape(f32[4,128,16,256]{3,2,1,0:T(8,128)} %mul.1126) | data formatting | bytes 16777216 | tf_op jit(solution)/shard_map/while/body/eval_jaxpr/mul | solution.py:84
  283.5 5.4 %fusion.84 = f32[4,128,4096]{2,1,0:T(8,128)S(1)} fusion(f32[4,128,4096]{2,1,0:T(8,128)S(1)} %copy-done, f32[128,4096]{1,0:T(8,128)S(1)} %bitcast.258, s32[4,128]{1,0:T(4,128)S(1)} %dynamic-slice_bitcast_fusion.9, pred[128,128]{1,0:T(8,128)(4,1)S(1)} %iota_compare_fusion.7), kind=kOutput, calls=%fused_computation.8.clone.1 | convolution fusion | flops 3223453696 | bytes 18892800 | tf_op jit(solution)/shard_map/while/body/eval_jaxpr/pij,pjk->pik/dot_general | solution.py:87
  289.0 3.9 copy.400
  292.9 5.8 %multiply_reduce_fusion.16 = (f32[256,4,128]{0,1,2:T(4,128)S(1)}, f32[4,128,16,256]{3,2,0,1:T(8,128)}) fusion(f32[256,16]{0,1:T(8,128)S(1)} %bitcast.289, f32[128,16,256]{2,1,0:T(8,128)S(1)} %get-tuple-element.620, f32[4,128,16,256]{3,2,1,0:T(8,128)S(1)} %bitcast.255), kind=kLoop, calls=%fused_computation.6.clone.1 | loop fusion | flops 6160384 | bytes 19415040 | tf_op jit(solution)/shard_map/while
  302.8 3.9 fusion.38
  308.3 5.3 %rev.15 = f32[1024,256]{1,0:T(8,128)} reverse(f32[1024,256]{1,0:T(8,128)S(1)} %bitcast.284), dimensions={0} | reverse | bytes 2097152 | tf_op jit(solution)/shard_map/rev | solution.py:183
  314.9 4.6 fusion.37
  319.5 2.6 copy.324
  322.2 2.5 fusion.51
  328.6 3.5 all-to-all-start.1
  335.3 11.4 %all-reduce.15 = (f32[16,256]{1,0:T(8,128)S(1)}, f32[256]{0:T(256)S(1)}) all-reduce(f32[16,256]{1,0:T(8,128)S(1)} %add.272, f32[256]{0:T(256)S(1)} %copy-done.72), channel_id=1, replica_groups=mesh['dp'=4,'ctx'=8] {'dp'}, use_global_device_ids=true, to_apply=%region_26.27 | all-reduce | flops 4352 | bytes 34816 | tf_op jit(solution)/shard_map/psum | solution.py:217
  348.7 5.4 %all-to-all-start.3 = ((bf16[1024,2,256]{2,1,0:T(2,128)(2,1)}), bf16[1024,2,256]{2,1,0:T(2,128)(2,1)}, u32[]{:S(2)}, u32[]{:S(2)}) async-start(bf16[1024,2,256]{2,1,0:T(2,128)(2,1)} %copy.293), calls=%async_computation.3 | async-start | bytes 2097152 | tf_op jit(solution)/shard_map/all_to_all | solution.py:200
  354.2 2.6 reshape.468
  358.7 3.4 multiply_reduce_fusion.11
  365.1 3.1 collective-permute-done
  371.0 117.3 %all-reduce.18.cloned.1.call-done = f32[3,6144]{1,0:T(4,128)} async-done(((f32[3,6144]{1,0:T(4,128)}), f32[3,6144]{1,0:T(4,128)}) %all-reduce.18.cloned.1.call-update) | async-done | bytes 73744 | tf_op jit(solution)/shard_map/psum | solution.py:216
  489.9 2.3 copy.294
  (345 shorter events, 80.4 us)
Async XLA Ops:
  9.1 51.0 %copy-start.9 = (bf16[1,128,6144]{1,2,0:T(8,128)(2,1)}, bf16[1,128,6144]{1,2,0:T(8,128)(2,1)S(1)}, u32[]{:S(2)}) copy-start(bf16[1,128,6144]{1,2,0:T(8,128)(2,1)S(1)} %copy.270) | copy-start | bytes 4718596
  9.1 7.0 %copy-start.80 = (s32[1,8]{1,0:T(1,128)S(1)}, s32[1,8]{1,0:T(1,128)}, u32[]{:S(2)}) copy-start(s32[1,8]{1,0:T(1,128)} %param.15) | copy-start | bytes 100
  9.1 7.2 %copy-start.38 = (f32[3,6144]{1,0:T(4,128)S(1)}, f32[3,6144]{1,0:T(4,128)}, u32[]{:S(2)}) copy-start(f32[3,6144]{1,0:T(4,128)} %param.16) | copy-start | bytes 221188
  10.3 16.3 %collective-permute-start.1 = (bf16[2,2048]{0,1:T(8,128)(2,1)}, bf16[2,2048]{0,1:T(8,128)(2,1)}, u32[]{:S(2)}, u32[]{:S(2)}) collective-permute-start(bf16[2,2048]{0,1:T(8,128)(2,1)} %slice.369), channel_id=1, source_target_pairs={{0,1},{1,2},{2,3},{3,4},{4,5},{5,6},{6,7},{8,9},{9,10},{10,11},{11... | collective-permute-start | bytes 24584 | tf_op jit(solution)/shard_map/ppermute | solution.py:14
  16.1 13.6 %copy-start.16 = (f32[128,2048]{0,1:T(8,128)}, f32[128,2048]{0,1:T(8,128)S(1)}, u32[]{:S(2)}) copy-start(f32[128,2048]{0,1:T(8,128)S(1)} %slice_convert_fusion) | copy-start | bytes 3145732
  16.3 13.4 %copy-start.39 = (f32[1,2048]{1,0:T(1,128)}, f32[1,2048]{1,0:T(1,128)S(1)}, u32[]{:S(2)}) copy-start(f32[1,2048]{1,0:T(1,128)S(1)} %get-tuple-element.476) | copy-start | bytes 24580
  16.3 13.4 %copy-start.41 = (f32[1,2048]{1,0:T(1,128)}, f32[1,2048]{1,0:T(1,128)S(1)}, u32[]{:S(2)}) copy-start(f32[1,2048]{1,0:T(1,128)S(1)} %get-tuple-element.477) | copy-start | bytes 24580
  16.4 13.4 %copy-start.43 = (f32[1,2048]{1,0:T(1,128)}, f32[1,2048]{1,0:T(1,128)S(1)}, u32[]{:S(2)}) copy-start(f32[1,2048]{1,0:T(1,128)S(1)} %get-tuple-element.478) | copy-start | bytes 24580
  17.1 12.7 %copy-start.68 = (f32[128]{0:T(128)}, f32[128]{0:T(128)S(1)}, u32[]{:S(2)}) copy-start(f32[128]{0:T(128)S(1)} %get-tuple-element.496) | copy-start | bytes 1540
  17.1 12.7 %copy-start.70 = (f32[128]{0:T(128)}, f32[128]{0:T(128)S(1)}, u32[]{:S(2)}) copy-start(f32[128]{0:T(128)S(1)} %get-tuple-element.497) | copy-start | bytes 1540
  18.4 11.4 %copy-start.20 = (bf16[1,128,2048]{1,2,0:T(8,128)(2,1)}, bf16[1,128,2048]{1,2,0:T(8,128)(2,1)S(1)}, u32[]{:S(2)}) copy-start(bf16[1,128,2048]{1,2,0:T(8,128)(2,1)S(1)} %copy.269) | copy-start | bytes 1572868
  27.8 11.0 %copy-start.18 = (f32[2,2048]{0,1:T(8,128)}, f32[2,2048]{0,1:T(8,128)S(1)}, u32[]{:S(2)}) copy-start(f32[2,2048]{0,1:T(8,128)S(1)} %convert_element_type.237) | copy-start | bytes 49156
  52.9 20.7 %all-to-all-start.2 = ((bf16[8,2,16384]{2,1,0:T(2,128)(2,1)}), bf16[8,2,16384]{2,1,0:T(2,128)(2,1)S(1)}, u32[]{:S(2)}, u32[]{:S(2)}) async-start(bf16[8,2,16384]{2,1,0:T(2,128)(2,1)} %reshape.465), calls=%async_computation.2 | async-start | bytes 1048576 | tf_op jit(solution)/shard_map/all_to_all | solution.py:167
  60.1 9.8 %copy-start.55 = (f32[16,256]{1,0:T(8,128)S(1)}, f32[16,256]{1,0:T(8,128)}, u32[]{:S(2)}) copy-start(f32[16,256]{1,0:T(8,128)} %param.18) | copy-start | bytes 49156
  69.8 12.1 %copy-start.31 = (s32[1024]{0:T(1024)}, s32[1024]{0:T(1024)S(1)}, u32[]{:S(2)}) copy-start(s32[1024]{0:T(1024)S(1)} %get-tuple-element.397) | copy-start | bytes 12292
  71.6 34.8 %copy-start.56 = (f32[1,1,256]{2,1,0:T(1,128)}, f32[1,1,256]{2,1,0:T(1,128)S(1)}, u32[]{:S(2)}) copy-start(f32[1,1,256]{2,1,0:T(1,128)S(1)} %get-tuple-element.470) | copy-start | bytes 3076
  71.7 34.8 %copy-start.58 = (f32[1,1,256]{2,1,0:T(1,128)}, f32[1,1,256]{2,1,0:T(1,128)S(1)}, u32[]{:S(2)}) copy-start(f32[1,1,256]{2,1,0:T(1,128)S(1)} %get-tuple-element.471) | copy-start | bytes 3076
  71.7 34.8 %copy-start.60 = (f32[1,1,256]{2,1,0:T(1,128)}, f32[1,1,256]{2,1,0:T(1,128)S(1)}, u32[]{:S(2)}) copy-start(f32[1,1,256]{2,1,0:T(1,128)S(1)} %get-tuple-element.472) | copy-start | bytes 3076
  71.7 34.8 %copy-start.62 = (f32[1,1,256]{2,1,0:T(1,128)}, f32[1,1,256]{2,1,0:T(1,128)S(1)}, u32[]{:S(2)}) copy-start(f32[1,1,256]{2,1,0:T(1,128)S(1)} %get-tuple-element.473) | copy-start | bytes 3076
  71.7 34.8 %copy-start.64 = (f32[1,1,256]{2,1,0:T(1,128)}, f32[1,1,256]{2,1,0:T(1,128)S(1)}, u32[]{:S(2)}) copy-start(f32[1,1,256]{2,1,0:T(1,128)S(1)} %get-tuple-element.474) | copy-start | bytes 3076
  71.7 34.8 %copy-start.66 = (f32[1,1,256]{2,1,0:T(1,128)}, f32[1,1,256]{2,1,0:T(1,128)S(1)}, u32[]{:S(2)}) copy-start(f32[1,1,256]{2,1,0:T(1,128)S(1)} %get-tuple-element.475) | copy-start | bytes 3076
  72.3 10.7 %copy-start.75 = (f32[7]{0:T(128)}, f32[7]{0:T(128)S(1)}, u32[]{:S(2)}) copy-start(f32[7]{0:T(128)S(1)} %convert_reduce_fusion.5) | copy-start | bytes 88
  73.6 29.3 %all-to-all-start = ((bf16[128,2,2048]{0,1,2:T(2,128)(2,1)}), bf16[128,2,2048]{0,1,2:T(2,128)(2,1)S(1)}, u32[]{:S(2)}, u32[]{:S(2)}) async-start(bf16[128,2,2048]{0,1,2:T(2,128)(2,1)} %copy.271), calls=%async_computation | async-start | bytes 2097152 | tf_op jit(solution)/shard_map/all_to_all | solution.py:166
  80.5 25.9 %copy-start.46 = (f32[1024]{0:T(1024)}, f32[1024]{0:T(1024)S(1)}, u32[]{:S(2)}) copy-start(f32[1024]{0:T(1024)S(1)} %get-tuple-element.491) | copy-start | bytes 12292
  80.6 25.9 %copy-start.48 = (f32[1024]{0:T(1024)}, f32[1024]{0:T(1024)S(1)}, u32[]{:S(2)}) copy-start(f32[1024]{0:T(1024)S(1)} %get-tuple-element.492) | copy-start | bytes 12292
  83.4 23.1 %copy-start.3 = (f32[128,1,8,256]{3,0,2,1:T(8,128)}, f32[128,1,8,256]{3,0,2,1:T(8,128)S(1)}, u32[]{:S(2)}) copy-start(f32[128,1,8,256]{3,0,2,1:T(8,128)S(1)} %copy.287) | copy-start | bytes 3145732
  111.6 119.4 %copy-start.30 = (f32[16,256]{1,0:T(8,128)S(1)}, f32[16,256]{1,0:T(8,128)}, u32[]{:S(2)}) copy-start(f32[16,256]{1,0:T(8,128)} %copy.275) | copy-start | bytes 49156
  111.7 119.4 %copy-start.32 = (s32[1024]{0:T(1024)S(1)}, s32[1024]{0:T(1024)}, u32[]{:S(2)}) copy-start(s32[1024]{0:T(1024)} %copy-done.31) | copy-start | bytes 12292
  124.3 30.0 %copy-start.7 = (f32[2,4,128,256]{3,2,1,0:T(8,128)}, f32[2,4,128,256]{3,2,1,0:T(8,128)S(1)}, u32[]{:S(2)}) copy-start(f32[2,4,128,256]{3,2,1,0:T(8,128)S(1)} %get-tuple-element.698) | copy-start | bytes 3145732 | tf_op jit(solution)/shard_map/while
  177.4 30.0 %copy-start.7 = (f32[2,4,128,256]{3,2,1,0:T(8,128)}, f32[2,4,128,256]{3,2,1,0:T(8,128)S(1)}, u32[]{:S(2)}) copy-start(f32[2,4,128,256]{3,2,1,0:T(8,128)S(1)} %get-tuple-element.698) | copy-start | bytes 3145732 | tf_op jit(solution)/shard_map/while
  231.1 69.0 %copy-start.37 = (f32[2,4,16,256]{3,2,1,0:T(8,128)S(1)}, f32[2,4,16,256]{3,2,1,0:T(8,128)}, u32[]{:S(2)}) copy-start(f32[2,4,16,256]{3,2,1,0:T(8,128)} %get-tuple-element.132) | copy-start | bytes 393220
  231.1 69.0 %copy-start.45 = (f32[16,256]{1,0:T(8,128)S(1)}, f32[16,256]{1,0:T(8,128)}, u32[]{:S(2)}) copy-start(f32[16,256]{1,0:T(8,128)} %copy.277) | copy-start | bytes 49156
  231.1 69.0 %copy-start.76 = (f32[7]{0:T(128)S(1)}, f32[7]{0:T(128)}, u32[]{:S(2)}) copy-start(f32[7]{0:T(128)} %copy-done.75) | copy-start | bytes 88
  231.1 69.0 %copy-start.78 = (f32[7]{0:T(128)S(1)}, f32[7]{0:T(128)}, u32[]{:S(2)}) copy-start(f32[7]{0:T(128)} %copy-done.77) | copy-start | bytes 88
  231.1 69.1 %copy-start.29 = (f32[7,16,256]{2,1,0:T(8,128)S(1)}, f32[7,16,256]{2,1,0:T(8,128)}, u32[]{:S(2)}) copy-start(f32[7,16,256]{2,1,0:T(8,128)} %get-tuple-element.484) | copy-start | bytes 344068
  231.2 69.2 %copy-start.28 = (f32[7,16,256]{2,1,0:T(8,128)S(1)}, f32[7,16,256]{2,1,0:T(8,128)}, u32[]{:S(2)}) copy-start(f32[7,16,256]{2,1,0:T(8,128)} %get-tuple-element.483) | copy-start | bytes 344068
  308.3 6.6 %copy-start.54 = (f32[8,128]{1,0:T(8,128)S(1)}, f32[8,128]{1,0:T(8,128)}, u32[]{:S(2)}) copy-start(f32[8,128]{1,0:T(8,128)} %compare_convert_fusion.2) | copy-start | bytes 12292
  314.9 7.2 %copy-start.2 = (f32[2,4,128,256]{3,2,1,0:T(8,128)S(1)}, f32[2,4,128,256]{3,2,1,0:T(8,128)}, u32[]{:S(2)}) copy-start(f32[2,4,128,256]{3,2,1,0:T(8,128)} %get-tuple-element.703) | copy-start | bytes 3145732
  314.9 7.2 %copy-start.4 = (f32[128,1,8,256]{3,0,2,1:T(8,128)S(1)}, f32[128,1,8,256]{3,0,2,1:T(8,128)}, u32[]{:S(2)}) copy-start(f32[128,1,8,256]{3,0,2,1:T(8,128)} %copy-done.3) | copy-start | bytes 3145732
  314.9 7.2 %copy-start.79 = (f32[256]{0:T(256)S(1)}, f32[256]{0:T(256)}, u32[]{:S(2)}) copy-start(f32[256]{0:T(256)} %param.19) | copy-start | bytes 3076
  314.9 9.8 %copy-start.49 = (f32[1024]{0:T(1024)S(1)}, f32[1024]{0:T(1024)}, u32[]{:S(2)}) copy-start(f32[1024]{0:T(1024)} %copy-done.48) | copy-start | bytes 12292
  328.6 19.3 %all-to-all-start.1 = ((bf16[8,2,16384]{2,1,0:T(2,128)(2,1)}), bf16[8,2,16384]{2,1,0:T(2,128)(2,1)S(1)}, u32[]{:S(2)}, u32[]{:S(2)}) async-start(bf16[8,2,16384]{2,1,0:T(2,128)(2,1)} %reshape.467), calls=%async_computation.1 | async-start | bytes 1048576 | tf_op jit(solution)/shard_map/all_to_all | solution.py:199
  348.7 141.1 %all-to-all-start.3 = ((bf16[1024,2,256]{2,1,0:T(2,128)(2,1)}), bf16[1024,2,256]{2,1,0:T(2,128)(2,1)}, u32[]{:S(2)}, u32[]{:S(2)}) async-start(bf16[1024,2,256]{2,1,0:T(2,128)(2,1)} %copy.293), calls=%async_computation.3 | async-start | bytes 2097152 | tf_op jit(solution)/shard_map/all_to_all | solution.py:200
  354.2 134.1 %all-reduce.18.cloned.1.call-start = ((), (), s32[]{:S(2)}) async-start(), calls=%async_computation.4 | async-start | bytes 196608 | tf_op jit(solution)/shard_map/psum | solution.py:216
  362.1 6.4 %copy-start.40 = (f32[1,2048]{1,0:T(1,128)S(1)}, f32[1,2048]{1,0:T(1,128)}, u32[]{:S(2)}) copy-start(f32[1,2048]{1,0:T(1,128)} %copy-done.39) | copy-start | bytes 24580
  362.2 6.4 %copy-start.42 = (f32[1,2048]{1,0:T(1,128)S(1)}, f32[1,2048]{1,0:T(1,128)}, u32[]{:S(2)}) copy-start(f32[1,2048]{1,0:T(1,128)} %copy-done.41) | copy-start | bytes 24580
  362.2 6.4 %copy-start.44 = (f32[1,2048]{1,0:T(1,128)S(1)}, f32[1,2048]{1,0:T(1,128)}, u32[]{:S(2)}) copy-start(f32[1,2048]{1,0:T(1,128)} %copy-done.43) | copy-start | bytes 24580
  362.5 5.7 %collective-permute-start = (f32[2,2048]{1,0:T(2,128)S(1)}, f32[2,2048]{1,0:T(2,128)S(1)}, u32[]{:S(2)}, u32[]{:S(2)}) collective-permute-start(f32[2,2048]{1,0:T(2,128)S(1)} %copy.283), channel_id=1, source_target_pairs={{1,0},{2,1},{3,2},{4,3},{5,4},{6,5},{7,6},{9,8},{10,9},{11,10},{12... | collective-permute-start | bytes 49160 | tf_op jit(solution)/shard_map/ppermute | solution.py:14
  (47 other events, 155.2 us)
Sparse Core Ops, SparseCore 0:
  365.2 123.0 all-reduce.17
where the time goes:
time: 505 us; the launch traced here: 501 us
  local copies, waits for them, and re-layouts  162 us (32%)
  waiting for transfers between devices  149 us (30%)
  other arithmetic  80.7 us (16%)
  matrix products  41.4 us (8%)
  starting transfers between devices  27.7 us (5%)
  between operations  15.7 us (3%)
  loops' own time  13.5 us (3%)
  blocking collectives  11.4 us (2%)
    psum x1, waiting for transfers between devices, per_device(): grad_taps = lax.psum(tap_sum, ('dp', 'ctx')) * grad_scale  117 us
    mul x12, local copies, waits for them, and re-layouts, group_fn(): src_blk[:, :, None, :] * rising[None]  55.3 us
    while x38, local copies, waits for them, and re-layouts  33.9 us
    dot_general x4, matrix products, group_fn(): jnp.einsum('pij,pjk->pik', joined_mask, lifted, precision=lax.Precision.H...  26 us
    while x4, other arithmetic  23 us
    all_to_all x1, waiting for transfers between devices, per_device(): lax.all_to_all(outgoing, 'ctx', split_axis=2, concat_axis=0, tiled=True)  19 us
    dot_general x2, other arithmetic, group_fn(): jnp.einsum('pic,pimc->mc', other_blk, inner_state, precision=lax.Precisio...  13.8 us
    another operation x2, loops' own time, modal_sweep(): lax.map(group_fn, (src_groups, seg_groups, other_groups))  13.5 us
  transfers between devices with their start and end apart: 7, of which 5 were waited for; matrix products, arithmetic and copies ran while one was open for 8% of the time, Pallas kernels for 0%

commit v1 on v0

v1 whole, which is shorter than its diff:
```python
import functools
import math

import jax
import jax.numpy as jnp
from jax import lax
from jax.experimental import pallas as pl
from jax.experimental.pallas import tpu as pltpu
from jax.sharding import PartitionSpec as P

F32 = jnp.float32
BF16 = jnp.bfloat16
LANES = 128
SUB = 8
GROUP = SUB * LANES
HALO = 2


def shifted(block, axis, distance):
    count = lax.axis_size(axis)
    route = [(i - distance, i) for i in range(count) if 0 <= i - distance < count]
    return lax.ppermute(block, axis, route)


def vec(ref, index):
    return ref[pl.ds(pl.multiple_of(index * SUB, SUB), SUB), :]


def put(ref, index, value):
    ref[pl.ds(pl.multiple_of(index * SUB, SUB), SUB), :] = value


def spread(dst, first, src, rows):
    for j in range(SUB):
        value = src[:, j * LANES : (j + 1) * LANES].astype(F32)
        dst[pl.ds(first * SUB + j, rows, stride=SUB), :] = value


def spread_rows(dst, first, src, rows):
    def step(i, carry):
        for j in range(SUB):
            value = src[0, pl.ds(pl.multiple_of(i * 16, 16), 16), j * LANES : (j + 1) * LANES]
            dst[pl.ds((i * 16 + first) * SUB + j, 16, stride=SUB), :] = value.astype(F32)
        return carry

    lax.fori_loop(0, rows // 16, step, 0)


def spread_params(dst, par, rows):
    pieces, _, width = par.shape
    for j in range(SUB):
        if width >= LANES:
            per = width // LANES
            at = (j % per) * LANES
            parts = [(j // per, at, LANES)]
        else:
            per = LANES // width
            parts = [(j * per + i, 0, width) for i in range(per)]
        for first in range(0, rows, SUB):
            many = min(SUB, rows - first)
            got = [par[k, first : first + many, at : at + w] for k, at, w in parts]
            value = got[0] if len(got) == 1 else jnp.concatenate(got, axis=1)
            dst[pl.ds(first * SUB + j, many, stride=SUB), :] = value


def segment_starts(lengths):
    starts = [jnp.int32(0)]
    for j in range(lengths.shape[1]):
        starts.append(starts[-1] + lengths[0, j])
    return starts


def fill_keep(keep, starts, base, rows):
    count = rows + HALO + 2

    def step(i, carry):
        keep[i] = jnp.float32(1.0)
        return carry

    lax.fori_loop(0, count, step, 0, unroll=4)
    for start in starts:
        at = start - base + 1

        @pl.when((at >= 0) & (at < count))
        def _():
            keep[at] = jnp.float32(0.0)


def load_inputs(cur, left, right, taps, feat_scr, tap_scr, up_scr, rows):
    for third in range(3):
        spread_rows(feat_scr[third], HALO, cur[third], rows)
        spread(feat_scr[third], 0, left[third], HALO)
        spread(feat_scr[third], rows + HALO, right[third], HALO)
        spread(tap_scr[third], 0, taps[third], 3)
    spread_rows(up_scr, 0, cur[3], rows)
    spread(up_scr, rows, right[3], HALO)


def featured(feat, taps, p, keep_one, keep_two):
    return (
        taps[0] * vec(feat, p + 2)
        + taps[1] * (keep_one * vec(feat, p + 1))
        + taps[2] * (keep_two * vec(feat, p))
    )


def rounded(value):
    return value.astype(BF16).astype(F32)


def ends_kernel(rows, count, lengths, *refs):
    cur, left, right, taps = refs[0:4], refs[4:7], refs[7:11], refs[11:14]
    par, out = refs[14], refs[15]
    feat_scr, up_scr, tap_scr = refs[16:19], refs[19], refs[20:23]
    par_scr, mixed_scr, gout_scr, stack, keep = refs[23:28]
    me = lax.axis_index("ctx")
    base = me * rows
    poles = (par.shape[1] - 1) // 2
    starts = segment_starts(lengths)
    fill_keep(keep, starts, base, rows)
    load_inputs(cur, left, right, taps, feat_scr, tap_scr, up_scr, rows)
    spread_params(par_scr, par, poles)
    tap = [[vec(tap_scr[third], j) for j in range(3)] for third in range(3)]

    def product(p, carry):
        keep_one = keep[p + 1]
        keep_two = keep_one * keep[p]
        query, key, val = (featured(feat_scr[i], tap[i], p, keep_one, keep_two) for i in range(3))
        put(mixed_scr, p, rounded(key * val))
        put(gout_scr, p, rounded(vec(up_scr, p) * query))
        return carry

    lax.fori_loop(0, rows + HALO, product, 0, unroll=2)
    low, high = jnp.int32(0), jnp.int32(rows + HALO)
    for start in starts:
        at = start - base
        low = jnp.where(at < rows, jnp.maximum(low, at), low)
        high = jnp.where(at > HALO, jnp.minimum(high, at), high)
    decay = [jnp.exp(-jnp.exp(vec(par_scr, m))) for m in range(poles)]

    def sweep(i, carry):
        state, adjoint = carry
        back = rows + HALO - 1 - i
        x = vec(mixed_scr, i) * jnp.where(i >= low, 1.0, 0.0).astype(F32)
        g = vec(gout_scr, back) * jnp.where(back < high, 1.0, 0.0).astype(F32)
        state = [decay[m] * state[m] + x for m in range(poles)]
        adjoint = [decay[m] * adjoint[m] + g for m in range(poles)]
        return state, adjoint

    zeros = [jnp.zeros((SUB, LANES), F32)] * poles
    state, adjoint = lax.fori_loop(0, rows, sweep, (zeros, zeros), unroll=2)
    for m in range(0, poles, 2):
        at = slice(m * SUB, (m + 2) * SUB)
        stack[0, at, :] = jnp.concatenate(state[m : m + 2], axis=0).astype(BF16)
        stack[1, at, :] = jnp.concatenate(adjoint[m : m + 2], axis=0).astype(BF16)
    for e in range(count):
        out[e, 0] = stack[jnp.where(e > me, 0, 1)]


def main_kernel(rows, count, lengths, *refs):
    cur, left, right, taps = refs[0:4], refs[4:7], refs[7:11], refs[11:14]
    par, arrived, grads, sums = refs[14], refs[15], refs[16], refs[17]
    feat_scr, up_scr, tap_scr = refs[18:21], refs[21], refs[22:25]
    par_scr, mixed_scr, gout_scr, conv_scr, adj_scr = refs[25:30]
    post_scr, zero_scr, keep = refs[30:33], refs[33], refs[34]
    me = lax.axis_index("ctx")
    half = pl.program_id(0)
    groups = pl.num_programs(0)
    base = me * rows
    poles = (par.shape[1] - 1) // 2
    extended = rows + HALO
    starts = segment_starts(lengths)
    fill_keep(keep, starts, base, rows)
    load_inputs(cur, left, right, taps, feat_scr, tap_scr, up_scr, rows)
    spread_params(par_scr, par, 2 * poles + 1)
    tap = [[vec(tap_scr[third], j) for j in range(3)] for third in range(3)]

    def product(p, carry):
        keep_one = keep[p + 1]
        keep_two = keep_one * keep[p]
        query, key, val = (featured(feat_scr[i], tap[i], p, keep_one, keep_two) for i in range(3))
        put(mixed_scr, p, rounded(key * val))
        put(gout_scr, p, rounded(vec(up_scr, p) * query))
        put(post_scr[1], p, val)
        put(post_scr[2], p, key)
        return carry

    lax.fori_loop(0, extended, product, 0, unroll=2)

    first, last = jnp.int32(0), jnp.int32(2**30)
    after = base + extended
    for start in starts:
        first = jnp.where(start <= base, jnp.maximum(first, start), first)
        last = jnp.where(start > after, jnp.minimum(last, start), last)
    per_pass = poles // 2
    zero_scr[...] = jnp.zeros((SUB, LANES), F32)
    zero = zero_scr[...]
    for part in range(2):
        chosen = list(range(part * per_pass, (part + 1) * per_pass))
        rate = [jnp.exp(vec(par_scr, m)) for m in chosen]
        block = [jnp.exp(-rows * r) for r in rate]
        zeros = [zero] * per_pass

        def arrived_states(d):
            got = []
            for m in range(chosen[0], chosen[-1] + 1, 2):
                pair = arrived[d, 0, m * SUB : (m + 2) * SUB, :].astype(F32)
                got += [pair[:SUB], pair[SUB:]]
            return got

        def from_before(d, carry):
            joined = jnp.where((d + 1) * rows - 1 >= first, 1.0, 0.0).astype(F32)
            got = arrived_states(d)
            return [block[i] * carry[i] + joined * got[i] for i in range(per_pass)]

        def from_after(i, carry):
            d = count - 1 - i
            joined = jnp.where(d * rows + HALO < last, 1.0, 0.0).astype(F32)
            got = arrived_states(d)
            return [block[i] * carry[i] + joined * got[i] for i in range(per_pass)]

        state = lax.fori_loop(0, me, from_before, zeros)
        adjoint = lax.fori_loop(0, count - 1 - me, from_after, zeros)
        decay = [jnp.exp(-r) for r in rate]
        coeff = [vec(par_scr, poles + m) for m in chosen]

        def sweep(i, carry):
            state, adjoint, resid = carry
            back = extended - 1 - i
            x = vec(mixed_scr, i)
            g = vec(gout_scr, back)
            own = vec(mixed_scr, back) * jnp.where(back < rows, 1.0, 0.0).astype(F32)
            keep_fwd = keep[i + 1]
            keep_bwd = keep[back + 2]
            state = [decay[m] * (state[m] * keep_fwd) + x for m in range(per_pass)]
            adjoint = [decay[m] * (adjoint[m] * keep_bwd) + g for m in range(per_pass)]
            resid = [resid[m] + own * adjoint[m] for m in range(per_pass)]
            conv = sum(coeff[m] * state[m] for m in range(per_pass))
            adj = sum(coeff[m] * adjoint[m] for m in range(per_pass))
            if part == 0:
                put(conv_scr, i, conv)
                put(adj_scr, back, adj)
            else:
                put(conv_scr, i, conv + vec(conv_scr, i))
                put(adj_scr, back, adj + vec(adj_scr, back))
            return state, adjoint, resid

        _, _, resid = lax.fori_loop(0, extended, sweep, (state, adjoint, zeros), unroll=2)
        for i, m in enumerate(chosen):
            at = (9 + m) * groups * SUB + half * SUB
            sums[pl.ds(pl.multiple_of(at, SUB), SUB), :] = resid[i]

    gain = vec(par_scr, 2 * poles)

    def finish(i, carry):
        one, two, tap_sums, skip_sum = carry
        p = extended - 1 - i
        own = jnp.where(p < rows, 1.0, 0.0).astype(F32)
        x = vec(mixed_scr, p)
        g = vec(gout_scr, p)
        conv = rounded(vec(conv_scr, p) + gain * x)
        grad_mixed = rounded(vec(adj_scr, p) + gain * g)
        val, key = vec(post_scr[1], p), vec(post_scr[2], p)
        post = [vec(up_scr, p) * conv, grad_mixed * val, grad_mixed * key]
        keep_one = keep[p + 1]
        keep_two = keep_one * keep[p]
        next_one = keep[p + 2]
        next_two = next_one * keep[jnp.minimum(p + 3, extended + 1)]
        new_sums = []
        for third in range(3):
            back = (
                tap[third][0] * post[third]
                + tap[third][1] * (next_one * one[third])
                + tap[third][2] * (next_two * two[third])
            )
            put(post_scr[third], p, back)
            mine = post[third] * own
            new_sums += [
                tap_sums[3 * third] + mine * vec(feat_scr[third], p + 2),
                tap_sums[3 * third + 1] + mine * (keep_one * vec(feat_scr[third], p + 1)),
                tap_sums[3 * third + 2] + mine * (keep_two * vec(feat_scr[third], p)),
            ]
        return post, one, new_sums, skip_sum + own * (x * g)

    _, _, tap_sums, skip_sum = lax.fori_loop(
        0, extended, finish, ([zero] * 3, [zero] * 3, [zero] * 9, zero), unroll=2
    )
    for third in range(3):
        for j in range(3):
            at = (3 * j + third) * groups * SUB + half * SUB
            sums[pl.ds(pl.multiple_of(at, SUB), SUB), :] = tap_sums[3 * third + j]
    at = (9 + poles) * groups * SUB + half * SUB
    sums[pl.ds(pl.multiple_of(at, SUB), SUB), :] = skip_sum

    def write(i, carry):
        for third in range(3):
            for j in range(SUB):
                value = post_scr[third][pl.ds(i * 16 * SUB + j, 16, stride=SUB), :]
                column = (third * groups + half) * GROUP + j * LANES
                grads[
                    0,
                    pl.ds(pl.multiple_of(i * 16, 16), 16),
                    pl.ds(pl.multiple_of(column, LANES), LANES),
                ] = value.astype(BF16)
        return carry

    lax.fori_loop(0, rows // 16, write, 0)


def per_device(features, upstream, lengths, conv_taps, residues, log_rate, skip_gain):
    rows = features.shape[1]
    channels = upstream.shape[2]
    poles = residues.shape[0]
    ctx_count = lax.axis_size("ctx")
    total = ctx_count * lax.axis_size("dp")
    shard_index = lax.axis_index("ctx")
    per_shard = channels // ctx_count
    groups = channels // GROUP
    grad_scale = 1.0 / math.sqrt(rows * ctx_count * lax.axis_size("dp"))
    extended = rows + HALO

    edge = features[0, rows - HALO :, :]
    head = jnp.concatenate([features[0, :HALO, :], upstream[0, :HALO, :]], axis=1)
    left = shifted(edge, "ctx", 1)
    right = shifted(head, "ctx", -1)
    params = jnp.concatenate([log_rate, residues, skip_gain[None]], axis=0)
    params = lax.all_to_all(
        jnp.broadcast_to(params[None], (ctx_count,) + params.shape),
        "ctx",
        split_axis=0,
        concat_axis=0,
        tiled=True,
    )

    def row_spec(third):
        return pl.BlockSpec((1, rows, GROUP), lambda h: (0, 0, third * groups + h))

    def edge_spec(height, third):
        return pl.BlockSpec((height, GROUP), lambda h: (0, third * groups + h))

    in_specs = (
        [pl.BlockSpec(memory_space=pltpu.SMEM)]
        + [row_spec(0), row_spec(1), row_spec(2), row_spec(0)]
        + [edge_spec(HALO, i) for i in range(3)]
        + [edge_spec(HALO, i) for i in range(4)]
        + [edge_spec(3, i) for i in range(3)]
        + [
            pl.BlockSpec(
                (ctx_count // groups, 2 * poles + 1, per_shard), lambda h: (h, 0, 0)
            )
        ]
    )
    operands = (
        [lengths]
        + [features, features, features, upstream]
        + [left] * 3
        + [right] * 4
        + [conv_taps] * 3
        + [params]
    )

    def tall(height):
        return pltpu.VMEM((height * SUB, LANES), F32)

    common = (
        [tall(rows + 2 * HALO)] * 3
        + [tall(extended)]
        + [tall(3)] * 3
        + [tall(2 * poles + 1)]
        + [tall(extended)] * 2
    )
    keep = pltpu.SMEM((rows + 8,), F32)
    limits = pltpu.CompilerParams(
        dimension_semantics=("arbitrary",), vmem_limit_bytes=40 * 1024 * 1024
    )
    state_rows = poles * SUB
    ends = pl.pallas_call(
        functools.partial(ends_kernel, rows, ctx_count),
        out_shape=jax.ShapeDtypeStruct((ctx_count, groups, state_rows, LANES), BF16),
        grid=(groups,),
        in_specs=in_specs,
        out_specs=pl.BlockSpec((ctx_count, 1, state_rows, LANES), lambda h: (0, h, 0, 0)),
        scratch_shapes=common + [pltpu.VMEM((2, state_rows, LANES), BF16), keep],
        compiler_params=limits,
        name="ends",
    )(*operands)
    arrived = lax.all_to_all(ends, "ctx", split_axis=0, concat_axis=0, tiled=True)

    used = (10 + poles) * groups * SUB
    share = -(-used // (total * SUB)) * SUB
    grads, sums = pl.pallas_call(
        functools.partial(main_kernel, rows, ctx_count),
        out_shape=(
            jax.ShapeDtypeStruct(features.shape, BF16),
            jax.ShapeDtypeStruct((total * share, LANES), F32),
        ),
        grid=(groups,),
        in_specs=in_specs
        + [pl.BlockSpec((ctx_count, 1, state_rows, LANES), lambda h: (0, h, 0, 0))],
        out_specs=(
            pl.BlockSpec(features.shape, lambda h: (0, 0, 0)),
            pl.BlockSpec((total * share, LANES), lambda h: (0, 0)),
        ),
        scratch_shapes=common + [tall(extended)] * 5 + [tall(1), keep],
        compiler_params=limits,
        name="main",
    )(*operands, arrived)

    both = ("dp", "ctx")
    parts = lax.all_to_all(
        sums.reshape(total, share, LANES), both, split_axis=0, concat_axis=0, tiled=True
    )
    mine = jnp.sum(parts, axis=0) * grad_scale
    whole = lax.all_to_all(
        jnp.broadcast_to(mine[None], parts.shape), both, split_axis=0, concat_axis=0, tiled=True
    ).reshape(total * share, LANES)
    width = groups * SUB
    grad_taps = whole[: 9 * width].reshape(3, 3 * channels)
    rest = whole[9 * width : used].reshape(poles + 1, channels)
    rest = lax.dynamic_slice(rest, (0, shard_index * per_shard), (poles + 1, per_shard))
    return grads, grad_taps, rest[:poles], rest[poles]


def solution(mesh):
    return jax.shard_map(
        per_device,
        mesh=mesh,
        in_specs=(
            P("dp", "ctx", None),
            P("dp", "ctx", None),
            P("dp", None),
            P(),
            P(None, "ctx"),
            P(None, "ctx"),
            P("ctx"),
        ),
        out_specs=(P("dp", "ctx", None), P(), P(None, "ctx"), P("ctx")),
        check_vma=False,
    )
```

time: 505 us -> 101 us (0.20)
  local copies, waits for them, and re-layouts: 162 us -> 8.12 us
  waiting for transfers between devices: 149 us -> 13.7 us
  other arithmetic: 80.7 us -> 0.88 us
  matrix products: 41.4 us -> 0 us
  Pallas kernels: 0 us -> 28.9 us
  blocking collectives: 11.4 us -> 32.6 us
  between operations: 15.7 us -> 0.72 us
  loops' own time: 13.5 us -> 0 us
  starting transfers between devices: 27.7 us -> 15.7 us
    psum x1 -> x0, waiting for transfers between devices: 117 us -> none  [per_device(): grad_taps = lax.psum(tap_sum, ('dp', 'ctx')) * grad_scale]
    mul x14 -> x0, local copies, waits for them, and re-layouts: 58 us -> none  [the longest x12 55.3 us: group_fn(): src_blk[:, :, None, :] * rising[None]]
    dot_general x8 -> x0, matrix products: 41.4 us -> none  [the longest x4 26 us: group_fn(): jnp.einsum('pij,pjk->pik', joined_mask, lifted, precision=lax.Precision.H...]
    while x38 -> x0, local copies, waits for them, and re-layouts: 33.9 us -> none
    all_to_all x0 -> x2, blocking collectives: none -> 32.6 us  [the longest x1 18.5 us: per_device(): lax.all_to_all(ends, 'ctx', split_axis=0, concat_axis=0, tiled=True)]
    pallas_call x0 -> x2, Pallas kernels: none -> 28.9 us  [the longest x1 20.5 us: per_device(): pl.pallas_call(functools.partial(main_kernel, rows, ctx_count), out_shape...]
    while x4 -> x0, other arithmetic: 23 us -> none
    dot_general x3 -> x0, other arithmetic: 13.8 us -> none  [the longest x2 13.8 us: group_fn(): jnp.einsum('pic,pimc->mc', other_blk, inner_state, precision=lax.Precisio...]
  transfers between devices with their start and end apart: 7 -> 4, of which waited for: 5 -> 3; matrix products, arithmetic and copies ran while one was open for 8% -> 2% of each run, Pallas kernels for 0% -> 0%
where the time goes in v1:
time: 101 us
  blocking collectives  32.6 us (32%)
  Pallas kernels  28.9 us (29%)
  starting transfers between devices  15.7 us (16%)
  waiting for transfers between devices  13.7 us (14%)
  local copies, waits for them, and re-layouts  8.12 us (8%)
    pallas_call x1, Pallas kernels, per_device(): pl.pallas_call(functools.partial(main_kernel, rows, ctx_count), out_shape...  20.5 us
    all_to_all x1, blocking collectives, per_device(): lax.all_to_all(ends, 'ctx', split_axis=0, concat_axis=0, tiled=True)  18.5 us
    all_to_all x1, blocking collectives, per_device(): lax.all_to_all(sums.reshape(total, share, LANES), both, split_axis=0, con...  14.1 us
    all_to_all x1, waiting for transfers between devices, per_device(): lax.all_to_all(jnp.broadcast_to(mine[None], parts.shape), both, split_axi...  10.6 us
    pallas_call x1, Pallas kernels, per_device(): pl.pallas_call(functools.partial(ends_kernel, rows, ctx_count), out_shape...  8.38 us
    all_to_all x1, starting transfers between devices, per_device(): lax.all_to_all(jnp.broadcast_to(params[None], (ctx_count,) + params.shape...  7.28 us
    ppermute x2, starting transfers between devices, shifted(): return lax.ppermute(block, axis, route)  5.85 us
    unnamed x10, local copies, waits for them, and re-layouts  3.04 us
  transfers between devices with their start and end apart: 4, of which 3 were waited for; matrix products, arithmetic and copies ran while one was open for 2% of the time, Pallas kernels for 0%

profile of v1, /device:TPU:0, one launch (start us, length us, event | category | flops | bytes accessed | tf_op | source)
XLA Modules:
  0.0 100.6 jit_solution(4688191759704038795)
XLA Ops:
  0.6 0.0 copy-start.2
  0.6 0.8 pad_maximum_fusion
  1.5 0.7 broadcast_in_dim.7
  2.2 7.3 %all-to-all-start = ((f32[8,33,256]{2,1,0:T(8,128)}), f32[8,33,256]{2,1,0:T(8,128)S(1)}, u32[]{:S(2)}, u32[]{:S(2)}) async-start(f32[8,33,256]{2,1,0:T(8,128)} %broadcast_in_dim.7), calls=%async_computation | async-start | bytes 655360 | tf_op jit(solution)/shard_map/all_to_all | solution.py:327
  9.5 1.0 slice_bitcast_fusion
  10.5 0.8 slice_bitcast_fusion.2
  11.3 1.3 %collective-permute-start.1 = (bf16[2,8192]{1,0:T(2,128)(2,1)S(1)}, bf16[2,8192]{1,0:T(2,128)(2,1)S(1)}, u32[]{:S(2)}, u32[]{:S(2)}) collective-permute-start(bf16[2,8192]{1,0:T(2,128)(2,1)S(1)} %pad_maximum_fusion.1), channel_id=1, source_target_pairs={{1,0},{2,1},{3,2},{4,3},{5,4},{6,5},{7,6},{9,8},{10,9},{11,10},{12... | collective-permute-start | bytes 98312 | tf_op jit(solution)/shard_map/ppermute | solution.py:22
  12.6 4.6 %collective-permute-start = (bf16[2,6144]{1,0:T(2,128)(2,1)S(1)}, bf16[2,6144]{1,0:T(2,128)(2,1)S(1)}, u32[]{:S(2)}, u32[]{:S(2)}) collective-permute-start(bf16[2,6144]{1,0:T(2,128)(2,1)S(1)} %get-tuple-element.9), channel_id=1, source_target_pairs={{0,1},{1,2},{2,3},{3,4},{4,5},{5,6},{6,7},{8,9},{9,10},{10,11},{11... | collective-permute-start | bytes 73736 | tf_op jit(solution)/shard_map/ppermute | solution.py:22
  17.1 1.5 %collective-permute-done.refs_4_.refs_5_.refs_6_ = bf16[2,6144]{1,0:T(2,128)(2,1)S(1)} collective-permute-done((bf16[2,6144]{1,0:T(2,128)(2,1)S(1)}, bf16[2,6144]{1,0:T(2,128)(2,1)S(1)}, u32[]{:S(2)}, u32[]{:S(2)}) %collective-permute-start) | collective-permute-done | bytes 24608 | tf_op jit(solution)/shard_map/ppermute | solution.py:22
  18.6 0.0 collective-permute-done.1.refs_7_.refs_8_.refs_9_.refs_10_
  18.6 1.5 %all-to-all-done.refs_14_ = f32[8,33,256]{2,1,0:T(8,128)S(1)} async-done(((f32[8,33,256]{2,1,0:T(8,128)}), f32[8,33,256]{2,1,0:T(8,128)S(1)}, u32[]{:S(2)}, u32[]{:S(2)}) %all-to-all-start) | async-done | bytes 270368 | tf_op jit(solution)/shard_map/all_to_all | solution.py:327
  20.2 0.0 copy-done.2
  20.2 0.0 copy-start
  20.2 1.4 %copy-done = bf16[1,128,6144]{2,1,0:T(8,128)(2,1)S(1)} copy-done((bf16[1,128,6144]{2,1,0:T(8,128)(2,1)S(1)}, bf16[1,128,6144]{2,1,0:T(8,128)(2,1)}, u32[]{:S(2)}) %copy-start) | copy-done | bytes 1572888
  21.6 0.0 copy-start.1
  21.6 0.9 copy-done.1
  22.5 0.0 copy-start.3
  22.5 0.7 copy-done.3
  23.1 8.4 %ends.1 = bf16[8,2,128,128]{3,2,1,0:T(8,128)(2,1)S(1)} custom-call(s32[1,8]{1,0:T(1,128)S(1)} %copy-done.3, bf16[1,128,6144]{2,1,0:T(8,128)(2,1)S(1)} %copy-done, bf16[1,128,6144]{2,1,0:T(8,128)(2,1)S(1)} %copy-done, bf16[1,128,6144]{2,1,0:T(8,128)(2,1)S(1)} %copy-done, bf16[1,128,2048]{2,1,0:T(8,128)(2,1)S(1)} %copy-done.2, ...), custom_call_target="tpu_custom_call" | custom-call | tf_op jit(solution)/shard_map/ends/pallas_call | solution.py:377
  31.5 18.5 %all_to_all.20.refs_15_ = bf16[8,2,128,128]{3,2,1,0:T(8,128)(2,1)S(1)} all-to-all(bf16[8,2,128,128]{3,2,1,0:T(8,128)(2,1)S(1)} %ends.1), channel_id=1, replica_groups=mesh['dp'=4,'ctx'=8] {'ctx'}, dimensions={0} | all-to-all | bytes 1048576 | tf_op jit(solution)/shard_map/all_to_all | solution.py:387
  50.0 20.5 %main.1 = (bf16[1,128,6144]{2,1,0:T(8,128)(2,1)}, f32[512,128]{1,0:T(8,128)S(1)}) custom-call(s32[1,8]{1,0:T(1,128)S(1)} %copy-done.3, bf16[1,128,6144]{2,1,0:T(8,128)(2,1)S(1)} %copy-done, bf16[1,128,6144]{2,1,0:T(8,128)(2,1)S(1)} %copy-done, bf16[1,128,6144]{2,1,0:T(8,128)(2,1)S(1)} %copy-done, bf16[1,128,2048]{2,1,0:T(8,128)(2,1)S(1)} %copy-done.2, ...), custom_call_target="tpu_custom_call" | custom-call | tf_op jit(solution)/shard_map/main/pallas_call | solution.py:391
  70.5 14.1 %all_to_all.21 = f32[32,16,128]{2,1,0:T(8,128)S(1)} all-to-all(f32[32,16,128]{2,1,0:T(8,128)S(1)} %bitcast.12), channel_id=1, replica_groups=mesh['dp'=4,'ctx'=8] {'dp','ctx'}, dimensions={0} | all-to-all | bytes 524288 | tf_op jit(solution)/shard_map/all_to_all | solution.py:410
  84.6 0.7 broadcast_in_dim.8
  85.4 2.6 %all-to-all-start.3 = ((f32[32,16,128]{2,1,0:T(8,128)}), f32[32,16,128]{2,1,0:T(8,128)S(1)}, u32[]{:S(2)}, u32[]{:S(2)}) async-start(f32[32,16,128]{2,1,0:T(8,128)} %broadcast_in_dim.8), calls=%async_computation.3 | async-start | bytes 524288 | tf_op jit(solution)/shard_map/all_to_all | solution.py:414
  88.0 10.6 %all-to-all-done.3 = f32[32,16,128]{2,1,0:T(8,128)S(1)} async-done(((f32[32,16,128]{2,1,0:T(8,128)}), f32[32,16,128]{2,1,0:T(8,128)S(1)}, u32[]{:S(2)}, u32[]{:S(2)}) %all-to-all-start.3) | async-done | bytes 262176 | tf_op jit(solution)/shard_map/all_to_all | solution.py:414
  98.6 0.1 copy.11
  98.7 0.6 constant_dynamic-slice_fusion
  99.3 0.6 dynamic-slice.1
  99.9 0.7 reshape.27
  (6 shorter events, 0.1 us)
Async XLA Ops:
  0.6 19.5 %copy-start.2 = (bf16[1,128,2048]{2,1,0:T(8,128)(2,1)S(1)}, bf16[1,128,2048]{2,1,0:T(8,128)(2,1)}, u32[]{:S(2)}) copy-start(bf16[1,128,2048]{2,1,0:T(8,128)(2,1)} %refs_3_.3) | copy-start | bytes 1572868
  2.2 18.0 %all-to-all-start = ((f32[8,33,256]{2,1,0:T(8,128)}), f32[8,33,256]{2,1,0:T(8,128)S(1)}, u32[]{:S(2)}, u32[]{:S(2)}) async-start(f32[8,33,256]{2,1,0:T(8,128)} %broadcast_in_dim.7), calls=%async_computation | async-start | bytes 655360 | tf_op jit(solution)/shard_map/all_to_all | solution.py:327
  11.3 7.4 %collective-permute-start.1 = (bf16[2,8192]{1,0:T(2,128)(2,1)S(1)}, bf16[2,8192]{1,0:T(2,128)(2,1)S(1)}, u32[]{:S(2)}, u32[]{:S(2)}) collective-permute-start(bf16[2,8192]{1,0:T(2,128)(2,1)S(1)} %pad_maximum_fusion.1), channel_id=1, source_target_pairs={{1,0},{2,1},{3,2},{4,3},{5,4},{6,5},{7,6},{9,8},{10,9},{11,10},{12... | collective-permute-start | bytes 98312 | tf_op jit(solution)/shard_map/ppermute | solution.py:22
  12.6 6.1 %collective-permute-start = (bf16[2,6144]{1,0:T(2,128)(2,1)S(1)}, bf16[2,6144]{1,0:T(2,128)(2,1)S(1)}, u32[]{:S(2)}, u32[]{:S(2)}) collective-permute-start(bf16[2,6144]{1,0:T(2,128)(2,1)S(1)} %get-tuple-element.9), channel_id=1, source_target_pairs={{0,1},{1,2},{2,3},{3,4},{4,5},{5,6},{6,7},{8,9},{9,10},{10,11},{11... | collective-permute-start | bytes 73736 | tf_op jit(solution)/shard_map/ppermute | solution.py:22
  20.2 1.4 %copy-start = (bf16[1,128,6144]{2,1,0:T(8,128)(2,1)S(1)}, bf16[1,128,6144]{2,1,0:T(8,128)(2,1)}, u32[]{:S(2)}) copy-start(bf16[1,128,6144]{2,1,0:T(8,128)(2,1)} %refs_2_.3) | copy-start | bytes 4718596
  21.6 0.9 copy-start.1
  22.5 0.7 copy-start.3
  85.4 13.2 %all-to-all-start.3 = ((f32[32,16,128]{2,1,0:T(8,128)}), f32[32,16,128]{2,1,0:T(8,128)S(1)}, u32[]{:S(2)}, u32[]{:S(2)}) async-start(f32[32,16,128]{2,1,0:T(8,128)} %broadcast_in_dim.8), calls=%async_computation.3 | async-start | bytes 524288 | tf_op jit(solution)/shard_map/all_to_all | solution.py:414

commit v2 on v0

v2 whole, which is shorter than its diff:
```python
import functools
import math

import jax
import jax.numpy as jnp
from jax import lax
from jax.experimental import pallas as pl
from jax.experimental.pallas import tpu as pltpu
from jax.sharding import PartitionSpec as P

F32 = jnp.float32
BF16 = jnp.bfloat16
LANES = 128
SUB = 8
GROUP = SUB * LANES
HALO = 2


def shifted(block, axis, distance):
    count = lax.axis_size(axis)
    route = [(i - distance, i) for i in range(count) if 0 <= i - distance < count]
    return lax.ppermute(block, axis, route)


def vec(ref, index):
    return ref[pl.ds(pl.multiple_of(index * SUB, SUB), SUB), :]


def put(ref, index, value):
    ref[pl.ds(pl.multiple_of(index * SUB, SUB), SUB), :] = value


def spread(dst, first, src, row_count, column):
    for j in range(SUB):
        value = src[:, pl.ds(pl.multiple_of(column + j * LANES, LANES), LANES)].astype(F32)
        dst[pl.ds(first * SUB + j, row_count, stride=SUB), :] = value


def spread_rows(dst, first, src, row_count, column):
    def step(i, carry):
        for j in range(SUB):
            lanes = pl.ds(pl.multiple_of(column + j * LANES, LANES), LANES)
            value = src[0, pl.ds(pl.multiple_of(i * 16, 16), 16), lanes]
            dst[pl.ds((i * 16 + first) * SUB + j, 16, stride=SUB), :] = value.astype(F32)
        return carry

    lax.fori_loop(0, row_count // 16, step, 0)


def spread_params(dst, par, half, groups, first_row, rows):
    pieces, _, width = par.shape
    base = half * (pieces // groups)
    for j in range(SUB):
        if width >= LANES:
            per = width // LANES
            at = (j % per) * LANES
            parts = [(j // per, at, LANES)]
        else:
            per = LANES // width
            parts = [(j * per + i, 0, width) for i in range(per)]
        for first in range(0, rows, SUB):
            many = min(SUB, rows - first)
            at_row = first_row + first
            got = [par[base + k, at_row : at_row + many, at : at + w] for k, at, w in parts]
            value = got[0] if len(got) == 1 else jnp.concatenate(got, axis=1)
            dst[pl.ds(first * SUB + j, many, stride=SUB), :] = value


def segment_starts(lengths):
    starts = [jnp.int32(0)]
    for j in range(lengths.shape[1]):
        starts.append(starts[-1] + lengths[0, j])
    return starts


def fill_keep(keep, starts, base, rows):
    count = rows + HALO + 2

    def step(i, carry):
        keep[i] = jnp.float32(1.0)
        return carry

    lax.fori_loop(0, count, step, 0, unroll=4)
    for start in starts:
        at = start - base + 1

        @pl.when((at >= 0) & (at < count))
        def _():
            keep[at] = jnp.float32(0.0)


def rounded(value):
    return value.astype(BF16).astype(F32)


def flag(condition):
    return jnp.where(condition, 1.0, 0.0).astype(F32)


def each_group(groups, body):
    def step(half, carry):
        body(half)
        return carry

    lax.fori_loop(0, groups, step, 0)


def features_kernel(
    rows, groups, lengths, features, upstream, left, right, taps,
    feat, tapv, up, mixed, gout, key_out, val_out, keep,
):
    base = lax.axis_index("ctx") * rows
    extended = rows + HALO
    fill_keep(keep, segment_starts(lengths), base, rows)

    def group(half):
        def feat_at(third):
            return (half * 3 + third) * (rows + 2 * HALO)

        def tap_at(third):
            return (half * 3 + third) * 3

        for third in range(3):
            column = (third * groups + half) * GROUP
            spread_rows(feat, feat_at(third) + HALO, features, rows, column)
            spread(feat, feat_at(third), left, HALO, column)
            spread(feat, feat_at(third) + rows + HALO, right, HALO, column)
            spread(tapv, tap_at(third), taps, 3, column)
        spread_rows(up, half * extended, upstream, rows, half * GROUP)
        spread(up, half * extended + rows, right, HALO, (3 * groups + half) * GROUP)
        tap = [[vec(tapv, tap_at(third) + j) for j in range(3)] for third in range(3)]

        def product(p, carry):
            keep_one = keep[p + 1]
            keep_two = keep_one * keep[p]
            query, key, val = (
                tap[third][0] * vec(feat, feat_at(third) + p + 2)
                + tap[third][1] * (keep_one * vec(feat, feat_at(third) + p + 1))
                + tap[third][2] * (keep_two * vec(feat, feat_at(third) + p))
                for third in range(3)
            )
            at = half * extended + p
            put(mixed, at, rounded(key * val))
            put(gout, at, rounded(vec(up, at) * query))
            put(key_out, at, key)
            put(val_out, at, val)
            return carry

        lax.fori_loop(0, extended, product, 0, unroll=2)

    each_group(groups, group)


def ends_kernel(rows, groups, lengths, params, mixed, gout, payload, own, par, stack, zero_scr):
    me = lax.axis_index("ctx")
    base = me * rows
    count = payload.shape[0]
    poles = (params.shape[1] - 1) // 2
    extended = rows + HALO
    starts = segment_starts(lengths)
    low, high = jnp.int32(0), jnp.int32(extended)
    for start in starts:
        at = start - base
        low = jnp.where(at < rows, jnp.maximum(low, at), low)
        high = jnp.where(at > HALO, jnp.minimum(high, at), high)
    zero_scr[...] = jnp.zeros((SUB, LANES), F32)
    zeros = [zero_scr[...]] * poles

    def group(half):
        spread_params(par, params, half, groups, 0, poles)
        decay = [jnp.exp(-jnp.exp(vec(par, m))) for m in range(poles)]

        def sweep(i, carry):
            state, adjoint = carry
            back = extended - 1 - i
            x = vec(mixed, half * extended + i) * flag(i >= low)
            g = vec(gout, half * extended + back) * flag(back < high)
            state = [decay[m] * state[m] + x for m in range(poles)]
            adjoint = [decay[m] * adjoint[m] + g for m in range(poles)]
            return state, adjoint

        state, adjoint = lax.fori_loop(0, rows, sweep, (zeros, zeros), unroll=2)
        for m in range(poles):
            put(own, half * poles + m, state[m])
        for m in range(0, poles, 2):
            at = slice(m * SUB, (m + 2) * SUB)
            stack[0, at, :] = jnp.concatenate(state[m : m + 2], axis=0).astype(BF16)
            stack[1, at, :] = jnp.concatenate(adjoint[m : m + 2], axis=0).astype(BF16)
        for e in range(count):
            payload[e, half] = stack[jnp.where(e > me, 0, 1)]

    each_group(groups, group)


def local_kernel(
    rows, groups, lengths, params, mixed, gout, conv, adj, partial, par, zero_scr, keep
):
    base = lax.axis_index("ctx") * rows
    poles = (params.shape[1] - 1) // 2
    extended = rows + HALO
    fill_keep(keep, segment_starts(lengths), base, rows)
    zero_scr[...] = jnp.zeros((SUB, LANES), F32)
    zero = zero_scr[...]
    per_pass = poles // 2
    zeros = [zero] * per_pass

    def group(half):
        spread_params(par, params, half, groups, 0, 2 * poles)
        for part in range(2):
            chosen = list(range(part * per_pass, (part + 1) * per_pass))
            decay = [jnp.exp(-jnp.exp(vec(par, m))) for m in chosen]
            coeff = [vec(par, poles + m) for m in chosen]

            def sweep(i, carry):
                state, adjoint, resid, skip = carry
                back = extended - 1 - i
                at, back_at = half * extended + i, half * extended + back
                x = vec(mixed, at)
                g = vec(gout, back_at)
                own = vec(mixed, back_at) * flag(back < rows)
                keep_fwd = keep[i + 1]
                keep_bwd = keep[back + 2]
                state = [decay[m] * (state[m] * keep_fwd) + x for m in range(per_pass)]
                adjoint = [decay[m] * (adjoint[m] * keep_bwd) + g for m in range(per_pass)]
                resid = [resid[m] + own * adjoint[m] for m in range(per_pass)]
                forward = sum(coeff[m] * state[m] for m in range(per_pass))
                backward = sum(coeff[m] * adjoint[m] for m in range(per_pass))
                if part == 0:
                    put(conv, at, forward)
                    put(adj, back_at, backward)
                    skip = skip + own * g
                else:
                    put(conv, at, forward + vec(conv, at))
                    put(adj, back_at, backward + vec(adj, back_at))
                return state, adjoint, resid, skip

            _, _, resid, skip = lax.fori_loop(
                0, extended, sweep, (zeros, zeros, zeros, zero), unroll=2
            )
            for i, m in enumerate(chosen):
                put(partial, m * groups + half, resid[i])
            if part == 0:
                put(partial, poles * groups + half, skip)

    each_group(groups, group)


def carry_kernel(
    rows, groups, lengths, params, arrived, own, partial, before, after, sums, par, zero_scr
):
    me = lax.axis_index("ctx")
    base = me * rows
    count = arrived.shape[0]
    poles = (params.shape[1] - 1) // 2
    extended = rows + HALO
    first, last, newest = jnp.int32(0), jnp.int32(2**30), jnp.int32(0)
    for start in segment_starts(lengths):
        first = jnp.where(start <= base, jnp.maximum(first, start), first)
        last = jnp.where(start > base + extended, jnp.minimum(last, start), last)
        newest = jnp.where(start <= base + extended, jnp.maximum(newest, start), newest)
    through = flag(newest < base + rows)
    zero_scr[...] = jnp.zeros((SUB, LANES), F32)
    per_pass = poles // 2
    zeros = [zero_scr[...]] * per_pass

    def group(half):
        spread_params(par, params, half, groups, 0, poles)
        for part in range(2):
            chosen = list(range(part * per_pass, (part + 1) * per_pass))
            rate = [jnp.exp(vec(par, m)) for m in chosen]
            block = [jnp.exp(-rows * r) for r in rate]

            def arrived_states(d):
                got = []
                for m in range(chosen[0], chosen[-1] + 1, 2):
                    pair = arrived[d, half, m * SUB : (m + 2) * SUB, :].astype(F32)
                    got += [pair[:SUB], pair[SUB:]]
                return got

            def from_before(d, carry):
                joined = flag((d + 1) * rows - 1 >= first)
                got = arrived_states(d)
                return [block[i] * carry[i] + joined * got[i] for i in range(per_pass)]

            def from_after(i, carry):
                d = count - 1 - i
                joined = flag(d * rows + HALO < last)
                got = arrived_states(d)
                return [block[i] * carry[i] + joined * got[i] for i in range(per_pass)]

            state = lax.fori_loop(0, me, from_before, zeros)
            adjoint = lax.fori_loop(0, count - 1 - me, from_after, zeros)
            for i, m in enumerate(chosen):
                put(before, half * poles + m, state[i])
                put(after, half * poles + m, adjoint[i])
                cross = jnp.exp(-(HALO + 1) * rate[i]) * (adjoint[i] * through)
                at = m * groups + half
                put(sums, at, vec(partial, at) + cross * vec(own, half * poles + m))
        at = poles * groups + half
        put(sums, at, vec(partial, at))

    each_group(groups, group)


def finish_kernel(
    rows, groups, lengths, params, feat, tapv, up, mixed, gout, key_in, val_in, conv, adj,
    before, after, grads, sums, par, post, zero_scr, keep,
):
    base = lax.axis_index("ctx") * rows
    poles = (params.shape[1] - 1) // 2
    extended = rows + HALO
    starts = segment_starts(lengths)
    fill_keep(keep, starts, base, rows)
    until, since = jnp.int32(extended), jnp.int32(0)
    for start in starts:
        at = start - base
        until = jnp.where(at >= 0, jnp.minimum(until, at), until)
        since = jnp.where(at <= extended, jnp.maximum(since, at), since)
    steps = jnp.maximum(until, extended - since)
    zero_scr[...] = jnp.zeros((SUB, LANES), F32)
    zero = zero_scr[...]

    def group(half):
        start_at = half * extended
        spread_params(par, params, half, groups, 0, 2 * poles + 1)
        decay = [jnp.exp(-jnp.exp(vec(par, m))) for m in range(poles)]
        enter = [
            vec(par, poles + m) * (decay[m] * vec(before, half * poles + m)) for m in range(poles)
        ]
        leave = [
            vec(par, poles + m) * (decay[m] * vec(after, half * poles + m)) for m in range(poles)
        ]

        def carried(i, carry):
            enter, leave = carry
            for step in range(2):
                p = 2 * i + step
                back = extended - 1 - p
                at, back_at = start_at + p, start_at + back
                put(conv, at, vec(conv, at) + flag(p < until) * sum(enter))
                put(adj, back_at, vec(adj, back_at) + flag(back >= since) * sum(leave))
                enter = [decay[m] * enter[m] for m in range(poles)]
                leave = [decay[m] * leave[m] for m in range(poles)]
            return enter, leave

        lax.fori_loop(0, (steps + 1) // 2, carried, (enter, leave))
        gain = vec(par, 2 * poles)
        tap = [[vec(tapv, (half * 3 + third) * 3 + j) for j in range(3)] for third in range(3)]

        def finish(i, carry):
            one, two, tap_sums = carry
            p = extended - 1 - i
            at = start_at + p
            mine = flag(p < rows)
            conv_out = rounded(vec(conv, at) + gain * vec(mixed, at))
            grad_mixed = rounded(vec(adj, at) + gain * vec(gout, at))
            now = [vec(up, at) * conv_out, grad_mixed * vec(val_in, at), grad_mixed * vec(key_in, at)]
            keep_one = keep[p + 1]
            keep_two = keep_one * keep[p]
            next_one = keep[p + 2]
            next_two = next_one * keep[jnp.minimum(p + 3, extended + 1)]
            new_sums = []
            for third in range(3):
                back = (
                    tap[third][0] * now[third]
                    + tap[third][1] * (next_one * one[third])
                    + tap[third][2] * (next_two * two[third])
                )
                put(post, third * extended + p, back)
                own = now[third] * mine
                f_at = (half * 3 + third) * (rows + 2 * HALO) + p
                new_sums += [
                    tap_sums[3 * third] + own * vec(feat, f_at + 2),
                    tap_sums[3 * third + 1] + own * (keep_one * vec(feat, f_at + 1)),
                    tap_sums[3 * third + 2] + own * (keep_two * vec(feat, f_at)),
                ]
            return now, one, new_sums

        _, _, tap_sums = lax.fori_loop(
            0, extended, finish, ([zero] * 3, [zero] * 3, [zero] * 9), unroll=2
        )
        for third in range(3):
            for j in range(3):
                put(sums, (3 * j + third) * groups + half, tap_sums[3 * third + j])

        def write(i, carry):
            for third in range(3):
                for j in range(SUB):
                    first = (third * extended + i * 16) * SUB + j
                    value = post[pl.ds(first, 16, stride=SUB), :]
                    column = (third * groups + half) * GROUP + j * LANES
                    lanes = pl.ds(pl.multiple_of(column, LANES), LANES)
                    grads[0, pl.ds(pl.multiple_of(i * 16, 16), 16), lanes] = value.astype(BF16)
            return carry

        lax.fori_loop(0, rows // 16, write, 0)

    each_group(groups, group)


def swap(block, axes):
    return lax.all_to_all(block, axes, split_axis=0, concat_axis=0, tiled=True)


def sum_over_all(rows, used):
    total = lax.axis_size("dp") * lax.axis_size("ctx")
    parts = swap(rows.reshape(total, -1, LANES), ("dp", "ctx"))
    mine = jnp.sum(parts, axis=0)
    whole = swap(jnp.broadcast_to(mine[None], parts.shape), ("dp", "ctx"))
    return whole.reshape(-1, LANES)[:used]


def per_device(features, upstream, lengths, conv_taps, residues, log_rate, skip_gain):
    rows = features.shape[1]
    channels = upstream.shape[2]
    poles = residues.shape[0]
    ctx_count = lax.axis_size("ctx")
    total = ctx_count * lax.axis_size("dp")
    shard_index = lax.axis_index("ctx")
    per_shard = channels // ctx_count
    groups = channels // GROUP
    grad_scale = 1.0 / math.sqrt(rows * ctx_count * lax.axis_size("dp"))
    extended = rows + HALO
    vmem = pl.BlockSpec(memory_space=pltpu.VMEM)
    smem = pl.BlockSpec(memory_space=pltpu.SMEM)
    limits = pltpu.CompilerParams(vmem_limit_bytes=32 * 1024 * 1024)

    def tall(height):
        return jax.ShapeDtypeStruct((height * SUB, LANES), F32)

    def scratch(height):
        return pltpu.VMEM((height * SUB, LANES), F32)

    def call(kernel, name, out_shape, scratch_shapes, *operands):
        outs = [vmem] * len(out_shape)
        return pl.pallas_call(
            functools.partial(kernel, rows, groups),
            out_shape=out_shape,
            in_specs=[smem] + [vmem] * len(operands),
            out_specs=outs,
            scratch_shapes=scratch_shapes,
            compiler_params=limits,
            name=name,
        )(lengths, *operands)

    keep = pltpu.SMEM((rows + 8,), F32)
    edge = features[0, rows - HALO :, :]
    head = jnp.concatenate([features[0, :HALO, :], upstream[0, :HALO, :]], axis=1)
    left = shifted(edge, "ctx", 1)
    right = shifted(head, "ctx", -1)
    params = jnp.concatenate([log_rate, residues, skip_gain[None]], axis=0)
    params = swap(jnp.broadcast_to(params[None], (ctx_count,) + params.shape), "ctx")

    whole = tall(groups * extended)
    feat, tapv, up, mixed, gout, key, val = call(
        features_kernel,
        "features",
        [tall(groups * 3 * (rows + 2 * HALO)), tall(groups * 9)] + [whole] * 5,
        [keep],
        features, upstream, left, right, conv_taps,
    )
    states = tall(groups * poles)
    payload, own = call(
        ends_kernel,
        "ends",
        [jax.ShapeDtypeStruct((ctx_count, groups, poles * SUB, LANES), BF16), states],
        [scratch(poles), pltpu.VMEM((2, poles * SUB, LANES), BF16), scratch(1)],
        params, mixed, gout,
    )
    arrived = swap(payload, "ctx")
    conv, adj, partial = call(
        local_kernel,
        "local",
        [whole, whole, tall(groups * (poles + 1))],
        [scratch(2 * poles), scratch(1), keep],
        params, mixed, gout,
    )

    def shares(used):
        return total * -(-used // (total * SUB))

    before, after, resid_rows = call(
        carry_kernel,
        "carry",
        [states, states, tall(shares(groups * (poles + 1) * SUB))],
        [scratch(poles), scratch(1)],
        params, arrived, own, partial,
    )
    resid = sum_over_all(resid_rows, groups * (poles + 1) * SUB)
    grads, tap_rows = call(
        finish_kernel,
        "finish",
        [jax.ShapeDtypeStruct(features.shape, BF16), tall(shares(groups * 9 * SUB))],
        [scratch(2 * poles + 1), scratch(3 * extended), scratch(1), keep],
        params, feat, tapv, up, mixed, gout, key, val, conv, adj, before, after,
    )
    grad_taps = sum_over_all(tap_rows, groups * 9 * SUB).reshape(3, 3 * channels) * grad_scale
    rest = resid.reshape(poles + 1, channels)
    rest = lax.dynamic_slice(rest, (0, shard_index * per_shard), (poles + 1, per_shard))
    rest = rest * grad_scale
    return grads, grad_taps, rest[:poles], rest[poles]


def solution(mesh):
    return jax.shard_map(
        per_device,
        mesh=mesh,
        in_specs=(
            P("dp", "ctx", None),
            P("dp", "ctx", None),
            P("dp", None),
            P(),
            P(None, "ctx"),
            P(None, "ctx"),
            P("ctx"),
        ),
        out_specs=(P("dp", "ctx", None), P(), P(None, "ctx"), P("ctx")),
        check_vma=False,
    )
```

time: 505 us -> 127 us (0.25)
  local copies, waits for them, and re-layouts: 162 us -> 19.9 us
  waiting for transfers between devices: 149 us -> 29.8 us
  other arithmetic: 80.7 us -> 0.94 us
  matrix products: 41.4 us -> 0 us
  Pallas kernels: 0 us -> 29.6 us
  between operations: 15.7 us -> 0.83 us
  loops' own time: 13.5 us -> 0 us
    psum x1 -> x0, waiting for transfers between devices: 117 us -> none  [per_device(): grad_taps = lax.psum(tap_sum, ('dp', 'ctx')) * grad_scale]
    mul x14 -> x1, local copies, waits for them, and re-layouts: 58 us -> 0.67 us  [per_device(): sum_over_all(tap_rows, groups * 9 * SUB).reshape(3, 3 * channels)]
    dot_general x8 -> x0, matrix products: 41.4 us -> none  [the longest x4 26 us: group_fn(): jnp.einsum('pij,pjk->pik', joined_mask, lifted, precision=lax.Precision.H...]
    while x38 -> x0, local copies, waits for them, and re-layouts: 33.9 us -> none
    pallas_call x0 -> x5, Pallas kernels: none -> 29.6 us  [call(): pl.pallas_call(functools.partial(kernel, rows, groups), out_shape=out_sha...]
    while x4 -> x0, other arithmetic: 23 us -> none
    all_to_all x0 -> x1, blocking collectives: none -> 16.1 us  [swap(): return lax.all_to_all(block, axes, split_axis=0, concat_axis=0, tiled=True)]
    dot_general x3 -> x0, other arithmetic: 13.8 us -> none  [the longest x2 13.8 us: group_fn(): jnp.einsum('pic,pimc->mc', other_blk, inner_state, precision=lax.Precisio...]
  transfers between devices with their start and end apart: 7 -> 7, of which waited for: 5 -> 4; matrix products, arithmetic and copies ran while one was open for 8% -> 1% of each run, Pallas kernels for 0% -> 12%
where the time goes in v2:
time: 127 us; the launch traced here: 126 us
  waiting for transfers between devices  29.8 us (23%)
  Pallas kernels  29.6 us (23%)
  starting transfers between devices  28.6 us (23%)
  local copies, waits for them, and re-layouts  19.9 us (16%)
  blocking collectives  16.1 us (13%)
    pallas_call x5, Pallas kernels, call(): pl.pallas_call(functools.partial(kernel, rows, groups), out_shape=out_sha...  29.6 us
    all_to_all x5, waiting for transfers between devices, swap(): return lax.all_to_all(block, axes, split_axis=0, concat_axis=0, tiled=True)  28.3 us
    all_to_all x5, starting transfers between devices, swap(): return lax.all_to_all(block, axes, split_axis=0, concat_axis=0, tiled=True)  22.7 us
    all_to_all x1, blocking collectives, swap(): return lax.all_to_all(block, axes, split_axis=0, concat_axis=0, tiled=True)  16.1 us
    unnamed x34, local copies, waits for them, and re-layouts  15 us
    ppermute x2, starting transfers between devices, shifted(): return lax.ppermute(block, axis, route)  5.85 us
  transfers between devices with their start and end apart: 7, of which 4 were waited for; matrix products, arithmetic and copies ran while one was open for 1% of the time, Pallas kernels for 12%

profile of v2, /device:TPU:0, one launch (start us, length us, event | category | flops | bytes accessed | tf_op | source)
XLA Modules:
  0.0 125.7 jit_solution(84536887065645092)
XLA Ops:
  0.6 0.0 copy-start.13
  0.6 0.0 copy-start.14
  0.7 0.0 copy-start.15
  0.7 0.8 pad_maximum_fusion
  1.5 0.7 broadcast_in_dim.9
  2.2 7.3 %all-to-all-start = ((f32[8,33,256]{2,1,0:T(8,128)}), f32[8,33,256]{2,1,0:T(8,128)S(1)}, u32[]{:S(2)}, u32[]{:S(2)}) async-start(f32[8,33,256]{2,1,0:T(8,128)} %broadcast_in_dim.9), calls=%async_computation | async-start | bytes 655360 | tf_op jit(solution)/shard_map/all_to_all | solution.py:402
  9.5 1.0 slice_bitcast_fusion
  10.5 0.0 copy-done.13
  10.6 1.3 %collective-permute-start.1 = (bf16[2,8192]{1,0:T(2,128)(2,1)S(1)}, bf16[2,8192]{1,0:T(2,128)(2,1)S(1)}, u32[]{:S(2)}, u32[]{:S(2)}) collective-permute-start(bf16[2,8192]{1,0:T(2,128)(2,1)S(1)} %pad_maximum_fusion.1), channel_id=1, source_target_pairs={{1,0},{2,1},{3,2},{4,3},{5,4},{6,5},{7,6},{9,8},{10,9},{11,10},{12... | collective-permute-start | bytes 98312 | tf_op jit(solution)/shard_map/ppermute | solution.py:22
  11.9 4.6 %collective-permute-start = (bf16[2,6144]{1,0:T(2,128)(2,1)S(1)}, bf16[2,6144]{1,0:T(2,128)(2,1)S(1)}, u32[]{:S(2)}, u32[]{:S(2)}) collective-permute-start(bf16[2,6144]{1,0:T(2,128)(2,1)S(1)} %get-tuple-element.39), channel_id=1, source_target_pairs={{0,1},{1,2},{2,3},{3,4},{4,5},{5,6},{6,7},{8,9},{9,10},{10,11},{11... | collective-permute-start | bytes 73736 | tf_op jit(solution)/shard_map/ppermute | solution.py:22
  16.4 1.5 %collective-permute-done.left = bf16[2,6144]{1,0:T(2,128)(2,1)S(1)} collective-permute-done((bf16[2,6144]{1,0:T(2,128)(2,1)S(1)}, bf16[2,6144]{1,0:T(2,128)(2,1)S(1)}, u32[]{:S(2)}, u32[]{:S(2)}) %collective-permute-start) | collective-permute-done | bytes 24608 | tf_op jit(solution)/shard_map/ppermute | solution.py:22
  17.9 0.0 collective-permute-done.1.right
  17.9 0.0 copy-done.14
  17.9 0.0 copy-done.15
  17.9 1.4 %copy-done.2 = bf16[1,128,6144]{2,1,0:T(8,128)(2,1)S(1)} copy-done((bf16[1,128,6144]{2,1,0:T(8,128)(2,1)S(1)}, bf16[1,128,6144]{2,1,0:T(8,128)(2,1)}, u32[]{:S(2)}) %copy-start.2) | copy-done | bytes 1572888
  19.3 4.4 %features.2 = (f32[6336,128]{1,0:T(8,128)S(1)}, f32[144,128]{1,0:T(8,128)S(1)}, f32[2080,128]{1,0:T(8,128)S(1)}, f32[2080,128]{1,0:T(8,128)S(1)}, f32[2080,128]{...) custom-call(s32[1,8]{1,0:T(1,128)S(1)} %copy-done.15, bf16[1,128,6144]{2,1,0:T(8,128)(2,1)S(1)} %copy-done.2, ...), custom_call_target="tpu_custom_call" | custom-call | tf_op jit(solution)/shard_map/features/pallas_call | solution.py:436
  23.8 0.0 copy-start
  23.8 1.7 %copy-done = f32[6336,128]{1,0:T(8,128)} copy-done((f32[6336,128]{1,0:T(8,128)}, f32[6336,128]{1,0:T(8,128)S(1)}, u32[]{:S(2)}) %copy-start) | copy-done | bytes 3244056
  25.4 1.0 copy-done.3
  26.4 1.0 copy-done.5
  27.4 1.0 copy-done.7
  28.4 0.0 all-to-all-done.params
  28.4 5.2 %ends.1 = (bf16[8,2,128,128]{3,2,1,0:T(8,128)(2,1)}, f32[256,128]{1,0:T(8,128)S(1)}) custom-call(s32[1,8]{1,0:T(1,128)S(1)} %copy-done.15, f32[8,33,256]{2,1,0:T(8,128)S(1)} %all-to-all-done.params, f32[2080,128]{1,0:T(8,128)S(1)} %get-tuple-element.24.mixed, f32[2080,128]{1,0:T(8,128)S(1)} %get-tuple-element.25.gout), custom_call_target="tpu_custom_call" | custom-call | tf_op jit(solution)/shard_map/ends/pallas_call | solution.py:436
  33.6 7.7 %all-to-all-start.1 = ((bf16[8,2,128,128]{3,2,1,0:T(8,128)(2,1)}), bf16[8,2,128,128]{3,2,1,0:T(8,128)(2,1)S(1)}, u32[]{:S(2)}, u32[]{:S(2)}) async-start(bf16[8,2,128,128]{3,2,1,0:T(8,128)(2,1)} %get-tuple-element.30), calls=%async_computation.1 | async-start | bytes 1048576 | tf_op jit(solution)/shard_map/all_to_all | solution.py:402
  41.4 11.0 %local.1 = (f32[2080,128]{1,0:T(8,128)S(1)}, f32[2080,128]{1,0:T(8,128)S(1)}, f32[272,128]{1,0:T(8,128)S(1)}) custom-call(s32[1,8]{1,0:T(1,128)S(1)} %copy-done.15, f32[8,33,256]{2,1,0:T(8,128)S(1)} %all-to-all-done.params, f32[2080,128]{1,0:T(8,128)S(1)} %get-tuple-element.24.mixed, f32[2080,128]{1,0:T(8,128)S(1)} %get-tuple-element.25.gout), custom_call_target="tpu_custom_call" | custom-call | tf_op jit(solution)/shard_map/local/pallas_call | solution.py:436
  52.4 1.0 copy-done.9
  53.4 1.0 copy-done.11
  54.4 0.0 all-to-all-done.1.arrived
  54.4 1.7 %carry.1 = (f32[256,128]{1,0:T(8,128)S(1)}, f32[256,128]{1,0:T(8,128)S(1)}, f32[512,128]{1,0:T(8,128)}) custom-call(s32[1,8]{1,0:T(1,128)S(1)} %copy-done.15, f32[8,33,256]{2,1,0:T(8,128)S(1)} %all-to-all-done.params, bf16[8,2,128,128]{3,2,1,0:T(8,128)(2,1)S(1)} %all-to-all-done.1.arrived, f32[256,128]{1,0:T(8,128)S(1)} %get-tuple-element.31.own, ...), custom_call_target="tpu_custom_call" | custom-call | tf_op jit(solution)/shard_map/carry/pallas_call | solution.py:436
  56.0 1.9 %copy-done.1 = f32[6336,128]{1,0:T(8,128)S(1)} copy-done((f32[6336,128]{1,0:T(8,128)S(1)}, f32[6336,128]{1,0:T(8,128)}, u32[]{:S(2)}) %copy-start.1) | copy-done | bytes 3244056
  57.9 1.2 copy-done.6
  59.2 1.2 copy-done.8
  60.4 1.2 copy-done.10
  61.6 1.2 copy-done.12
  62.9 7.3 %finish.1 = (bf16[1,128,6144]{2,1,0:T(8,128)(2,1)}, f32[256,128]{1,0:T(8,128)S(1)}) custom-call(s32[1,8]{1,0:T(1,128)S(1)} %copy-done.15, f32[8,33,256]{2,1,0:T(8,128)S(1)} %all-to-all-done.params, f32[6336,128]{1,0:T(8,128)S(1)} %copy-done.1, f32[144,128]{1,0:T(8,128)S(1)} %get-tuple-element.22.tapv, f32[2080,128]{1,0:T(8,128)S(1)} %copy-done.4, ...), custom_call_target="tpu_custom_call" | custom-call | tf_op jit(solution)/shard_map/finish/pallas_call | solution.py:436
  70.1 16.1 %all_to_all.30 = f32[32,8,128]{2,1,0:T(8,128)S(1)} all-to-all(f32[32,8,128]{2,1,0:T(8,128)S(1)} %bitcast.13), channel_id=1, replica_groups=mesh['dp'=4,'ctx'=8] {'dp','ctx'}, dimensions={0} | all-to-all | bytes 262144 | tf_op jit(solution)/shard_map/all_to_all | solution.py:402
  86.2 2.6 %all-to-all-start.4 = ((f32[32,16,128]{2,1,0:T(8,128)}), f32[32,16,128]{2,1,0:T(8,128)S(1)}, u32[]{:S(2)}, u32[]{:S(2)}) async-start(f32[32,16,128]{2,1,0:T(8,128)} %bitcast.5), calls=%async_computation.4 | async-start | bytes 524288 | tf_op jit(solution)/shard_map/all_to_all | solution.py:402
  88.9 10.6 %all-to-all-done.4 = f32[32,16,128]{2,1,0:T(8,128)S(1)} async-done(((f32[32,16,128]{2,1,0:T(8,128)}), f32[32,16,128]{2,1,0:T(8,128)S(1)}, u32[]{:S(2)}, u32[]{:S(2)}) %all-to-all-start.4) | async-done | bytes 262176 | tf_op jit(solution)/shard_map/all_to_all | solution.py:402
  99.5 0.7 broadcast_in_dim.10
  100.2 2.6 %all-to-all-start.3 = ((f32[32,8,128]{2,1,0:T(8,128)}), f32[32,8,128]{2,1,0:T(8,128)S(1)}, u32[]{:S(2)}, u32[]{:S(2)}) async-start(f32[32,8,128]{2,1,0:T(8,128)} %broadcast_in_dim.10), calls=%async_computation.3 | async-start | bytes 262144 | tf_op jit(solution)/shard_map/all_to_all | solution.py:402
  102.8 7.7 %all-to-all-done.3 = f32[32,8,128]{2,1,0:T(8,128)S(1)} async-done(((f32[32,8,128]{2,1,0:T(8,128)}), f32[32,8,128]{2,1,0:T(8,128)S(1)}, u32[]{:S(2)}, u32[]{:S(2)}) %all-to-all-start.3) | async-done | bytes 131104 | tf_op jit(solution)/shard_map/all_to_all | solution.py:402
  110.5 0.7 broadcast_in_dim.11
  111.2 2.6 %all-to-all-start.5 = ((f32[32,16,128]{2,1,0:T(8,128)}), f32[32,16,128]{2,1,0:T(8,128)S(1)}, u32[]{:S(2)}, u32[]{:S(2)}) async-start(f32[32,16,128]{2,1,0:T(8,128)} %broadcast_in_dim.11), calls=%async_computation.5 | async-start | bytes 524288 | tf_op jit(solution)/shard_map/all_to_all | solution.py:402
  113.8 0.7 mul.20
  114.5 10.0 %all-to-all-done.5 = f32[32,16,128]{2,1,0:T(8,128)S(1)} async-done(((f32[32,16,128]{2,1,0:T(8,128)}), f32[32,16,128]{2,1,0:T(8,128)S(1)}, u32[]{:S(2)}, u32[]{:S(2)}) %all-to-all-start.5) | async-done | bytes 262176 | tf_op jit(solution)/shard_map/all_to_all | solution.py:402
  124.5 0.1 copy.11
  124.6 0.6 slice.32
  125.2 0.6 slice.33
  (21 shorter events, 0.2 us)
Async XLA Ops:
  0.6 9.9 %copy-start.13 = (bf16[1,128,2048]{2,1,0:T(8,128)(2,1)S(1)}, bf16[1,128,2048]{2,1,0:T(8,128)(2,1)}, u32[]{:S(2)}) copy-start(bf16[1,128,2048]{2,1,0:T(8,128)(2,1)} %upstream.1) | copy-start | bytes 1572868
  0.6 17.3 %copy-start.14 = (f32[3,6144]{1,0:T(4,128)S(1)}, f32[3,6144]{1,0:T(4,128)}, u32[]{:S(2)}) copy-start(f32[3,6144]{1,0:T(4,128)} %taps.1) | copy-start | bytes 221188
  0.7 17.3 %copy-start.15 = (s32[1,8]{1,0:T(1,128)S(1)}, s32[1,8]{1,0:T(1,128)}, u32[]{:S(2)}) copy-start(s32[1,8]{1,0:T(1,128)} %lengths.9) | copy-start | bytes 100
  2.2 26.2 %all-to-all-start = ((f32[8,33,256]{2,1,0:T(8,128)}), f32[8,33,256]{2,1,0:T(8,128)S(1)}, u32[]{:S(2)}, u32[]{:S(2)}) async-start(f32[8,33,256]{2,1,0:T(8,128)} %broadcast_in_dim.9), calls=%async_computation | async-start | bytes 655360 | tf_op jit(solution)/shard_map/all_to_all | solution.py:402
  10.6 7.4 %collective-permute-start.1 = (bf16[2,8192]{1,0:T(2,128)(2,1)S(1)}, bf16[2,8192]{1,0:T(2,128)(2,1)S(1)}, u32[]{:S(2)}, u32[]{:S(2)}) collective-permute-start(bf16[2,8192]{1,0:T(2,128)(2,1)S(1)} %pad_maximum_fusion.1), channel_id=1, source_target_pairs={{1,0},{2,1},{3,2},{4,3},{5,4},{6,5},{7,6},{9,8},{10,9},{11,10},{12... | collective-permute-start | bytes 98312 | tf_op jit(solution)/shard_map/ppermute | solution.py:22
  11.9 6.1 %collective-permute-start = (bf16[2,6144]{1,0:T(2,128)(2,1)S(1)}, bf16[2,6144]{1,0:T(2,128)(2,1)S(1)}, u32[]{:S(2)}, u32[]{:S(2)}) collective-permute-start(bf16[2,6144]{1,0:T(2,128)(2,1)S(1)} %get-tuple-element.39), channel_id=1, source_target_pairs={{0,1},{1,2},{2,3},{3,4},{4,5},{5,6},{6,7},{8,9},{9,10},{10,11},{11... | collective-permute-start | bytes 73736 | tf_op jit(solution)/shard_map/ppermute | solution.py:22
  17.9 1.4 %copy-start.2 = (bf16[1,128,6144]{2,1,0:T(8,128)(2,1)S(1)}, bf16[1,128,6144]{2,1,0:T(8,128)(2,1)}, u32[]{:S(2)}) copy-start(bf16[1,128,6144]{2,1,0:T(8,128)(2,1)} %features.3) | copy-start | bytes 4718596
  23.8 1.7 %copy-start = (f32[6336,128]{1,0:T(8,128)}, f32[6336,128]{1,0:T(8,128)S(1)}, u32[]{:S(2)}) copy-start(f32[6336,128]{1,0:T(8,128)S(1)} %get-tuple-element.21.feat) | copy-start | bytes 9732100
  25.4 1.0 copy-start.3
  26.4 1.0 copy-start.5
  27.4 1.0 copy-start.7
  33.6 20.7 %all-to-all-start.1 = ((bf16[8,2,128,128]{3,2,1,0:T(8,128)(2,1)}), bf16[8,2,128,128]{3,2,1,0:T(8,128)(2,1)S(1)}, u32[]{:S(2)}, u32[]{:S(2)}) async-start(bf16[8,2,128,128]{3,2,1,0:T(8,128)(2,1)} %get-tuple-element.30), calls=%async_computation.1 | async-start | bytes 1048576 | tf_op jit(solution)/shard_map/all_to_all | solution.py:402
  52.4 1.0 copy-start.9
  53.4 1.0 copy-start.11
  54.4 1.7 %copy-start.4 = (f32[2080,128]{1,0:T(8,128)S(1)}, f32[2080,128]{1,0:T(8,128)}, u32[]{:S(2)}) copy-start(f32[2080,128]{1,0:T(8,128)} %copy-done.3) | copy-start | bytes 3194884
  56.0 1.9 %copy-start.1 = (f32[6336,128]{1,0:T(8,128)S(1)}, f32[6336,128]{1,0:T(8,128)}, u32[]{:S(2)}) copy-start(f32[6336,128]{1,0:T(8,128)} %copy-done) | copy-start | bytes 9732100
  57.9 1.2 copy-start.6
  59.2 1.2 copy-start.8
  60.4 1.2 copy-start.10
  61.6 1.2 copy-start.12
  86.2 13.2 %all-to-all-start.4 = ((f32[32,16,128]{2,1,0:T(8,128)}), f32[32,16,128]{2,1,0:T(8,128)S(1)}, u32[]{:S(2)}, u32[]{:S(2)}) async-start(f32[32,16,128]{2,1,0:T(8,128)} %bitcast.5), calls=%async_computation.4 | async-start | bytes 524288 | tf_op jit(solution)/shard_map/all_to_all | solution.py:402
  100.2 10.3 %all-to-all-start.3 = ((f32[32,8,128]{2,1,0:T(8,128)}), f32[32,8,128]{2,1,0:T(8,128)S(1)}, u32[]{:S(2)}, u32[]{:S(2)}) async-start(f32[32,8,128]{2,1,0:T(8,128)} %broadcast_in_dim.10), calls=%async_computation.3 | async-start | bytes 262144 | tf_op jit(solution)/shard_map/all_to_all | solution.py:402
  111.2 13.2 %all-to-all-start.5 = ((f32[32,16,128]{2,1,0:T(8,128)}), f32[32,16,128]{2,1,0:T(8,128)S(1)}, u32[]{:S(2)}, u32[]{:S(2)}) async-start(f32[32,16,128]{2,1,0:T(8,128)} %broadcast_in_dim.11), calls=%async_computation.5 | async-start | bytes 524288 | tf_op jit(solution)/shard_map/all_to_all | solution.py:402

commit v3 on v1

v3 whole, which is shorter than its diff:
```python
import functools
import math

import jax
import jax.numpy as jnp
from jax import lax
from jax.experimental import pallas as pl
from jax.experimental.pallas import tpu as pltpu
from jax.sharding import PartitionSpec as P

F32 = jnp.float32
BF16 = jnp.bfloat16
LANES = 128
SUB = 8
GROUP = SUB * LANES
HALO = 2


def shifted(block, axis, distance):
    count = lax.axis_size(axis)
    route = [(i - distance, i) for i in range(count) if 0 <= i - distance < count]
    return lax.ppermute(block, axis, route)


def vec(ref, index):
    return ref[pl.ds(pl.multiple_of(index * SUB, SUB), SUB), :]


def put(ref, index, value):
    ref[pl.ds(pl.multiple_of(index * SUB, SUB), SUB), :] = value


def spread(dst, first, src, row_count):
    for j in range(SUB):
        value = src[:, j * LANES : (j + 1) * LANES].astype(F32)
        dst[pl.ds(first * SUB + j, row_count, stride=SUB), :] = value


def spread_rows(dst, first, src, row_count):
    def step(i, carry):
        for j in range(SUB):
            value = src[0, pl.ds(pl.multiple_of(i * 16, 16), 16), j * LANES : (j + 1) * LANES]
            dst[pl.ds((i * 16 + first) * SUB + j, 16, stride=SUB), :] = value.astype(F32)
        return carry

    lax.fori_loop(0, row_count // 16, step, 0)


def spread_params(dst, par, rows):
    pieces, _, width = par.shape
    for j in range(SUB):
        if width >= LANES:
            per = width // LANES
            at = (j % per) * LANES
            parts = [(j // per, at, LANES)]
        else:
            per = LANES // width
            parts = [(j * per + i, 0, width) for i in range(per)]
        for first in range(0, rows, SUB):
            many = min(SUB, rows - first)
            got = [par[k, first : first + many, at : at + w] for k, at, w in parts]
            value = got[0] if len(got) == 1 else jnp.concatenate(got, axis=1)
            dst[pl.ds(first * SUB + j, many, stride=SUB), :] = value


def segment_starts(lengths):
    starts = [jnp.int32(0)]
    for j in range(lengths.shape[1]):
        starts.append(starts[-1] + lengths[0, j])
    return starts


def fill_keep(keep, starts, base, rows):
    count = rows + HALO + 2

    def step(i, carry):
        keep[i] = jnp.float32(1.0)
        return carry

    lax.fori_loop(0, count, step, 0, unroll=4)
    for start in starts:
        at = start - base + 1

        @pl.when((at >= 0) & (at < count))
        def _():
            keep[at] = jnp.float32(0.0)


def rounded(value):
    return value.astype(BF16).astype(F32)


def flag(condition):
    return jnp.where(condition, 1.0, 0.0).astype(F32)


def featured(feat, tap, p, keep_one, keep_two):
    return (
        tap[0] * vec(feat, p + 2)
        + tap[1] * (keep_one * vec(feat, p + 1))
        + tap[2] * (keep_two * vec(feat, p))
    )


def spread_inputs(rows, inputs, feats, up, taps):
    cur, left, right, tap_rows = inputs[0:4], inputs[4:7], inputs[7:11], inputs[11:14]
    for third in range(3):
        feat, first = feats[third]
        spread_rows(feat, first + HALO, cur[third], rows)
        spread(feat, first, left[third], HALO)
        spread(feat, first + rows + HALO, right[third], HALO)
        spread(taps, third * 3, tap_rows[third], 3)
    spread_rows(up, 0, cur[3], rows)
    spread(up, rows, right[3], HALO)


def features_kernel(rows, lengths, *refs):
    inputs, (mixed, gout), (query_in, key_in, val_in, up, taps, keep) = (
        refs[:14], refs[14:16], refs[16:],
    )
    base = lax.axis_index("ctx") * rows
    fill_keep(keep, segment_starts(lengths), base, rows)
    feats = (query_in, key_in, val_in)
    spread_inputs(rows, inputs, [(feat, 0) for feat in feats], up, taps)
    tap = [[vec(taps, third * 3 + j) for j in range(3)] for third in range(3)]

    def product(p, carry):
        keep_one = keep[p + 1]
        keep_two = keep_one * keep[p]
        query, key, val = (featured(feats[i], tap[i], p, keep_one, keep_two) for i in range(3))
        put(mixed, p, rounded(key * val))
        put(gout, p, rounded(vec(up, p) * query))
        return carry

    lax.fori_loop(0, rows + HALO, product, 0, unroll=2)


def ends_kernel(rows, lengths, params, mixed, gout, payload, own, par, stack, zero_scr):
    me = lax.axis_index("ctx")
    base = me * rows
    count = payload.shape[0]
    poles = (params.shape[1] - 1) // 2
    extended = rows + HALO
    low, high = jnp.int32(0), jnp.int32(extended)
    for start in segment_starts(lengths):
        at = start - base
        low = jnp.where(at < rows, jnp.maximum(low, at), low)
        high = jnp.where(at > HALO, jnp.minimum(high, at), high)
    zero_scr[...] = jnp.zeros((SUB, LANES), F32)
    zeros = [zero_scr[...]] * poles
    spread_params(par, params, poles)
    decay = [jnp.exp(-jnp.exp(vec(par, m))) for m in range(poles)]

    def sweep(i, carry):
        state, adjoint = carry
        back = extended - 1 - i
        x = vec(mixed, i) * flag(i >= low)
        g = vec(gout, back) * flag(back < high)
        state = [decay[m] * state[m] + x for m in range(poles)]
        adjoint = [decay[m] * adjoint[m] + g for m in range(poles)]
        return state, adjoint

    state, adjoint = lax.fori_loop(0, rows, sweep, (zeros, zeros), unroll=2)
    for m in range(poles):
        put(own, m, state[m])
    for m in range(0, poles, 2):
        at = slice(m * SUB, (m + 2) * SUB)
        stack[0, at, :] = jnp.concatenate(state[m : m + 2], axis=0).astype(BF16)
        stack[1, at, :] = jnp.concatenate(adjoint[m : m + 2], axis=0).astype(BF16)
    for e in range(count):
        payload[e] = stack[jnp.where(e > me, 0, 1)]


def local_kernel(rows, lengths, *refs):
    inputs, (params, mixed, gout) = refs[:14], refs[14:17]
    feat, taps, up, key_out, val_out, conv, adj, partial = refs[17:25]
    par, zero_scr, keep = refs[25:]
    base = lax.axis_index("ctx") * rows
    poles = (params.shape[1] - 1) // 2
    extended = rows + HALO
    padded = rows + 2 * HALO
    fill_keep(keep, segment_starts(lengths), base, rows)
    spread_inputs(rows, inputs, [(feat, third * padded) for third in range(3)], up, taps)
    tap = [[vec(taps, third * 3 + j) for j in range(3)] for third in range(3)]

    def product(p, carry):
        keep_one = keep[p + 1]
        keep_two = keep_one * keep[p]
        put(key_out, p, featured(feat, tap[1], padded + p, keep_one, keep_two))
        put(val_out, p, featured(feat, tap[2], 2 * padded + p, keep_one, keep_two))
        return carry

    lax.fori_loop(0, extended, product, 0, unroll=2)
    zero_scr[...] = jnp.zeros((SUB, LANES), F32)
    zero = zero_scr[...]
    per_pass = poles // 2
    zeros = [zero] * per_pass
    spread_params(par, params, 2 * poles)
    for part in range(2):
        chosen = list(range(part * per_pass, (part + 1) * per_pass))
        decay = [jnp.exp(-jnp.exp(vec(par, m))) for m in chosen]
        coeff = [vec(par, poles + m) for m in chosen]

        def sweep(i, carry):
            state, adjoint, resid, skip = carry
            back = extended - 1 - i
            x = vec(mixed, i)
            g = vec(gout, back)
            own = vec(mixed, back) * flag(back < rows)
            keep_fwd = keep[i + 1]
            keep_bwd = keep[back + 2]
            state = [decay[m] * (state[m] * keep_fwd) + x for m in range(per_pass)]
            adjoint = [decay[m] * (adjoint[m] * keep_bwd) + g for m in range(per_pass)]
            resid = [resid[m] + own * adjoint[m] for m in range(per_pass)]
            forward = sum(coeff[m] * state[m] for m in range(per_pass))
            backward = sum(coeff[m] * adjoint[m] for m in range(per_pass))
            if part == 0:
                put(conv, i, forward)
                put(adj, back, backward)
                skip = skip + own * g
            else:
                put(conv, i, forward + vec(conv, i))
                put(adj, back, backward + vec(adj, back))
            return state, adjoint, resid, skip

        _, _, resid, skip = lax.fori_loop(
            0, extended, sweep, (zeros, zeros, zeros, zero), unroll=2
        )
        for i, m in enumerate(chosen):
            put(partial, m, resid[i])
        if part == 0:
            put(partial, poles, skip)


def carry_states(rows, lengths, params, arrived, own, partial, sums, before, after, par, zeros):
    me = lax.axis_index("ctx")
    half = pl.program_id(0)
    groups = pl.num_programs(0)
    base = me * rows
    count = arrived.shape[0]
    poles = (params.shape[1] - 1) // 2
    extended = rows + HALO
    first, last, newest = jnp.int32(0), jnp.int32(2**30), jnp.int32(0)
    for start in segment_starts(lengths):
        first = jnp.where(start <= base, jnp.maximum(first, start), first)
        last = jnp.where(start > base + extended, jnp.minimum(last, start), last)
        newest = jnp.where(start <= base + extended, jnp.maximum(newest, start), newest)
    through = flag(newest < base + rows)
    per_pass = poles // 2
    zeros = zeros[:per_pass]
    for part in range(2):
        chosen = list(range(part * per_pass, (part + 1) * per_pass))
        rate = [jnp.exp(vec(par, m)) for m in chosen]
        block = [jnp.exp(-rows * r) for r in rate]

        def arrived_states(d):
            got = []
            for m in range(chosen[0], chosen[-1] + 1, 2):
                pair = arrived[d, m * SUB : (m + 2) * SUB, :].astype(F32)
                got += [pair[:SUB], pair[SUB:]]
            return got

        def from_before(d, carry):
            joined = flag((d + 1) * rows - 1 >= first)
            got = arrived_states(d)
            return [block[i] * carry[i] + joined * got[i] for i in range(per_pass)]

        def from_after(i, carry):
            d = count - 1 - i
            joined = flag(d * rows + HALO < last)
            got = arrived_states(d)
            return [block[i] * carry[i] + joined * got[i] for i in range(per_pass)]

        state = lax.fori_loop(0, me, from_before, zeros)
        adjoint = lax.fori_loop(0, count - 1 - me, from_after, zeros)
        for i, m in enumerate(chosen):
            put(before, m, state[i])
            put(after, m, adjoint[i])
            cross = jnp.exp(-(HALO + 1) * rate[i]) * (adjoint[i] * through)
            put(sums, (9 + m) * groups + half, vec(partial, m) + cross * vec(own, m))
    put(sums, (9 + poles) * groups + half, vec(partial, poles))


def finish_kernel(rows, lengths, *refs):
    params, arrived, own, partial, taps = refs[0:5]
    far, grads, sums_out = refs[5:13], refs[13], refs[14]
    near, (sums, before, after, par, post, zero_scr, keep, sems) = refs[15:23], refs[23:]
    half = pl.program_id(0)
    groups = pl.num_programs(0)
    base = lax.axis_index("ctx") * rows
    poles = (params.shape[1] - 1) // 2
    extended = rows + HALO
    padded = rows + 2 * HALO

    def copies(group):
        return [
            pltpu.make_async_copy(far[i].at[group], near[i].at[group], sems.at[i, group])
            for i in range(len(far))
        ]

    @pl.when(half == 0)
    def _():
        for group in range(far[0].shape[0]):
            for copy in copies(group):
                copy.start()

    starts = segment_starts(lengths)
    fill_keep(keep, starts, base, rows)
    until, since = jnp.int32(extended), jnp.int32(0)
    for start in starts:
        at = start - base
        until = jnp.where(at >= 0, jnp.minimum(until, at), until)
        since = jnp.where(at <= extended, jnp.maximum(since, at), since)
    steps = jnp.maximum(until, extended - since)
    zero_scr[...] = jnp.zeros((SUB, LANES), F32)
    zero = zero_scr[...]
    spread_params(par, params, 2 * poles + 1)
    carry_states(
        rows, lengths, params, arrived, own, partial, sums, before, after, par, [zero] * poles
    )
    decay = [jnp.exp(-jnp.exp(vec(par, m))) for m in range(poles)]
    enter = [vec(par, poles + m) * (decay[m] * vec(before, m)) for m in range(poles)]
    leave = [vec(par, poles + m) * (decay[m] * vec(after, m)) for m in range(poles)]
    for copy in copies(half):
        copy.wait()
    conv, adj, up, mixed, gout, key_in, val_in, feat = [ref.at[half] for ref in near]

    def carried(i, carry):
        enter, leave = carry
        for step in range(2):
            p = 2 * i + step
            back = extended - 1 - p
            put(conv, p, vec(conv, p) + flag(p < until) * sum(enter))
            put(adj, back, vec(adj, back) + flag(back >= since) * sum(leave))
            enter = [decay[m] * enter[m] for m in range(poles)]
            leave = [decay[m] * leave[m] for m in range(poles)]
        return enter, leave

    lax.fori_loop(0, (steps + 1) // 2, carried, (enter, leave))
    gain = vec(par, 2 * poles)
    tap = [[vec(taps, third * 3 + j) for j in range(3)] for third in range(3)]

    def finish(i, carry):
        one, two, tap_sums = carry
        p = extended - 1 - i
        mine = flag(p < rows)
        conv_out = rounded(vec(conv, p) + gain * vec(mixed, p))
        grad_mixed = rounded(vec(adj, p) + gain * vec(gout, p))
        now = [vec(up, p) * conv_out, grad_mixed * vec(val_in, p), grad_mixed * vec(key_in, p)]
        keep_one = keep[p + 1]
        keep_two = keep_one * keep[p]
        next_one = keep[p + 2]
        next_two = next_one * keep[jnp.minimum(p + 3, extended + 1)]
        new_sums = []
        for third in range(3):
            back = (
                tap[third][0] * now[third]
                + tap[third][1] * (next_one * one[third])
                + tap[third][2] * (next_two * two[third])
            )
            put(post, third * extended + p, back)
            mine_now = now[third] * mine
            at = third * padded + p
            new_sums += [
                tap_sums[3 * third] + mine_now * vec(feat, at + 2),
                tap_sums[3 * third + 1] + mine_now * (keep_one * vec(feat, at + 1)),
                tap_sums[3 * third + 2] + mine_now * (keep_two * vec(feat, at)),
            ]
        return now, one, new_sums

    _, _, tap_sums = lax.fori_loop(
        0, extended, finish, ([zero] * 3, [zero] * 3, [zero] * 9), unroll=2
    )
    for third in range(3):
        for j in range(3):
            put(sums, (3 * j + third) * groups + half, tap_sums[3 * third + j])

    def write(i, carry):
        for third in range(3):
            for j in range(SUB):
                first = (third * extended + i * 16) * SUB + j
                value = post[pl.ds(first, 16, stride=SUB), :]
                column = (third * groups + half) * GROUP + j * LANES
                lanes = pl.ds(pl.multiple_of(column, LANES), LANES)
                grads[0, pl.ds(pl.multiple_of(i * 16, 16), 16), lanes] = value.astype(BF16)
        return carry

    lax.fori_loop(0, rows // 16, write, 0)

    @pl.when(half == groups - 1)
    def _():
        sums_out[...] = sums[...].astype(BF16)


def swap(block, axes):
    return lax.all_to_all(block, axes, split_axis=0, concat_axis=0, tiled=True)


def per_device(features, upstream, lengths, conv_taps, residues, log_rate, skip_gain):
    rows = features.shape[1]
    channels = upstream.shape[2]
    poles = residues.shape[0]
    ctx_count = lax.axis_size("ctx")
    total = ctx_count * lax.axis_size("dp")
    shard_index = lax.axis_index("ctx")
    per_shard = channels // ctx_count
    groups = channels // GROUP
    grad_scale = 1.0 / math.sqrt(rows * total)
    extended = rows + HALO
    padded = rows + 2 * HALO
    limits = pltpu.CompilerParams(
        dimension_semantics=("arbitrary",), vmem_limit_bytes=58 * 1024 * 1024
    )

    def tall(height):
        return jax.ShapeDtypeStruct((groups, height * SUB, LANES), F32)

    def tall_spec(height):
        return pl.BlockSpec((None, height * SUB, LANES), lambda h: (h, 0, 0))

    def scratch(height):
        return pltpu.VMEM((height * SUB, LANES), F32)

    def row_spec(third):
        return pl.BlockSpec((1, rows, GROUP), lambda h: (0, 0, third * groups + h))

    def edge_spec(height, third):
        return pl.BlockSpec((height, GROUP), lambda h: (0, third * groups + h))

    smem = pl.BlockSpec(memory_space=pltpu.SMEM)
    anywhere = pl.BlockSpec(memory_space=pl.ANY)
    keep = pltpu.SMEM((rows + 8,), F32)

    def call(kernel, name, operands, in_specs, outs, out_specs, scratch_shapes):
        return pl.pallas_call(
            functools.partial(kernel, rows),
            out_shape=outs,
            grid=(groups,),
            in_specs=[smem] + in_specs,
            out_specs=out_specs,
            scratch_shapes=scratch_shapes,
            compiler_params=limits,
            name=name,
        )(lengths, *operands)

    edge = features[0, rows - HALO :, :]
    head = jnp.concatenate([features[0, :HALO, :], upstream[0, :HALO, :]], axis=1)
    left = shifted(edge, "ctx", 1)
    right = shifted(head, "ctx", -1)
    params = jnp.concatenate([log_rate, residues, skip_gain[None]], axis=0)
    params = swap(jnp.broadcast_to(params[None], (ctx_count,) + params.shape), "ctx")
    params_spec = pl.BlockSpec(
        (ctx_count // groups, 2 * poles + 1, per_shard), lambda h: (h, 0, 0)
    )

    inputs = [features] * 3 + [upstream] + [left] * 3 + [right] * 4 + [conv_taps] * 3
    input_specs = (
        [row_spec(0), row_spec(1), row_spec(2), row_spec(0)]
        + [edge_spec(HALO, i) for i in range(3)]
        + [edge_spec(HALO, i) for i in range(4)]
        + [edge_spec(3, i) for i in range(3)]
    )
    mixed, gout = call(
        features_kernel,
        "features",
        inputs,
        input_specs,
        [tall(extended)] * 2,
        [tall_spec(extended)] * 2,
        [scratch(padded)] * 3 + [scratch(extended), scratch(9), keep],
    )
    state_rows = poles * SUB
    payload_spec = pl.BlockSpec((ctx_count, None, state_rows, LANES), lambda h: (0, h, 0, 0))
    payload, own = call(
        ends_kernel,
        "ends",
        [params, mixed, gout],
        [params_spec] + [tall_spec(extended)] * 2,
        [jax.ShapeDtypeStruct((ctx_count, groups, state_rows, LANES), BF16), tall(poles)],
        [payload_spec, tall_spec(poles)],
        [scratch(poles), pltpu.VMEM((2, state_rows, LANES), BF16), scratch(1)],
    )
    arrived = swap(payload, "ctx")
    heights = [3 * padded, 9] + [extended] * 5 + [poles + 1]
    feat, tap_rows, up, key, val, conv, adj, partial = call(
        local_kernel,
        "local",
        inputs + [params, mixed, gout],
        input_specs + [params_spec] + [tall_spec(extended)] * 2,
        [tall(height) for height in heights],
        [tall_spec(height) for height in heights],
        [scratch(2 * poles), scratch(1), keep],
    )
    far = [conv, adj, up, mixed, gout, key, val, feat]
    used = (10 + poles) * groups * SUB
    share = -(-used // (total * 16)) * 16
    grads, sums = call(
        finish_kernel,
        "finish",
        [params, arrived, own, partial, tap_rows] + far,
        [params_spec, payload_spec, tall_spec(poles), tall_spec(poles + 1), tall_spec(9)]
        + [anywhere] * len(far),
        [
            jax.ShapeDtypeStruct(features.shape, BF16),
            jax.ShapeDtypeStruct((total * share, LANES), BF16),
        ],
        [
            pl.BlockSpec(features.shape, lambda h: (0, 0, 0)),
            pl.BlockSpec((total * share, LANES), lambda h: (0, 0)),
        ],
        [pltpu.VMEM(array.shape, F32) for array in far]
        + [pltpu.VMEM((total * share, LANES), F32)]
        + [scratch(poles)] * 2
        + [scratch(2 * poles + 1), scratch(3 * extended), scratch(1), keep]
        + [pltpu.SemaphoreType.DMA((len(far), groups))],
    )

    both = ("dp", "ctx")
    parts = swap(sums.reshape(total, share, LANES), both).astype(F32)
    mine = (jnp.sum(parts, axis=0) * grad_scale).astype(BF16)
    whole = swap(jnp.broadcast_to(mine[None], parts.shape), both).reshape(total * share, LANES)
    width = groups * SUB
    grad_taps = whole[: 9 * width].reshape(3, 3 * channels).astype(F32)
    rest = whole[9 * width : used].reshape(poles + 1, channels)
    rest = lax.dynamic_slice(rest, (0, shard_index * per_shard), (poles + 1, per_shard))
    rest = rest.astype(F32)
    return grads, grad_taps, rest[:poles], rest[poles]


def solution(mesh):
    return jax.shard_map(
        per_device,
        mesh=mesh,
        in_specs=(
            P("dp", "ctx", None),
            P("dp", "ctx", None),
            P("dp", None),
            P(),
            P(None, "ctx"),
            P(None, "ctx"),
            P("ctx"),
        ),
        out_specs=(P("dp", "ctx", None), P(), P(None, "ctx"), P("ctx")),
        check_vma=False,
    )
```

time: 101 us -> 99.7 us (0.987)
  blocking collectives: 32.6 us -> 16.1 us
  Pallas kernels: 28.9 us -> 40.8 us
  starting transfers between devices: 15.7 us -> 23.4 us
  waiting for transfers between devices: 13.7 us -> 9.24 us
    all_to_all x2 -> x1, blocking collectives: 32.6 us -> 16.1 us  [swap(): return lax.all_to_all(block, axes, split_axis=0, concat_axis=0, tiled=True)]
    pallas_call x2 -> x4, Pallas kernels: 28.9 us -> 40.8 us  [call(): pl.pallas_call(functools.partial(kernel, rows), out_shape=outs, grid=(gro...]
    all_to_all x2 -> x3, starting transfers between devices: 9.86 us -> 17.6 us  [swap(): return lax.all_to_all(block, axes, split_axis=0, concat_axis=0, tiled=True)]
    all_to_all x2 -> x3, waiting for transfers between devices: 12.2 us -> 7.74 us  [swap(): return lax.all_to_all(block, axes, split_axis=0, concat_axis=0, tiled=True)]
  transfers between devices with their start and end apart: 4 -> 5, of which waited for: 3 -> 2; matrix products, arithmetic and copies ran while one was open for 2% -> 2% of each run, Pallas kernels for 0% -> 24%
where the time goes in v3:
time: 99.7 us; the launch traced here: 98.9 us
  Pallas kernels  40.8 us (41%)
  starting transfers between devices  23.4 us (23%)
  blocking collectives  16.1 us (16%)
  waiting for transfers between devices  9.24 us (9%)
  local copies, waits for them, and re-layouts  7.76 us (8%)
    pallas_call x4, Pallas kernels, call(): pl.pallas_call(functools.partial(kernel, rows), out_shape=outs, grid=(gro...  40.8 us
    all_to_all x3, starting transfers between devices, swap(): return lax.all_to_all(block, axes, split_axis=0, concat_axis=0, tiled=True)  17.6 us
    all_to_all x1, blocking collectives, swap(): return lax.all_to_all(block, axes, split_axis=0, concat_axis=0, tiled=True)  16.1 us
    all_to_all x3, waiting for transfers between devices, swap(): return lax.all_to_all(block, axes, split_axis=0, concat_axis=0, tiled=True)  7.74 us
    ppermute x2, starting transfers between devices, shifted(): return lax.ppermute(block, axis, route)  5.85 us
    unnamed x10, local copies, waits for them, and re-layouts  2.75 us
  transfers between devices with their start and end apart: 5, of which 2 were waited for; matrix products, arithmetic and copies ran while one was open for 2% of the time, Pallas kernels for 24%

profile of v3, /device:TPU:0, one launch (start us, length us, event | category | flops | bytes accessed | tf_op | source)
XLA Modules:
  0.0 98.9 jit_solution(4408968055696361549)
XLA Ops:
  0.6 0.8 pad_maximum_fusion
  1.4 0.7 broadcast_in_dim.7
  2.1 7.3 %all-to-all-start = ((f32[8,33,256]{2,1,0:T(8,128)}), f32[8,33,256]{2,1,0:T(8,128)S(1)}, u32[]{:S(2)}, u32[]{:S(2)}) async-start(f32[8,33,256]{2,1,0:T(8,128)} %broadcast_in_dim.7), calls=%async_computation | async-start | bytes 655360 | tf_op jit(solution)/shard_map/all_to_all | solution.py:396
  9.4 1.0 slice_bitcast_fusion
  10.4 0.8 slice_bitcast_fusion.2
  11.2 1.3 %collective-permute-start.1 = (bf16[2,8192]{1,0:T(2,128)(2,1)S(1)}, bf16[2,8192]{1,0:T(2,128)(2,1)S(1)}, u32[]{:S(2)}, u32[]{:S(2)}) collective-permute-start(bf16[2,8192]{1,0:T(2,128)(2,1)S(1)} %pad_maximum_fusion.1), channel_id=1, source_target_pairs={{1,0},{2,1},{3,2},{4,3},{5,4},{6,5},{7,6},{9,8},{10,9},{11,10},{12... | collective-permute-start | bytes 98312 | tf_op jit(solution)/shard_map/ppermute | solution.py:22
  12.5 4.6 %collective-permute-start = (bf16[2,6144]{1,0:T(2,128)(2,1)S(1)}, bf16[2,6144]{1,0:T(2,128)(2,1)S(1)}, u32[]{:S(2)}, u32[]{:S(2)}) collective-permute-start(bf16[2,6144]{1,0:T(2,128)(2,1)S(1)} %get-tuple-element.33), channel_id=1, source_target_pairs={{0,1},{1,2},{2,3},{3,4},{4,5},{5,6},{6,7},{8,9},{9,10},{10,11},{11... | collective-permute-start | bytes 73736 | tf_op jit(solution)/shard_map/ppermute | solution.py:22
  17.1 1.5 %collective-permute-done.refs_4_.refs_5_.refs_6_ = bf16[2,6144]{1,0:T(2,128)(2,1)S(1)} collective-permute-done((bf16[2,6144]{1,0:T(2,128)(2,1)S(1)}, bf16[2,6144]{1,0:T(2,128)(2,1)S(1)}, u32[]{:S(2)}, u32[]{:S(2)}) %collective-permute-start) | collective-permute-done | bytes 24608 | tf_op jit(solution)/shard_map/ppermute | solution.py:22
  18.6 0.0 copy-start.3
  18.6 0.0 collective-permute-done.1.refs_7_.refs_8_.refs_9_.refs_10_
  18.6 0.6 copy-done.3
  19.2 0.0 copy-start.1
  19.2 0.6 copy-done.1
  19.8 6.2 %features.1 = (f32[2,1040,128]{2,1,0:T(8,128)}, f32[2,1040,128]{2,1,0:T(8,128)}) custom-call(s32[1,8]{1,0:T(1,128)} %lengths.7, bf16[1,128,6144]{2,1,0:T(8,128)(2,1)} %refs_2_.3, bf16[1,128,6144]{2,1,0:T(8,128)(2,1)} %refs_2_.3, bf16[1,128,6144]{2,1,0:T(8,128)(2,1)} %refs_2_.3, bf16[1,128,2048]{2,1,0:T(8,128)(2,1)} %refs_3_.3, bf16[2,6144]{1,0:T(2,128)(2,1)} %copy-done.3, ...), custom_call_target="tpu_custom_call" | custom-call | tf_op jit(solution)/shard_map/features/pallas_call | solution.py:435
  25.9 0.0 all-to-all-done.params.refs_14_.refs_0_
  25.9 0.0 copy-start
  26.0 0.7 copy-done
  26.7 5.9 %ends.1 = (bf16[8,2,128,128]{3,2,1,0:T(8,128)(2,1)}, f32[2,128,128]{2,1,0:T(8,128)}) custom-call(s32[1,8]{1,0:T(1,128)} %lengths.7, f32[8,33,256]{2,1,0:T(8,128)} %copy-done, f32[2,1040,128]{2,1,0:T(8,128)} %get-tuple-element.18.mixed.refs_15_.refs_8_, f32[2,1040,128]{2,1,0:T(8,128)} %get-tuple-element.19.gout.refs_16_.refs_9_), custom_call_target="tpu_custom_call" | custom-call | tf_op jit(solution)/shard_map/ends/pallas_call | solution.py:435
  32.5 7.7 %all-to-all-start.1 = ((bf16[8,2,128,128]{3,2,1,0:T(8,128)(2,1)}), bf16[8,2,128,128]{3,2,1,0:T(8,128)(2,1)S(1)}, u32[]{:S(2)}, u32[]{:S(2)}) async-start(bf16[8,2,128,128]{3,2,1,0:T(8,128)(2,1)} %get-tuple-element.20), calls=%async_computation.1 | async-start | bytes 1048576 | tf_op jit(solution)/shard_map/all_to_all | solution.py:396
  40.3 17.1 %local.1 = (f32[2,3168,128]{2,1,0:T(8,128)}, f32[2,72,128]{2,1,0:T(8,128)}, f32[2,1040,128]{2,1,0:T(8,128)}, f32[2,1040,128]{2,1,0:T(8,128)}, f32[2,1040,128]{2,...) custom-call(s32[1,8]{1,0:T(1,128)} %lengths.7, ...), custom_call_target="tpu_custom_call" | custom-call | tf_op jit(solution)/shard_map/local/pallas_call | solution.py:435
  57.4 0.0 all-to-all-done.1.refs_1_
  57.4 0.0 copy-start.2
  57.4 0.8 copy-done.2
  58.2 11.6 %finish.1 = (bf16[1,128,6144]{2,1,0:T(8,128)(2,1)}, bf16[512,128]{1,0:T(8,128)(2,1)}) custom-call(s32[1,8]{1,0:T(1,128)} %lengths.7, f32[8,33,256]{2,1,0:T(8,128)} %copy-done, bf16[8,2,128,128]{3,2,1,0:T(8,128)(2,1)} %copy-done.2, f32[2,128,128]{2,1,0:T(8,128)} %get-tuple-element.21.refs_2_, f32[2,136,128]{2,1,0:T(8,128)} %get-tuple-element.22.refs_3_, ...), custom_call_target="tpu_custom_call" | custom-call | tf_op jit(solution)/shard_map/finish/pallas_call | solution.py:435
  69.8 16.1 %all_to_all.20 = bf16[32,16,128]{2,1,0:T(8,128)(2,1)S(1)} all-to-all(bf16[32,16,128]{2,1,0:T(8,128)(2,1)} %bitcast.13), channel_id=1, replica_groups=mesh['dp'=4,'ctx'=8] {'dp','ctx'}, dimensions={0} | all-to-all | bytes 262144 | tf_op jit(solution)/shard_map/all_to_all | solution.py:396
  86.0 0.7 broadcast_in_dim.8
  86.7 2.6 %all-to-all-start.3 = ((bf16[32,16,128]{2,1,0:T(8,128)(2,1)}), bf16[32,16,128]{2,1,0:T(8,128)(2,1)S(1)}, u32[]{:S(2)}, u32[]{:S(2)}) async-start(bf16[32,16,128]{2,1,0:T(8,128)(2,1)} %broadcast_in_dim.8), calls=%async_computation.3 | async-start | bytes 262144 | tf_op jit(solution)/shard_map/all_to_all | solution.py:396
  89.2 7.7 %all-to-all-done.3 = bf16[32,16,128]{2,1,0:T(8,128)(2,1)S(1)} async-done(((bf16[32,16,128]{2,1,0:T(8,128)(2,1)}), bf16[32,16,128]{2,1,0:T(8,128)(2,1)S(1)}, u32[]{:S(2)}, u32[]{:S(2)}) %all-to-all-start.3) | async-done | bytes 131104 | tf_op jit(solution)/shard_map/all_to_all | solution.py:396
  97.0 0.6 slice.32
  97.6 0.6 slice.33
  98.2 0.7 reshape.29
  (8 shorter events, 0.1 us)
Async XLA Ops:
  2.1 23.8 %all-to-all-start = ((f32[8,33,256]{2,1,0:T(8,128)}), f32[8,33,256]{2,1,0:T(8,128)S(1)}, u32[]{:S(2)}, u32[]{:S(2)}) async-start(f32[8,33,256]{2,1,0:T(8,128)} %broadcast_in_dim.7), calls=%async_computation | async-start | bytes 655360 | tf_op jit(solution)/shard_map/all_to_all | solution.py:396
  11.2 7.4 %collective-permute-start.1 = (bf16[2,8192]{1,0:T(2,128)(2,1)S(1)}, bf16[2,8192]{1,0:T(2,128)(2,1)S(1)}, u32[]{:S(2)}, u32[]{:S(2)}) collective-permute-start(bf16[2,8192]{1,0:T(2,128)(2,1)S(1)} %pad_maximum_fusion.1), channel_id=1, source_target_pairs={{1,0},{2,1},{3,2},{4,3},{5,4},{6,5},{7,6},{9,8},{10,9},{11,10},{12... | collective-permute-start | bytes 98312 | tf_op jit(solution)/shard_map/ppermute | solution.py:22
  12.5 6.1 %collective-permute-start = (bf16[2,6144]{1,0:T(2,128)(2,1)S(1)}, bf16[2,6144]{1,0:T(2,128)(2,1)S(1)}, u32[]{:S(2)}, u32[]{:S(2)}) collective-permute-start(bf16[2,6144]{1,0:T(2,128)(2,1)S(1)} %get-tuple-element.33), channel_id=1, source_target_pairs={{0,1},{1,2},{2,3},{3,4},{4,5},{5,6},{6,7},{8,9},{9,10},{10,11},{11... | collective-permute-start | bytes 73736 | tf_op jit(solution)/shard_map/ppermute | solution.py:22
  18.6 0.6 copy-start.3
  19.2 0.6 copy-start.1
  25.9 0.7 copy-start
  32.5 24.9 %all-to-all-start.1 = ((bf16[8,2,128,128]{3,2,1,0:T(8,128)(2,1)}), bf16[8,2,128,128]{3,2,1,0:T(8,128)(2,1)S(1)}, u32[]{:S(2)}, u32[]{:S(2)}) async-start(bf16[8,2,128,128]{3,2,1,0:T(8,128)(2,1)} %get-tuple-element.20), calls=%async_computation.1 | async-start | bytes 1048576 | tf_op jit(solution)/shard_map/all_to_all | solution.py:396
  57.4 0.8 copy-start.2
  86.7 10.3 %all-to-all-start.3 = ((bf16[32,16,128]{2,1,0:T(8,128)(2,1)}), bf16[32,16,128]{2,1,0:T(8,128)(2,1)S(1)}, u32[]{:S(2)}, u32[]{:S(2)}) async-start(bf16[32,16,128]{2,1,0:T(8,128)(2,1)} %broadcast_in_dim.8), calls=%async_computation.3 | async-start | bytes 262144 | tf_op jit(solution)/shard_map/all_to_all | solution.py:396

commit v4 on v2

v4 whole, which is shorter than its diff:
```python
import functools
import math

import jax
import jax.numpy as jnp
from jax import lax
from jax.experimental import pallas as pl
from jax.experimental.pallas import tpu as pltpu
from jax.sharding import PartitionSpec as P

F32 = jnp.float32
BF16 = jnp.bfloat16
LANES = 128
SUB = 8
GROUP = SUB * LANES
HALO = 2


def shifted(block, axis, distance):
    count = lax.axis_size(axis)
    route = [(i - distance, i) for i in range(count) if 0 <= i - distance < count]
    return lax.ppermute(block, axis, route)


def vec(ref, index):
    return ref[pl.ds(pl.multiple_of(index * SUB, SUB), SUB), :]


def put(ref, index, value):
    ref[pl.ds(pl.multiple_of(index * SUB, SUB), SUB), :] = value


def spread(dst, first, src, column, row_count):
    for j in range(SUB):
        lanes = pl.ds(pl.multiple_of(column + j * LANES, LANES), LANES)
        dst[pl.ds(first * SUB + j, row_count, stride=SUB), :] = src[:, lanes].astype(F32)


def spread_rows(dst, first, src, row_count):
    def step(i, carry):
        for j in range(SUB):
            value = src[pl.ds(pl.multiple_of(i * 16, 16), 16), j * LANES : (j + 1) * LANES]
            dst[pl.ds((i * 16 + first) * SUB + j, 16, stride=SUB), :] = value.astype(F32)
        return carry

    lax.fori_loop(0, row_count // 16, step, 0)


def spread_params(dst, par, half, groups):
    pieces, rows, width = par.shape
    base = half * (pieces // groups)
    for j in range(SUB):
        if width >= LANES:
            per = width // LANES
            at = (j % per) * LANES
            parts = [(j // per, at, LANES)]
        else:
            per = LANES // width
            parts = [(j * per + i, 0, width) for i in range(per)]
        for first in range(0, rows, SUB):
            many = min(SUB, rows - first)
            got = [par[base + k, first : first + many, at : at + w] for k, at, w in parts]
            value = got[0] if len(got) == 1 else jnp.concatenate(got, axis=1)
            dst[pl.ds(first * SUB + j, many, stride=SUB), :] = value


def segment_starts(lengths):
    starts = [jnp.int32(0)]
    for j in range(lengths.shape[1]):
        starts.append(starts[-1] + lengths[0, j])
    return starts


def fill_keep(keep, starts, base, rows):
    count = rows + HALO + 2

    def step(i, carry):
        keep[i] = jnp.float32(1.0)
        return carry

    lax.fori_loop(0, count, step, 0, unroll=4)
    for start in starts:
        at = start - base + 1

        @pl.when((at >= 0) & (at < count))
        def _():
            keep[at] = jnp.float32(0.0)


def rounded(value):
    return value.astype(BF16).astype(F32)


def flag(condition):
    return jnp.where(condition, 1.0, 0.0).astype(F32)


def unroll_of(trips):
    return max(d for d in range(1, 14) if trips % d == 0)


def featured(feat, tap, p, keep_one, keep_two):
    return (
        tap[0] * vec(feat, p + 2)
        + tap[1] * (keep_one * vec(feat, p + 1))
        + tap[2] * (keep_two * vec(feat, p))
    )


def each_group(groups, body):
    def step(half, carry):
        body(half)
        return carry

    lax.fori_loop(0, groups, step, 0)


def group_copies(sources, targets, sems, half):
    return [
        pltpu.make_async_copy(source.at[half], target.at[half], sems.at[half, i])
        for i, (source, target) in enumerate(zip(sources, targets))
    ]


def start_all(copies):
    for copy in copies:
        copy.start()


def wait_all(copies):
    for copy in copies:
        copy.wait()


def ends_kernel(
    rows, groups, far_lengths, features, upstream, left, right, taps, params,
    payload, feat_out, up_out, mixed_out, gout_out, par_out, tap_out,
    lengths, raw, raw_up, feat, up, mixed, gout, par, tap, stack, zero_scr, keep,
    length_sem, in_sems, out_sems,
):
    me = lax.axis_index("ctx")
    base = me * rows
    count = payload.shape[0]
    poles = (params.shape[1] - 1) // 2
    extended = rows + HALO
    padded = rows + 2 * HALO
    get_lengths = pltpu.make_async_copy(far_lengths, lengths, length_sem)
    get_lengths.start()

    def arriving(half):
        lanes = [
            pl.ds(pl.multiple_of((third * groups + half) * GROUP, GROUP), GROUP)
            for third in range(3)
        ]
        return [
            pltpu.make_async_copy(
                features.at[0, :, lanes[third]], raw.at[half, third], in_sems.at[half, third]
            )
            for third in range(3)
        ] + [pltpu.make_async_copy(upstream.at[0, :, lanes[0]], raw_up.at[half], in_sems.at[half, 3])]

    near = [feat, up, tap, par, mixed, gout]
    far = [feat_out, up_out, tap_out, par_out, mixed_out, gout_out]

    each_group(groups, lambda half: start_all(arriving(half)))
    zero_scr[...] = jnp.zeros((SUB, LANES), F32)
    zeros = [zero_scr[...]] * poles

    def prepare(half):
        spread_params(par.at[half], params, half, groups)
        for third in range(3):
            column = (third * groups + half) * GROUP
            spread(feat.at[half], third * padded, left, column, HALO)
            spread(feat.at[half], third * padded + rows + HALO, right, column, HALO)
            spread(tap.at[half], third * 3, taps, column, 3)
        spread(up.at[half], rows, right, (3 * groups + half) * GROUP, HALO)

    each_group(groups, prepare)
    get_lengths.wait()
    starts = segment_starts(lengths)
    fill_keep(keep, starts, base, rows)
    low, high = jnp.int32(0), jnp.int32(extended)
    for start in starts:
        at = start - base
        low = jnp.where(at < rows, jnp.maximum(low, at), low)
        high = jnp.where(at > HALO, jnp.minimum(high, at), high)

    def group(half):
        incoming = arriving(half)
        outgoing = group_copies(near, far, out_sems, half)
        feat_h, up_h, mixed_h, gout_h = feat.at[half], up.at[half], mixed.at[half], gout.at[half]
        for third in range(3):
            incoming[third].wait()
            spread_rows(feat_h, third * padded + HALO, raw.at[half, third], rows)
        incoming[3].wait()
        spread_rows(up_h, 0, raw_up.at[half], rows)
        start_all(outgoing[:4])
        taps_h = [[vec(tap.at[half], third * 3 + j) for j in range(3)] for third in range(3)]

        def product(p, carry):
            keep_one = keep[p + 1]
            keep_two = keep_one * keep[p]
            query, key, val = (
                featured(feat_h, taps_h[third], third * padded + p, keep_one, keep_two)
                for third in range(3)
            )
            put(mixed_h, p, rounded(key * val))
            put(gout_h, p, rounded(vec(up_h, p) * query))
            return carry

        lax.fori_loop(0, extended, product, 0, unroll=unroll_of(extended))
        start_all(outgoing[4:])
        decay = [jnp.exp(-jnp.exp(vec(par.at[half], m))) for m in range(poles)]

        def sweep(i, carry):
            state, adjoint = carry
            back = extended - 1 - i
            x = vec(mixed_h, i) * flag(i >= low)
            g = vec(gout_h, back) * flag(back < high)
            state = [decay[m] * state[m] + x for m in range(poles)]
            adjoint = [decay[m] * adjoint[m] + g for m in range(poles)]
            return state, adjoint

        state, adjoint = lax.fori_loop(0, rows, sweep, (zeros, zeros), unroll=8)
        for m in range(0, poles, 2):
            at = slice(m * SUB, (m + 2) * SUB)
            stack[0, at, :] = jnp.concatenate(state[m : m + 2], axis=0).astype(BF16)
            stack[1, at, :] = jnp.concatenate(adjoint[m : m + 2], axis=0).astype(BF16)
        for e in range(count):
            payload[e, half] = stack[jnp.where(e >= me, 0, 1)]

    each_group(groups, group)
    each_group(groups, lambda half: wait_all(group_copies(near, far, out_sems, half)))


def local_kernel(
    rows, groups, far_lengths, feat_in, mixed_in, gout_in, par_in, tap_in,
    key_out, val_out, conv_out, adj_out, partial_out,
    lengths, mixed, gout, par, tap, feat, key, val, conv, adj, partial, zero_scr, keep,
    length_sem, in_sems, out_sems,
):
    poles = (par.shape[1] // SUB - 1) // 2
    extended = rows + HALO
    padded = rows + 2 * HALO
    get_lengths = pltpu.make_async_copy(far_lengths, lengths, length_sem)
    get_lengths.start()
    far_in, near_in = [par_in, tap_in, feat_in, mixed_in, gout_in], [par, tap, feat, mixed, gout]
    near_out = [key, val, conv, adj, partial]
    far_out = [key_out, val_out, conv_out, adj_out, partial_out]
    each_group(groups, lambda half: start_all(group_copies(far_in, near_in, in_sems, half)))
    zero_scr[...] = jnp.zeros((SUB, LANES), F32)
    zero = zero_scr[...]
    per_pass = poles // 4
    zeros = [zero] * per_pass
    get_lengths.wait()
    fill_keep(keep, segment_starts(lengths), lax.axis_index("ctx") * rows, rows)

    def group(half):
        incoming = group_copies(far_in, near_in, in_sems, half)
        outgoing = group_copies(near_out, far_out, out_sems, half)
        feat_h, mixed_h, gout_h, par_h = feat.at[half], mixed.at[half], gout.at[half], par.at[half]
        conv_h, adj_h, key_h, val_h = conv.at[half], adj.at[half], key.at[half], val.at[half]
        wait_all(incoming)
        taps_h = [[vec(tap.at[half], third * 3 + j) for j in range(3)] for third in range(3)]

        def product(p, carry):
            keep_one = keep[p + 1]
            keep_two = keep_one * keep[p]
            put(key_h, p, featured(feat_h, taps_h[1], padded + p, keep_one, keep_two))
            put(val_h, p, featured(feat_h, taps_h[2], 2 * padded + p, keep_one, keep_two))
            return carry

        lax.fori_loop(0, extended, product, 0, unroll=unroll_of(extended))
        start_all(outgoing[:2])
        gain = vec(par_h, 2 * poles)
        for part in range(poles // per_pass):
            chosen = list(range(part * per_pass, (part + 1) * per_pass))
            decay = [jnp.exp(-jnp.exp(vec(par_h, m))) for m in chosen]
            coeff = [vec(par_h, poles + m) for m in chosen]

            def sweep(i, carry):
                state, adjoint, resid, skip = carry
                back = extended - 1 - i
                x = vec(mixed_h, i)
                g = vec(gout_h, back)
                own = vec(mixed_h, back) * flag(back < rows)
                keep_fwd = keep[i + 1]
                keep_bwd = keep[back + 2]
                state = [decay[m] * (state[m] * keep_fwd) + x for m in range(per_pass)]
                adjoint = [decay[m] * (adjoint[m] * keep_bwd) + g for m in range(per_pass)]
                resid = [resid[m] + own * adjoint[m] for m in range(per_pass)]
                forward = sum(coeff[m] * state[m] for m in range(per_pass))
                backward = sum(coeff[m] * adjoint[m] for m in range(per_pass))
                if part == 0:
                    put(conv_h, i, forward + gain * x)
                    put(adj_h, back, backward + gain * g)
                    skip = skip + own * g
                else:
                    put(conv_h, i, forward + vec(conv_h, i))
                    put(adj_h, back, backward + vec(adj_h, back))
                return state, adjoint, resid, skip

            _, _, resid, skip = lax.fori_loop(
                0, extended, sweep, (zeros, zeros, zeros, zero), unroll=unroll_of(extended)
            )
            for i, m in enumerate(chosen):
                put(partial.at[half], m, resid[i])
            if part == 0:
                put(partial.at[half], poles, skip)
        start_all(outgoing[2:])

    each_group(groups, group)
    each_group(groups, lambda half: wait_all(group_copies(near_out, far_out, out_sems, half)))


def finish_kernel(
    rows, groups, far_lengths, arrived, par_in, partial_in, tap_in, conv_in, adj_in, up_in,
    key_in, val_in, feat_in, grads, sums,
    lengths, par, partial, tap, conv, adj, up, key, val, feat, before, after, post, ready,
    zero_scr, keep, length_sem, in_sems, out_sems,
):
    me = lax.axis_index("ctx")
    base = me * rows
    count = arrived.shape[0]
    poles = (par.shape[1] // SUB - 1) // 2
    extended = rows + HALO
    padded = rows + 2 * HALO
    get_lengths = pltpu.make_async_copy(far_lengths, lengths, length_sem)
    get_lengths.start()
    far = [par_in, partial_in, conv_in, adj_in, tap_in, up_in, key_in, val_in, feat_in]
    near = [par, partial, conv, adj, tap, up, key, val, feat]
    each_group(groups, lambda half: start_all(group_copies(far, near, in_sems, half)))

    def leaving(half):
        return [
            pltpu.make_async_copy(
                ready.at[half, third],
                grads.at[
                    0, :, pl.ds(pl.multiple_of((third * groups + half) * GROUP, GROUP), GROUP)
                ],
                out_sems.at[half, third],
            )
            for third in range(3)
        ]

    zero_scr[...] = jnp.zeros((SUB, LANES), F32)
    zero = zero_scr[...]
    get_lengths.wait()
    starts = segment_starts(lengths)
    fill_keep(keep, starts, base, rows)
    until, since = jnp.int32(extended), jnp.int32(0)
    first, last, newest = jnp.int32(0), jnp.int32(2**30), jnp.int32(0)
    for start in starts:
        at = start - base
        until = jnp.where(at >= 0, jnp.minimum(until, at), until)
        since = jnp.where(at <= extended, jnp.maximum(since, at), since)
        first = jnp.where(at <= 0, jnp.maximum(first, start), first)
        last = jnp.where(at > extended, jnp.minimum(last, start), last)
        newest = jnp.where(at <= extended, jnp.maximum(newest, start), newest)
    steps = jnp.maximum(until, extended - since)
    through = flag(newest < base + rows)
    chunk = unroll_of(extended)

    def group(half):
        incoming = group_copies(far, near, in_sems, half)
        par_h, partial_h, conv_h, adj_h = par.at[half], partial.at[half], conv.at[half], adj.at[half]
        up_h, key_h, val_h, feat_h = up.at[half], key.at[half], val.at[half], feat.at[half]
        wait_all(incoming[:2])
        per_pass = poles // 2
        zeros = [zero] * per_pass
        for part in range(2):
            chosen = list(range(part * per_pass, (part + 1) * per_pass))
            rate = [jnp.exp(vec(par_h, m)) for m in chosen]
            block = [jnp.exp(-rows * r) for r in rate]

            def arrived_states(d):
                got = []
                for m in range(chosen[0], chosen[-1] + 1, 2):
                    pair = arrived[d, half, m * SUB : (m + 2) * SUB, :].astype(F32)
                    got += [pair[:SUB], pair[SUB:]]
                return got

            def from_before(d, carry):
                joined = flag((d + 1) * rows - 1 >= first)
                got = arrived_states(d)
                return [block[i] * carry[i] + joined * got[i] for i in range(per_pass)]

            def from_after(i, carry):
                d = count - 1 - i
                joined = flag(d * rows + HALO < last)
                got = arrived_states(d)
                return [block[i] * carry[i] + joined * got[i] for i in range(per_pass)]

            state = lax.fori_loop(0, me, from_before, zeros)
            adjoint = lax.fori_loop(0, count - 1 - me, from_after, zeros)
            own = arrived_states(me)
            for i, m in enumerate(chosen):
                scale = vec(par_h, poles + m) * jnp.exp(-rate[i])
                put(before, m, scale * state[i])
                put(after, m, scale * adjoint[i])
                cross = jnp.exp(-(HALO + 1) * rate[i]) * (adjoint[i] * through)
                put(sums, (9 + m) * groups + half, vec(partial_h, m) + cross * own[i])
        put(sums, (9 + poles) * groups + half, vec(partial_h, poles))
        decay = [jnp.exp(-jnp.exp(vec(par_h, m))) for m in range(poles)]
        enter = [vec(before, m) for m in range(poles)]
        leave = [vec(after, m) for m in range(poles)]
        wait_all(incoming[2:4])

        def carried(i, carry):
            enter, leave = carry
            for step in range(chunk):
                p = chunk * i + step
                back = extended - 1 - p
                put(conv_h, p, vec(conv_h, p) + flag(p < until) * sum(enter))
                put(adj_h, back, vec(adj_h, back) + flag(back >= since) * sum(leave))
                enter = [decay[m] * enter[m] for m in range(poles)]
                leave = [decay[m] * leave[m] for m in range(poles)]
            return enter, leave

        lax.fori_loop(0, (steps + chunk - 1) // chunk, carried, (enter, leave))
        wait_all(incoming[4:])
        taps_h = [[vec(tap.at[half], third * 3 + j) for j in range(3)] for third in range(3)]

        def posted(p):
            keep_one = keep[p + 1]
            keep_two = keep_one * keep[p]
            conv_out = rounded(vec(conv_h, p))
            grad_mixed = rounded(vec(adj_h, p))
            now = [vec(up_h, p) * conv_out, grad_mixed * vec(val_h, p), grad_mixed * vec(key_h, p)]
            return now, [keep_one * g for g in now], [keep_two * g for g in now]

        _, _, far_two = posted(extended - 1)
        _, near_one, near_two = posted(extended - 2)

        def finish(i, carry):
            one, two, three, tap_sums = carry
            p = rows - 1 - i
            now, masked_one, masked_two = posted(p)
            new_sums = []
            for third in range(3):
                back = (
                    taps_h[third][0] * now[third]
                    + taps_h[third][1] * one[third]
                    + taps_h[third][2] * three[third]
                )
                put(post, third * rows + p, back)
                at = third * padded + p
                new_sums += [
                    tap_sums[3 * third] + now[third] * vec(feat_h, at + 2),
                    tap_sums[3 * third + 1] + masked_one[third] * vec(feat_h, at + 1),
                    tap_sums[3 * third + 2] + masked_two[third] * vec(feat_h, at),
                ]
            return masked_one, masked_two, two, new_sums

        _, _, _, tap_sums = lax.fori_loop(
            0, rows, finish, (near_one, near_two, far_two, [zero] * 9), unroll=4
        )
        for third in range(3):
            for j in range(3):
                put(sums, (3 * j + third) * groups + half, tap_sums[3 * third + j])

        def write(i, carry):
            for third in range(3):
                for j in range(SUB):
                    value = post[pl.ds((third * rows + i * 16) * SUB + j, 16, stride=SUB), :]
                    ready[
                        half, third, pl.ds(pl.multiple_of(i * 16, 16), 16), j * LANES : (j + 1) * LANES
                    ] = value.astype(BF16)
            return carry

        lax.fori_loop(0, rows // 16, write, 0)
        start_all(leaving(half))

    each_group(groups, group)
    each_group(groups, lambda half: wait_all(leaving(half)))


def share_kernel(scale, parts, out):
    count = lax.axis_size("dp") * lax.axis_size("ctx")
    share = parts.shape[0] // count
    mine = parts[0:share, :]
    for k in range(1, count):
        mine = mine + parts[k * share : (k + 1) * share, :]
    mine = mine * scale
    for k in range(count):
        out[k * share : (k + 1) * share, :] = mine


def emit_kernel(groups, whole, grad_taps, resid, skip):
    me = lax.axis_index("ctx")
    width = groups * SUB
    poles, per_shard = resid.shape
    for k in range(3 * width):
        lanes = slice(k * LANES, (k + 1) * LANES)
        grad_taps[:, lanes] = whole[pl.ds(k, 3, stride=3 * width), :]
    if per_shard >= LANES:
        per = per_shard // LANES
        for j in range(per):
            first = 9 * width + me * per + j
            lanes = slice(j * LANES, (j + 1) * LANES)
            resid[:, lanes] = whole[pl.ds(first, poles, stride=width), :]
            skip[:, lanes] = whole[pl.ds(first + poles * width, 1), :]
    else:
        per = LANES // per_shard
        first = 9 * width + me // per
        rows = whole[pl.ds(first, poles, stride=width), :]
        last = whole[pl.ds(first + poles * width, 1), :]
        place = lax.rem(me, per)
        chosen, chosen_last = rows[:, :per_shard], last[:, :per_shard]
        for i in range(1, per):
            lanes = slice(i * per_shard, (i + 1) * per_shard)
            chosen = jnp.where(place == i, rows[:, lanes], chosen)
            chosen_last = jnp.where(place == i, last[:, lanes], chosen_last)
        resid[...] = chosen
        skip[...] = chosen_last


def swap(block, axes):
    return lax.all_to_all(block, axes, split_axis=0, concat_axis=0, tiled=True)


def per_device(features, upstream, lengths, conv_taps, residues, log_rate, skip_gain):
    rows = features.shape[1]
    channels = upstream.shape[2]
    poles = residues.shape[0]
    ctx_count = lax.axis_size("ctx")
    total = ctx_count * lax.axis_size("dp")
    per_shard = channels // ctx_count
    groups = channels // GROUP
    grad_scale = 1.0 / math.sqrt(rows * total)
    extended = rows + HALO
    padded = rows + 2 * HALO
    state_rows = poles * SUB
    limits = pltpu.CompilerParams(vmem_limit_bytes=40 * 1024 * 1024)
    hbm = pl.BlockSpec(memory_space=pltpu.HBM)
    vmem = pl.BlockSpec(memory_space=pltpu.VMEM)

    def tall(height):
        return jax.ShapeDtypeStruct((groups, height * SUB, LANES), F32)

    def near(*heights):
        return [pltpu.VMEM((groups, height * SUB, LANES), F32) for height in heights]

    def scratch(height):
        return pltpu.VMEM((height * SUB, LANES), F32)

    def sems(*shape):
        return pltpu.SemaphoreType.DMA(shape)

    keep = pltpu.SMEM((rows + 8,), F32)
    small = pltpu.SMEM(lengths.shape, jnp.int32)

    def call(kernel, name, ins, in_specs, outs, out_specs, scratch_shapes=()):
        ins = [
            pltpu.with_memory_space_constraint(x, pltpu.HBM) if spec is hbm else x
            for x, spec in zip(ins, in_specs)
        ]
        if isinstance(outs, list):
            outs = [
                pltpu.HBM(out.shape, out.dtype) if spec is hbm else out
                for out, spec in zip(outs, out_specs)
            ]
        return pl.pallas_call(
            kernel,
            out_shape=outs,
            in_specs=in_specs,
            out_specs=out_specs,
            scratch_shapes=list(scratch_shapes),
            compiler_params=limits,
            name=name,
        )(*ins)

    edge = features[0, rows - HALO :, :]
    head = jnp.concatenate([features[0, :HALO, :], upstream[0, :HALO, :]], axis=1)
    left = shifted(edge, "ctx", 1)
    right = shifted(head, "ctx", -1)
    params = jnp.concatenate([log_rate, residues, skip_gain[None]], axis=0)
    params = swap(jnp.broadcast_to(params[None], (ctx_count,) + params.shape), "ctx")

    payload, feat, up, mixed, gout, par, tap = call(
        functools.partial(ends_kernel, rows, groups),
        "ends",
        [lengths, features, upstream, left, right, conv_taps, params],
        [hbm] * 3 + [vmem] * 4,
        [jax.ShapeDtypeStruct((ctx_count, groups, state_rows, LANES), BF16)]
        + [tall(height) for height in [3 * padded] + [extended] * 3 + [2 * poles + 1, 9]],
        [vmem] + [hbm] * 6,
        [
            small,
            pltpu.VMEM((groups, 3, rows, GROUP), BF16),
            pltpu.VMEM((groups, rows, GROUP), BF16),
        ]
        + near(3 * padded, extended, extended, extended, 2 * poles + 1, 9)
        + [pltpu.VMEM((2, state_rows, LANES), BF16), scratch(1), keep]
        + [sems(), sems(groups, 4), sems(groups, 6)],
    )
    arrived = swap(payload, "ctx")
    key, val, conv, adj, partial = call(
        functools.partial(local_kernel, rows, groups),
        "local",
        [lengths, feat, mixed, gout, par, tap],
        [hbm] * 6,
        [tall(extended)] * 4 + [tall(poles + 1)],
        [hbm] * 5,
        [small]
        + near(extended, extended, 2 * poles + 1, 9, 3 * padded)
        + near(extended, extended, extended, extended, poles + 1)
        + [scratch(1), keep, sems(), sems(groups, 5), sems(groups, 5)],
    )
    used = (10 + poles) * groups * SUB
    share = -(-used // total)
    grads, sums = call(
        functools.partial(finish_kernel, rows, groups),
        "finish",
        [lengths, arrived, par, partial, tap, conv, adj, up, key, val, feat],
        [hbm, vmem] + [hbm] * 9,
        [
            jax.ShapeDtypeStruct(features.shape, BF16),
            jax.ShapeDtypeStruct((total * share, LANES), F32),
        ],
        [hbm, vmem],
        [small]
        + near(2 * poles + 1, poles + 1, 9, extended, extended, extended, extended, extended)
        + near(3 * padded)
        + [scratch(poles), scratch(poles), scratch(3 * rows)]
        + [pltpu.VMEM((groups, 3, rows, GROUP), BF16), scratch(1), keep]
        + [sems(), sems(groups, 9), sems(groups, 3)],
    )

    both = ("dp", "ctx")
    flat = (total, 1, share * LANES)
    parts = swap(sums.reshape(flat), both).reshape(sums.shape)
    shares = call(
        functools.partial(share_kernel, grad_scale),
        "share",
        [parts],
        [vmem],
        jax.ShapeDtypeStruct(sums.shape, F32),
        vmem,
    )
    whole = swap(shares.reshape(flat), both).reshape(sums.shape)
    grad_taps, resid, skip = call(
        functools.partial(emit_kernel, groups),
        "emit",
        [whole],
        [vmem],
        [
            jax.ShapeDtypeStruct((3, 3 * channels), F32),
            jax.ShapeDtypeStruct((poles, per_shard), F32),
            jax.ShapeDtypeStruct((1, per_shard), F32),
        ],
        [vmem] * 3,
    )
    return grads, grad_taps, resid, skip.reshape(per_shard)


def solution(mesh):
    return jax.shard_map(
        per_device,
        mesh=mesh,
        in_specs=(
            P("dp", "ctx", None),
            P("dp", "ctx", None),
            P("dp", None),
            P(),
            P(None, "ctx"),
            P(None, "ctx"),
            P("ctx"),
        ),
        out_specs=(P("dp", "ctx", None), P(), P(None, "ctx"), P("ctx")),
        check_vma=False,
    )
```

time: 127 us -> 81.3 us (0.64)
  waiting for transfers between devices: 29.8 us -> 3.81 us
  local copies, waits for them, and re-layouts: 19.9 us -> 2.5 us
  blocking collectives: 16.1 us -> 25.7 us
  starting transfers between devices: 28.6 us -> 19.4 us
  Pallas kernels: 29.6 us -> 27.8 us
    all_to_all x5 -> x2, waiting for transfers between devices: 28.3 us -> 2.3 us  [swap(): return lax.all_to_all(block, axes, split_axis=0, concat_axis=0, tiled=True)]
    unnamed x34 -> x2, local copies, waits for them, and re-layouts: 15 us -> 0.01 us
    all_to_all x1 -> x2, blocking collectives: 16.1 us -> 25.7 us  [swap(): return lax.all_to_all(block, axes, split_axis=0, concat_axis=0, tiled=True)]
    all_to_all x5 -> x2, starting transfers between devices: 22.7 us -> 13.5 us  [swap(): return lax.all_to_all(block, axes, split_axis=0, concat_axis=0, tiled=True)]
    pallas_call x5, Pallas kernels: 29.6 us -> 27.8 us  [call(): pl.pallas_call(kernel, out_shape=outs, in_specs=in_specs, out_specs=out_s...]
    broadcast_in_dim x2 -> x0, local copies, waits for them, and re-layouts: 1.41 us -> none  [sum_over_all(): whole = swap(jnp.broadcast_to(mine[None], parts.shape), ('dp', 'ctx'))]
  transfers between devices with their start and end apart: 7 -> 4, of which waited for: 4 -> 3; matrix products, arithmetic and copies ran while one was open for 1% -> 2% of each run, Pallas kernels for 12% -> 15%
where the time goes in v4:
time: 81.3 us; the launch traced here: 80.7 us
  Pallas kernels  27.8 us (34%)
  blocking collectives  25.7 us (32%)
  starting transfers between devices  19.4 us (24%)
  waiting for transfers between devices  3.81 us (5%)
  local copies, waits for them, and re-layouts  2.5 us (3%)
  other arithmetic  0.82 us (1%)
    pallas_call x5, Pallas kernels, call(): pl.pallas_call(kernel, out_shape=outs, in_specs=in_specs, out_specs=out_s...  27.8 us
    all_to_all x2, blocking collectives, swap(): return lax.all_to_all(block, axes, split_axis=0, concat_axis=0, tiled=True)  25.7 us
    all_to_all x2, starting transfers between devices, swap(): return lax.all_to_all(block, axes, split_axis=0, concat_axis=0, tiled=True)  13.5 us
    ppermute x2, starting transfers between devices, shifted(): return lax.ppermute(block, axis, route)  5.85 us
    all_to_all x2, waiting for transfers between devices, swap(): return lax.all_to_all(block, axes, split_axis=0, concat_axis=0, tiled=True)  2.3 us
  transfers between devices with their start and end apart: 4, of which 3 were waited for; matrix products, arithmetic and copies ran while one was open for 2% of the time, Pallas kernels for 15%

profile of v4, /device:TPU:0, one launch (start us, length us, event | category | flops | bytes accessed | tf_op | source)
XLA Modules:
  0.0 80.7 jit_solution(10986044772871852715)
XLA Ops:
  0.6 0.0 copy-start
  0.6 0.8 pad_maximum_fusion
  1.4 0.7 broadcast_in_dim.10
  2.2 7.3 %all-to-all-start = ((f32[8,33,256]{2,1,0:T(8,128)}), f32[8,33,256]{2,1,0:T(8,128)S(1)}, u32[]{:S(2)}, u32[]{:S(2)}) async-start(f32[8,33,256]{2,1,0:T(8,128)} %broadcast_in_dim.10), calls=%async_computation | async-start | bytes 655360 | tf_op jit(solution)/shard_map/all_to_all | solution.py:519
  9.5 0.8 slice_bitcast_fusion.2
  10.2 1.0 %slice_bitcast_fusion = (bf16[2,6144]{1,0:T(2,128)(2,1)S(1)}, bf16[2,6144]{1,0:T(2,128)(2,1)S(1)}) fusion(bf16[1,128,6144]{2,1,0:T(8,128)(2,1)} %features.1), kind=kLoop, calls=%fused_computation.2 | loop fusion | bytes 98304 | tf_op jit(solution)/shard_map/squeeze | solution.py:574
  11.2 1.3 %collective-permute-start.1 = (bf16[2,8192]{1,0:T(2,128)(2,1)S(1)}, bf16[2,8192]{1,0:T(2,128)(2,1)S(1)}, u32[]{:S(2)}, u32[]{:S(2)}) collective-permute-start(bf16[2,8192]{1,0:T(2,128)(2,1)S(1)} %pad_maximum_fusion.1), channel_id=1, source_target_pairs={{1,0},{2,1},{3,2},{4,3},{5,4},{6,5},{7,6},{9,8},{10,9},{11,10},{12... | collective-permute-start | bytes 98312 | tf_op jit(solution)/shard_map/ppermute | solution.py:22
  12.5 4.6 %collective-permute-start = (bf16[2,6144]{1,0:T(2,128)(2,1)S(1)}, bf16[2,6144]{1,0:T(2,128)(2,1)S(1)}, u32[]{:S(2)}, u32[]{:S(2)}) collective-permute-start(bf16[2,6144]{1,0:T(2,128)(2,1)S(1)} %get-tuple-element.39), channel_id=1, source_target_pairs={{0,1},{1,2},{2,3},{3,4},{4,5},{5,6},{6,7},{8,9},{9,10},{10,11},{11... | collective-permute-start | bytes 73736 | tf_op jit(solution)/shard_map/ppermute | solution.py:22
  17.1 1.5 %collective-permute-done.left = bf16[2,6144]{1,0:T(2,128)(2,1)S(1)} collective-permute-done((bf16[2,6144]{1,0:T(2,128)(2,1)S(1)}, bf16[2,6144]{1,0:T(2,128)(2,1)S(1)}, u32[]{:S(2)}, u32[]{:S(2)}) %collective-permute-start) | collective-permute-done | bytes 24608 | tf_op jit(solution)/shard_map/ppermute | solution.py:22
  18.6 0.0 collective-permute-done.1.right
  18.6 1.5 %all-to-all-done.params = f32[8,33,256]{2,1,0:T(8,128)S(1)} async-done(((f32[8,33,256]{2,1,0:T(8,128)}), f32[8,33,256]{2,1,0:T(8,128)S(1)}, u32[]{:S(2)}, u32[]{:S(2)}) %all-to-all-start) | async-done | bytes 270368 | tf_op jit(solution)/shard_map/all_to_all | solution.py:519
  20.1 0.0 copy-done
  20.1 6.9 %ends.1 = (bf16[8,2,128,128]{3,2,1,0:T(8,128)(2,1)}, f32[2,3168,128]{2,1,0:T(8,128)}, f32[2,1040,128]{2,1,0:T(8,128)}, f32[2,1040,128]{2,1,0:T(8,128)}, f32[2,10...) custom-call(s32[1,8]{1,0:T(1,128)} %far_lengths.5, bf16[1,128,6144]{2,1,0:T(8,128)(2,1)} %features.1, ...), custom_call_target="tpu_custom_call" | custom-call | tf_op jit(solution)/shard_map/ends/pallas_call | solution.py:563
  27.1 6.2 %all-to-all-start.1 = ((bf16[8,2,128,128]{3,2,1,0:T(8,128)(2,1)}), bf16[8,2,128,128]{3,2,1,0:T(8,128)(2,1)S(1)}, u32[]{:S(2)}, u32[]{:S(2)}) async-start(bf16[8,2,128,128]{3,2,1,0:T(8,128)(2,1)} %get-tuple-element.21), calls=%async_computation.1 | async-start | bytes 1048576 | tf_op jit(solution)/shard_map/all_to_all | solution.py:519
  33.3 11.7 %local.1 = (f32[2,1040,128]{2,1,0:T(8,128)}, f32[2,1040,128]{2,1,0:T(8,128)}, f32[2,1040,128]{2,1,0:T(8,128)}, f32[2,1040,128]{2,1,0:T(8,128)}, f32[2,136,128]{2,1,0:T(8,128)}) custom-call(s32[1,8]{1,0:T(1,128)} %far_lengths.5, f32[2,3168,128]{2,1,0:T(8,128)} %get-tuple-element.23.feat_in, f32[2,1040,128]{2,1,0:T(8,128)} %get-tuple-element.24.mixed_in, ...), custom_call_target="tpu_custom_call" | custom-call | tf_op jit(solution)/shard_map/local/pallas_call | solution.py:563
  45.1 0.8 all-to-all-done.1.arrived
  45.9 8.3 %finish.1 = (bf16[1,128,6144]{2,1,0:T(8,128)(2,1)}, f32[416,128]{1,0:T(8,128)S(1)}) custom-call(s32[1,8]{1,0:T(1,128)} %far_lengths.5, bf16[8,2,128,128]{3,2,1,0:T(8,128)(2,1)S(1)} %all-to-all-done.1.arrived, f32[2,264,128]{2,1,0:T(8,128)} %get-tuple-element.22.par_in, f32[2,136,128]{2,1,0:T(8,128)} %get-tuple-element.27.partial_in, ...), custom_call_target="tpu_custom_call" | custom-call | tf_op jit(solution)/shard_map/finish/pallas_call | solution.py:563
  54.2 14.0 %all_to_all.20 = f32[32,1,1664]{2,1,0:T(1,128)S(1)} all-to-all(f32[32,1,1664]{2,1,0:T(1,128)S(1)} %bitcast.15), channel_id=1, replica_groups=mesh['dp'=4,'ctx'=8] {'dp','ctx'}, dimensions={0} | all-to-all | bytes 425984 | tf_op jit(solution)/shard_map/all_to_all | solution.py:519
  68.2 0.1 share.1
  68.2 11.8 %all_to_all.21 = f32[32,1,1664]{2,1,0:T(1,128)S(1)} all-to-all(f32[32,1,1664]{2,1,0:T(1,128)S(1)} %bitcast.14), channel_id=1, replica_groups=mesh['dp'=4,'ctx'=8] {'dp','ctx'}, dimensions={0} | all-to-all | bytes 425984 | tf_op jit(solution)/shard_map/all_to_all | solution.py:519
  80.0 0.7 emit.1
  (1 shorter events, 0.0 us)
Async XLA Ops:
  0.6 19.5 %copy-start = (f32[3,6144]{1,0:T(4,128)S(1)}, f32[3,6144]{1,0:T(4,128)}, u32[]{:S(2)}) copy-start(f32[3,6144]{1,0:T(4,128)} %taps.1) | copy-start | bytes 221188
  2.2 18.0 %all-to-all-start = ((f32[8,33,256]{2,1,0:T(8,128)}), f32[8,33,256]{2,1,0:T(8,128)S(1)}, u32[]{:S(2)}, u32[]{:S(2)}) async-start(f32[8,33,256]{2,1,0:T(8,128)} %broadcast_in_dim.10), calls=%async_computation | async-start | bytes 655360 | tf_op jit(solution)/shard_map/all_to_all | solution.py:519
  11.2 7.4 %collective-permute-start.1 = (bf16[2,8192]{1,0:T(2,128)(2,1)S(1)}, bf16[2,8192]{1,0:T(2,128)(2,1)S(1)}, u32[]{:S(2)}, u32[]{:S(2)}) collective-permute-start(bf16[2,8192]{1,0:T(2,128)(2,1)S(1)} %pad_maximum_fusion.1), channel_id=1, source_target_pairs={{1,0},{2,1},{3,2},{4,3},{5,4},{6,5},{7,6},{9,8},{10,9},{11,10},{12... | collective-permute-start | bytes 98312 | tf_op jit(solution)/shard_map/ppermute | solution.py:22
  12.5 6.1 %collective-permute-start = (bf16[2,6144]{1,0:T(2,128)(2,1)S(1)}, bf16[2,6144]{1,0:T(2,128)(2,1)S(1)}, u32[]{:S(2)}, u32[]{:S(2)}) collective-permute-start(bf16[2,6144]{1,0:T(2,128)(2,1)S(1)} %get-tuple-element.39), channel_id=1, source_target_pairs={{0,1},{1,2},{2,3},{3,4},{4,5},{5,6},{6,7},{8,9},{9,10},{10,11},{11... | collective-permute-start | bytes 73736 | tf_op jit(solution)/shard_map/ppermute | solution.py:22
  27.1 18.8 %all-to-all-start.1 = ((bf16[8,2,128,128]{3,2,1,0:T(8,128)(2,1)}), bf16[8,2,128,128]{3,2,1,0:T(8,128)(2,1)S(1)}, u32[]{:S(2)}, u32[]{:S(2)}) async-start(bf16[8,2,128,128]{3,2,1,0:T(8,128)(2,1)} %get-tuple-element.21), calls=%async_computation.1 | async-start | bytes 1048576 | tf_op jit(solution)/shard_map/all_to_all | solution.py:519

commit v5 on v4

--- a/solution.py
+++ b/solution.py
@@ -315,9 +315,9 @@
 
 def finish_kernel(
     rows, groups, far_lengths, arrived, par_in, partial_in, tap_in, conv_in, adj_in, up_in,
-    key_in, val_in, feat_in, grads, sums,
+    key_in, val_in, feat_in, grads, payload,
     lengths, par, partial, tap, conv, adj, up, key, val, feat, before, after, post, ready,
-    zero_scr, keep, length_sem, in_sems, out_sems,
+    sums, zero_scr, keep, length_sem, in_sems, out_sems,
 ):
     me = lax.axis_index("ctx")
     base = me * rows
@@ -472,45 +472,56 @@
         start_all(leaving(half))
 
     each_group(groups, group)
+    width = groups * SUB
+    same = 9 * width
+    tap_sums = sums[0:same, :].astype(BF16)
+    columns = (payload.shape[1] - same) // 16 - 1
+    for e in range(count):
+        payload[e, 0:same, :] = tap_sums
+        first = same + (e * width) // count
+        for j in range(columns):
+            value = sums[pl.ds(first + j, 16, stride=width), :]
+            payload[e, same + 16 * j : same + 16 * (j + 1), :] = value.astype(BF16)
+        last = first + poles * width
+        payload[e, same + 16 * columns :, :] = sums[last : last + 16, :].astype(BF16)
     each_group(groups, lambda half: wait_all(leaving(half)))
 
 
-def share_kernel(scale, parts, out):
-    count = lax.axis_size("dp") * lax.axis_size("ctx")
-    share = parts.shape[0] // count
-    mine = parts[0:share, :]
-    for k in range(1, count):
-        mine = mine + parts[k * share : (k + 1) * share, :]
-    mine = mine * scale
-    for k in range(count):
-        out[k * share : (k + 1) * share, :] = mine
-
-
-def emit_kernel(groups, whole, grad_taps, resid, skip):
+def share_kernel(parts, out):
+    mine = parts[0].astype(F32)
+    for k in range(1, parts.shape[0]):
+        mine = mine + parts[k].astype(F32)
+    out[...] = mine.astype(BF16)
+
+
+def emit_kernel(groups, scale, shares, grad_taps, resid, skip, whole):
     me = lax.axis_index("ctx")
     width = groups * SUB
     poles, per_shard = resid.shape
+    mine = shares[0].astype(F32)
+    for k in range(1, shares.shape[0]):
+        mine = mine + shares[k].astype(F32)
+    whole[...] = mine * scale
     for k in range(3 * width):
-        lanes = slice(k * LANES, (k + 1) * LANES)
-        grad_taps[:, lanes] = whole[pl.ds(k, 3, stride=3 * width), :]
+        grad_taps[:, k * LANES : (k + 1) * LANES] = whole[pl.ds(k, 3, stride=3 * width), :]
+    first = 9 * width
+    columns = (whole.shape[0] - first) // 16 - 1
+    last = first + 16 * columns
     if per_shard >= LANES:
-        per = per_shard // LANES
-        for j in range(per):
-            first = 9 * width + me * per + j
+        for j in range(columns):
             lanes = slice(j * LANES, (j + 1) * LANES)
-            resid[:, lanes] = whole[pl.ds(first, poles, stride=width), :]
-            skip[:, lanes] = whole[pl.ds(first + poles * width, 1), :]
+            resid[:, lanes] = whole[first + 16 * j : first + 16 * (j + 1), :]
+            skip[:, lanes] = whole[last + j : last + j + 1, :]
     else:
         per = LANES // per_shard
-        first = 9 * width + me // per
-        rows = whole[pl.ds(first, poles, stride=width), :]
-        last = whole[pl.ds(first + poles * width, 1), :]
+        rows = whole[first : first + 16, :]
+        final = whole[last : last + 1, :]
         place = lax.rem(me, per)
-        chosen, chosen_last = rows[:, :per_shard], last[:, :per_shard]
+        chosen, chosen_last = rows[:, :per_shard], final[:, :per_shard]
         for i in range(1, per):
             lanes = slice(i * per_shard, (i + 1) * per_shard)
             chosen = jnp.where(place == i, rows[:, lanes], chosen)
-            chosen_last = jnp.where(place == i, last[:, lanes], chosen_last)
+            chosen_last = jnp.where(place == i, final[:, lanes], chosen_last)
         resid[...] = chosen
         skip[...] = chosen_last
 
@@ -608,7 +619,7 @@
         + [scratch(1), keep, sems(), sems(groups, 5), sems(groups, 5)],
     )
     used = (10 + poles) * groups * SUB
-    share = -(-used // total)
+    sum_rows = 9 * groups * SUB + 16 * max(1, per_shard // LANES) + 16
     grads, sums = call(
         functools.partial(finish_kernel, rows, groups),
         "finish",
@@ -616,33 +627,30 @@
         [hbm, vmem] + [hbm] * 9,
         [
             jax.ShapeDtypeStruct(features.shape, BF16),
-            jax.ShapeDtypeStruct((total * share, LANES), F32),
+            jax.ShapeDtypeStruct((ctx_count, sum_rows, LANES), BF16),
         ],
         [hbm, vmem],
         [small]
         + near(2 * poles + 1, poles + 1, 9, extended, extended, extended, extended, extended)
         + near(3 * padded)
         + [scratch(poles), scratch(poles), scratch(3 * rows)]
-        + [pltpu.VMEM((groups, 3, rows, GROUP), BF16), scratch(1), keep]
+        + [pltpu.VMEM((groups, 3, rows, GROUP), BF16)]
+        + [pltpu.VMEM((used + 16, LANES), F32), scratch(1), keep]
         + [sems(), sems(groups, 9), sems(groups, 3)],
     )
 
-    both = ("dp", "ctx")
-    flat = (total, 1, share * LANES)
-    parts = swap(sums.reshape(flat), both).reshape(sums.shape)
-    shares = call(
-        functools.partial(share_kernel, grad_scale),
+    mine = call(
+        share_kernel,
         "share",
-        [parts],
+        [swap(sums, "ctx")],
         [vmem],
-        jax.ShapeDtypeStruct(sums.shape, F32),
+        jax.ShapeDtypeStruct((sum_rows, LANES), BF16),
         vmem,
     )
-    whole = swap(shares.reshape(flat), both).reshape(sums.shape)
     grad_taps, resid, skip = call(
-        functools.partial(emit_kernel, groups),
+        functools.partial(emit_kernel, groups, grad_scale),
         "emit",
-        [whole],
+        [lax.all_gather(mine, "dp")],
         [vmem],
         [
             jax.ShapeDtypeStruct((3, 3 * channels), F32),
@@ -650,6 +658,7 @@
             jax.ShapeDtypeStruct((1, per_shard), F32),
         ],
         [vmem] * 3,
+        [pltpu.VMEM((sum_rows, LANES), F32)],
     )
     return grads, grad_taps, resid, skip.reshape(per_shard)
 

time: 81.3 us -> 76.7 us (0.943)
  blocking collectives: 25.7 us -> 20.1 us
  Pallas kernels: 27.8 us -> 28.8 us
    all_to_all x2 -> x1, blocking collectives: 25.7 us -> 14.5 us  [swap(): return lax.all_to_all(block, axes, split_axis=0, concat_axis=0, tiled=True)]
    all_gather x0 -> x1, blocking collectives: none -> 5.61 us  [per_device(): lax.all_gather(mine, 'dp')]
    pallas_call x5, Pallas kernels: 27.8 us -> 28.8 us  [call(): pl.pallas_call(kernel, out_shape=outs, in_specs=in_specs, out_specs=out_s...]
where the time goes in v5:
time: 76.7 us; the launch traced here: 76.1 us
  Pallas kernels  28.8 us (38%)
  blocking collectives  20.1 us (26%)
  starting transfers between devices  19.4 us (25%)
  waiting for transfers between devices  3.81 us (5%)
  local copies, waits for them, and re-layouts  2.5 us (3%)
  other arithmetic  0.82 us (1%)
    pallas_call x5, Pallas kernels, call(): pl.pallas_call(kernel, out_shape=outs, in_specs=in_specs, out_specs=out_s...  28.8 us
    all_to_all x1, blocking collectives, swap(): return lax.all_to_all(block, axes, split_axis=0, concat_axis=0, tiled=True)  14.5 us
    all_to_all x2, starting transfers between devices, swap(): return lax.all_to_all(block, axes, split_axis=0, concat_axis=0, tiled=True)  13.5 us
    ppermute x2, starting transfers between devices, shifted(): return lax.ppermute(block, axis, route)  5.85 us
    all_gather x1, blocking collectives, per_device(): lax.all_gather(mine, 'dp')  5.61 us
    all_to_all x2, waiting for transfers between devices, swap(): return lax.all_to_all(block, axes, split_axis=0, concat_axis=0, tiled=True)  2.3 us
  transfers between devices with their start and end apart: 4, of which 3 were waited for; matrix products, arithmetic and copies ran while one was open for 2% of the time, Pallas kernels for 15%

profile of v5, /device:TPU:0, one launch (start us, length us, event | category | flops | bytes accessed | tf_op | source)
XLA Modules:
  0.0 76.1 jit_solution(12148589280974541048)
XLA Ops:
  0.6 0.0 copy-start
  0.6 0.8 %pad_maximum_fusion = f32[33,256]{1,0:T(8,128)S(1)} fusion(f32[1,256]{1,0:T(1,128)} %bitcast.10, f32[16,256]{1,0:T(8,128)} %param.11, f32[16,256]{1,0:T(8,128)} %param.12), kind=kLoop, calls=%fused_computation | loop fusion | flops 16896 | bytes 67584 | tf_op jit(solution)/shard_map/concatenate | solution.py:588
  1.4 0.7 broadcast_in_dim.10
  2.2 7.3 %all-to-all-start = ((f32[8,33,256]{2,1,0:T(8,128)}), f32[8,33,256]{2,1,0:T(8,128)S(1)}, u32[]{:S(2)}, u32[]{:S(2)}) async-start(f32[8,33,256]{2,1,0:T(8,128)} %broadcast_in_dim.10), calls=%async_computation | async-start | bytes 655360 | tf_op jit(solution)/shard_map/all_to_all | solution.py:530
  9.5 0.8 %slice_bitcast_fusion.2 = bf16[2,2048]{1,0:T(2,128)(2,1)S(1)} fusion(bf16[1,128,2048]{2,1,0:T(8,128)(2,1)} %upstream.1), kind=kLoop, calls=%fused_computation.4 | loop fusion | bytes 16384 | tf_op jit(solution)/shard_map/squeeze | solution.py:585
  10.2 1.0 %slice_bitcast_fusion = (bf16[2,6144]{1,0:T(2,128)(2,1)S(1)}, bf16[2,6144]{1,0:T(2,128)(2,1)S(1)}) fusion(bf16[1,128,6144]{2,1,0:T(8,128)(2,1)} %features.1), kind=kLoop, calls=%fused_computation.2 | loop fusion | bytes 98304 | tf_op jit(solution)/shard_map/squeeze | solution.py:585
  11.2 1.3 %collective-permute-start.1 = (bf16[2,8192]{1,0:T(2,128)(2,1)S(1)}, bf16[2,8192]{1,0:T(2,128)(2,1)S(1)}, u32[]{:S(2)}, u32[]{:S(2)}) collective-permute-start(bf16[2,8192]{1,0:T(2,128)(2,1)S(1)} %pad_maximum_fusion.1), channel_id=1, source_target_pairs={{1,0},{2,1},{3,2},{4,3},{5,4},{6,5},{7,6},{9,8},{10,9},{11,10},{12... | collective-permute-start | bytes 98312 | tf_op jit(solution)/shard_map/ppermute | solution.py:22
  12.5 4.6 %collective-permute-start = (bf16[2,6144]{1,0:T(2,128)(2,1)S(1)}, bf16[2,6144]{1,0:T(2,128)(2,1)S(1)}, u32[]{:S(2)}, u32[]{:S(2)}) collective-permute-start(bf16[2,6144]{1,0:T(2,128)(2,1)S(1)} %get-tuple-element.39), channel_id=1, source_target_pairs={{0,1},{1,2},{2,3},{3,4},{4,5},{5,6},{6,7},{8,9},{9,10},{10,11},{11... | collective-permute-start | bytes 73736 | tf_op jit(solution)/shard_map/ppermute | solution.py:22
  17.1 1.5 %collective-permute-done.left = bf16[2,6144]{1,0:T(2,128)(2,1)S(1)} collective-permute-done((bf16[2,6144]{1,0:T(2,128)(2,1)S(1)}, bf16[2,6144]{1,0:T(2,128)(2,1)S(1)}, u32[]{:S(2)}, u32[]{:S(2)}) %collective-permute-start) | collective-permute-done | bytes 24608 | tf_op jit(solution)/shard_map/ppermute | solution.py:22
  18.6 0.0 collective-permute-done.1.right
  18.6 1.5 %all-to-all-done.params = f32[8,33,256]{2,1,0:T(8,128)S(1)} async-done(((f32[8,33,256]{2,1,0:T(8,128)}), f32[8,33,256]{2,1,0:T(8,128)S(1)}, u32[]{:S(2)}, u32[]{:S(2)}) %all-to-all-start) | async-done | bytes 270368 | tf_op jit(solution)/shard_map/all_to_all | solution.py:530
  20.1 0.0 copy-done
  20.1 6.9 %ends.1 = (bf16[8,2,128,128]{3,2,1,0:T(8,128)(2,1)}, f32[2,3168,128]{2,1,0:T(8,128)}, f32[2,1040,128]{2,1,0:T(8,128)}, f32[2,1040,128]{2,1,0:T(8,128)}, f32[2,10...) custom-call(s32[1,8]{1,0:T(1,128)} %far_lengths.5, bf16[1,128,6144]{2,1,0:T(8,128)(2,1)} %features.1, ...), custom_call_target="tpu_custom_call" | custom-call | tf_op jit(solution)/shard_map/ends/pallas_call | solution.py:574
  27.1 6.2 %all-to-all-start.1 = ((bf16[8,2,128,128]{3,2,1,0:T(8,128)(2,1)}), bf16[8,2,128,128]{3,2,1,0:T(8,128)(2,1)S(1)}, u32[]{:S(2)}, u32[]{:S(2)}) async-start(bf16[8,2,128,128]{3,2,1,0:T(8,128)(2,1)} %get-tuple-element.21), calls=%async_computation.1 | async-start | bytes 1048576 | tf_op jit(solution)/shard_map/all_to_all | solution.py:530
  33.3 11.7 %local.1 = (f32[2,1040,128]{2,1,0:T(8,128)}, f32[2,1040,128]{2,1,0:T(8,128)}, f32[2,1040,128]{2,1,0:T(8,128)}, f32[2,1040,128]{2,1,0:T(8,128)}, f32[2,136,128]{2,1,0:T(8,128)}) custom-call(s32[1,8]{1,0:T(1,128)} %far_lengths.5, f32[2,3168,128]{2,1,0:T(8,128)} %get-tuple-element.23.feat_in, f32[2,1040,128]{2,1,0:T(8,128)} %get-tuple-element.24.mixed_in, ...), custom_call_target="tpu_custom_call" | custom-call | tf_op jit(solution)/shard_map/local/pallas_call | solution.py:574
  45.1 0.8 %all-to-all-done.1.arrived = bf16[8,2,128,128]{3,2,1,0:T(8,128)(2,1)S(1)} async-done(((bf16[8,2,128,128]{3,2,1,0:T(8,128)(2,1)}), bf16[8,2,128,128]{3,2,1,0:T(8,128)(2,1)S(1)}, u32[]{:S(2)}, u32[]{:S(2)}) %all-to-all-start.1) | async-done | bytes 524320 | tf_op jit(solution)/shard_map/all_to_all | solution.py:530
  45.9 9.4 %finish.1 = (bf16[1,128,6144]{2,1,0:T(8,128)(2,1)}, bf16[8,192,128]{2,1,0:T(8,128)(2,1)S(1)}) custom-call(s32[1,8]{1,0:T(1,128)} %far_lengths.5, bf16[8,2,128,128]{3,2,1,0:T(8,128)(2,1)S(1)} %all-to-all-done.1.arrived, f32[2,264,128]{2,1,0:T(8,128)} %get-tuple-element.22.par_in, f32[2,136,128]{2,1,0:T(8,128)} %get-tuple-element.27.partial_in, ...), custom_call_target="tpu_custom_call" | custom-call | tf_op jit(solution)/shard_map/finish/pallas_call | solution.py:574
  55.3 14.5 %all_to_all.15.parts = bf16[8,192,128]{2,1,0:T(8,128)(2,1)S(1)} all-to-all(bf16[8,192,128]{2,1,0:T(8,128)(2,1)S(1)} %get-tuple-element.34), channel_id=1, replica_groups=mesh['dp'=4,'ctx'=8] {'ctx'}, dimensions={0} | all-to-all | bytes 786432 | tf_op jit(solution)/shard_map/all_to_all | solution.py:530
  69.8 0.1 share.1
  69.8 5.6 %all-gather = bf16[768,128]{1,0:T(8,128)(2,1)S(1)} all-gather(bf16[192,128]{1,0:T(8,128)(2,1)S(1)} %share.1), channel_id=2, replica_groups=mesh['dp'=4,'ctx'=8] {'dp'}, dimensions={0}, use_global_device_ids=true | all-gather | bytes 245760 | tf_op jit(solution)/shard_map/all_gather | solution.py:653
  75.4 0.7 emit.1
  (1 shorter events, 0.0 us)
Async XLA Ops:
  0.6 19.5 %copy-start = (f32[3,6144]{1,0:T(4,128)S(1)}, f32[3,6144]{1,0:T(4,128)}, u32[]{:S(2)}) copy-start(f32[3,6144]{1,0:T(4,128)} %taps.1) | copy-start | bytes 221188
  2.2 18.0 %all-to-all-start = ((f32[8,33,256]{2,1,0:T(8,128)}), f32[8,33,256]{2,1,0:T(8,128)S(1)}, u32[]{:S(2)}, u32[]{:S(2)}) async-start(f32[8,33,256]{2,1,0:T(8,128)} %broadcast_in_dim.10), calls=%async_computation | async-start | bytes 655360 | tf_op jit(solution)/shard_map/all_to_all | solution.py:530
  11.2 7.4 %collective-permute-start.1 = (bf16[2,8192]{1,0:T(2,128)(2,1)S(1)}, bf16[2,8192]{1,0:T(2,128)(2,1)S(1)}, u32[]{:S(2)}, u32[]{:S(2)}) collective-permute-start(bf16[2,8192]{1,0:T(2,128)(2,1)S(1)} %pad_maximum_fusion.1), channel_id=1, source_target_pairs={{1,0},{2,1},{3,2},{4,3},{5,4},{6,5},{7,6},{9,8},{10,9},{11,10},{12... | collective-permute-start | bytes 98312 | tf_op jit(solution)/shard_map/ppermute | solution.py:22
  12.5 6.1 %collective-permute-start = (bf16[2,6144]{1,0:T(2,128)(2,1)S(1)}, bf16[2,6144]{1,0:T(2,128)(2,1)S(1)}, u32[]{:S(2)}, u32[]{:S(2)}) collective-permute-start(bf16[2,6144]{1,0:T(2,128)(2,1)S(1)} %get-tuple-element.39), channel_id=1, source_target_pairs={{0,1},{1,2},{2,3},{3,4},{4,5},{5,6},{6,7},{8,9},{9,10},{10,11},{11... | collective-permute-start | bytes 73736 | tf_op jit(solution)/shard_map/ppermute | solution.py:22
  27.1 18.8 %all-to-all-start.1 = ((bf16[8,2,128,128]{3,2,1,0:T(8,128)(2,1)}), bf16[8,2,128,128]{3,2,1,0:T(8,128)(2,1)S(1)}, u32[]{:S(2)}, u32[]{:S(2)}) async-start(bf16[8,2,128,128]{3,2,1,0:T(8,128)(2,1)} %get-tuple-element.21), calls=%async_computation.1 | async-start | bytes 1048576 | tf_op jit(solution)/shard_map/all_to_all | solution.py:530

commit v6 on v5

--- a/solution.py
+++ b/solution.py
@@ -46,22 +46,33 @@
     lax.fori_loop(0, row_count // 16, step, 0)
 
 
-def spread_params(dst, par, half, groups):
-    pieces, rows, width = par.shape
-    base = half * (pieces // groups)
-    for j in range(SUB):
-        if width >= LANES:
-            per = width // LANES
-            at = (j % per) * LANES
-            parts = [(j // per, at, LANES)]
-        else:
-            per = LANES // width
-            parts = [(j * per + i, 0, width) for i in range(per)]
-        for first in range(0, rows, SUB):
-            many = min(SUB, rows - first)
-            got = [par[base + k, first : first + many, at : at + w] for k, at, w in parts]
-            value = got[0] if len(got) == 1 else jnp.concatenate(got, axis=1)
-            dst[pl.ds(first * SUB + j, many, stride=SUB), :] = value
+def pack_kernel(log_rate, residues, skip_gain, out, slab):
+    poles, width = log_rate.shape
+    per = max(1, width // LANES)
+    for j in range(per):
+        lanes = slice(j * LANES, min(width, (j + 1) * LANES))
+        slab[pl.ds(j, poles, stride=per), :] = log_rate[:, lanes]
+        slab[pl.ds(poles * per + j, poles, stride=per), :] = residues[:, lanes]
+        slab[pl.ds(2 * poles * per + j, 1), :] = skip_gain[:, lanes]
+    for e in range(out.shape[0]):
+        out[e] = slab[...]
+
+
+def spread_params(dst, par, half, groups, rows):
+    pieces, height, width = par.shape
+    many = pieces // groups
+    base = half * many
+    if width == LANES:
+        per = height // rows
+        for k in range(many):
+            for j in range(per):
+                value = par[base + k, pl.ds(j, rows, stride=per), :]
+                dst[pl.ds(k * per + j, rows, stride=SUB), :] = value
+    else:
+        per = LANES // width
+        for j in range(SUB):
+            parts = [par[base + j * per + i] for i in range(per)]
+            dst[pl.ds(j, rows, stride=SUB), :] = jnp.concatenate(parts, axis=1)
 
 
 def segment_starts(lengths):
@@ -93,6 +104,14 @@
 
 def flag(condition):
     return jnp.where(condition, 1.0, 0.0).astype(F32)
+
+
+def total_of(terms):
+    terms = list(terms)
+    while len(terms) > 1:
+        odd = terms[-1:] if len(terms) % 2 else []
+        terms = [x + y for x, y in zip(terms[::2], terms[1::2])] + odd
+    return terms[0]
 
 
 def unroll_of(trips):
@@ -141,7 +160,7 @@
     me = lax.axis_index("ctx")
     base = me * rows
     count = payload.shape[0]
-    poles = (params.shape[1] - 1) // 2
+    poles = (par.shape[1] // SUB - 1) // 2
     extended = rows + HALO
     padded = rows + 2 * HALO
     get_lengths = pltpu.make_async_copy(far_lengths, lengths, length_sem)
@@ -167,7 +186,7 @@
     zeros = [zero_scr[...]] * poles
 
     def prepare(half):
-        spread_params(par.at[half], params, half, groups)
+        spread_params(par.at[half], params, half, groups, 2 * poles + 1)
         for third in range(3):
             column = (third * groups + half) * GROUP
             spread(feat.at[half], third * padded, left, column, HALO)
@@ -289,8 +308,8 @@
                 state = [decay[m] * (state[m] * keep_fwd) + x for m in range(per_pass)]
                 adjoint = [decay[m] * (adjoint[m] * keep_bwd) + g for m in range(per_pass)]
                 resid = [resid[m] + own * adjoint[m] for m in range(per_pass)]
-                forward = sum(coeff[m] * state[m] for m in range(per_pass))
-                backward = sum(coeff[m] * adjoint[m] for m in range(per_pass))
+                forward = total_of(coeff[m] * state[m] for m in range(per_pass))
+                backward = total_of(coeff[m] * adjoint[m] for m in range(per_pass))
                 if part == 0:
                     put(conv_h, i, forward + gain * x)
                     put(adj_h, back, backward + gain * g)
@@ -411,8 +430,8 @@
             for step in range(chunk):
                 p = chunk * i + step
                 back = extended - 1 - p
-                put(conv_h, p, vec(conv_h, p) + flag(p < until) * sum(enter))
-                put(adj_h, back, vec(adj_h, back) + flag(back >= since) * sum(leave))
+                put(conv_h, p, vec(conv_h, p) + flag(p < until) * total_of(enter))
+                put(adj_h, back, vec(adj_h, back) + flag(back >= since) * total_of(leave))
                 enter = [decay[m] * enter[m] for m in range(poles)]
                 leave = [decay[m] * leave[m] for m in range(poles)]
             return enter, leave
@@ -433,9 +452,10 @@
         _, near_one, near_two = posted(extended - 2)
 
         def finish(i, carry):
-            one, two, three, tap_sums = carry
+            one, two, three, tap_sums, feat_now, feat_one = carry
             p = rows - 1 - i
             now, masked_one, masked_two = posted(p)
+            feat_two = [vec(feat_h, third * padded + p) for third in range(3)]
             new_sums = []
             for third in range(3):
                 back = (
@@ -444,16 +464,21 @@
                     + taps_h[third][2] * three[third]
                 )
                 put(post, third * rows + p, back)
-                at = third * padded + p
                 new_sums += [
-                    tap_sums[3 * third] + now[third] * vec(feat_h, at + 2),
-                    tap_sums[3 * third + 1] + masked_one[third] * vec(feat_h, at + 1),
-                    tap_sums[3 * third + 2] + masked_two[third] * vec(feat_h, at),
+                    tap_sums[3 * third] + now[third] * feat_now[third],
+                    tap_sums[3 * third + 1] + masked_one[third] * feat_one[third],
+                    tap_sums[3 * third + 2] + masked_two[third] * feat_two[third],
                 ]
-            return masked_one, masked_two, two, new_sums
-
-        _, _, _, tap_sums = lax.fori_loop(
-            0, rows, finish, (near_one, near_two, far_two, [zero] * 9), unroll=4
+            return masked_one, masked_two, two, new_sums, feat_one, feat_two
+
+        feat_last = [vec(feat_h, third * padded + rows + 1) for third in range(3)]
+        feat_before = [vec(feat_h, third * padded + rows) for third in range(3)]
+        _, _, _, tap_sums, _, _ = lax.fori_loop(
+            0,
+            rows,
+            finish,
+            (near_one, near_two, far_two, [zero] * 9, feat_last, feat_before),
+            unroll=4,
         )
         for third in range(3):
             for j in range(3):
@@ -585,8 +610,17 @@
     head = jnp.concatenate([features[0, :HALO, :], upstream[0, :HALO, :]], axis=1)
     left = shifted(edge, "ctx", 1)
     right = shifted(head, "ctx", -1)
-    params = jnp.concatenate([log_rate, residues, skip_gain[None]], axis=0)
-    params = swap(jnp.broadcast_to(params[None], (ctx_count,) + params.shape), "ctx")
+    slab = ((2 * poles + 1) * max(1, per_shard // LANES), min(per_shard, LANES))
+    params = call(
+        pack_kernel,
+        "pack",
+        [log_rate, residues, skip_gain[None]],
+        [vmem] * 3,
+        jax.ShapeDtypeStruct((ctx_count,) + slab, F32),
+        vmem,
+        [pltpu.VMEM(slab, F32)],
+    )
+    params = swap(params, "ctx")
 
     payload, feat, up, mixed, gout, par, tap = call(
         functools.partial(ends_kernel, rows, groups),

time: 76.7 us -> 76.3 us (level)
  local copies, waits for them, and re-layouts: 2.5 us -> 3.89 us
  Pallas kernels: 28.8 us -> 27.7 us
  other arithmetic: 0.82 us -> 0.03 us
    unnamed x2 -> x8, local copies, waits for them, and re-layouts: 0.01 us -> 2.14 us
    pallas_call x5 -> x6, Pallas kernels: 28.8 us -> 27.7 us  [call(): pl.pallas_call(kernel, out_shape=outs, in_specs=in_specs, out_specs=out_s...]
    concatenate x1 -> x0, other arithmetic: 0.79 us -> none  [per_device(): params = jnp.concatenate([log_rate, residues, skip_gain[None]], axis=0)]
where the time goes in v6:
time: 76.3 us; the launch traced here: 76 us
  Pallas kernels  27.7 us (36%)
  blocking collectives  20.5 us (27%)
  starting transfers between devices  20.1 us (26%)
  local copies, waits for them, and re-layouts  3.89 us (5%)
  waiting for transfers between devices  3.13 us (4%)
    pallas_call x6, Pallas kernels, call(): pl.pallas_call(kernel, out_shape=outs, in_specs=in_specs, out_specs=out_s...  27.7 us
    all_to_all x1, blocking collectives, swap(): return lax.all_to_all(block, axes, split_axis=0, concat_axis=0, tiled=True)  14.2 us
    all_to_all x2, starting transfers between devices, swap(): return lax.all_to_all(block, axes, split_axis=0, concat_axis=0, tiled=True)  14.2 us
    all_gather x1, blocking collectives, per_device(): lax.all_gather(mine, 'dp')  6.25 us
    ppermute x2, starting transfers between devices, shifted(): return lax.ppermute(block, axis, route)  5.85 us
    unnamed x8, local copies, waits for them, and re-layouts  2.14 us
    all_to_all x2, waiting for transfers between devices, swap(): return lax.all_to_all(block, axes, split_axis=0, concat_axis=0, tiled=True)  1.63 us
  transfers between devices with their start and end apart: 4, of which 3 were waited for; matrix products, arithmetic and copies ran while one was open for 2% of the time, Pallas kernels for 15%

profile of v6, /device:TPU:0, one launch (start us, length us, event | category | flops | bytes accessed | tf_op | source)
XLA Modules:
  0.0 76.0 jit_solution(11873956307943770994)
XLA Ops:
  0.6 0.0 copy-start
  0.6 0.0 copy-start.1
  0.7 0.7 copy-done.1
  1.4 0.0 copy-start.2
  1.4 0.7 copy-done.2
  2.1 0.0 copy-start.3
  2.1 0.7 copy-done.3
  2.8 0.7 pack.1
  3.5 7.3 %all-to-all-start = ((f32[8,66,128]{2,1,0:T(8,128)}), f32[8,66,128]{2,1,0:T(8,128)S(1)}, u32[]{:S(2)}, u32[]{:S(2)}) async-start(f32[8,66,128]{2,1,0:T(8,128)} %pack.1), calls=%async_computation | async-start | bytes 589824 | tf_op jit(solution)/shard_map/all_to_all | solution.py:555
  10.8 0.8 %slice_bitcast_fusion.2 = bf16[2,2048]{1,0:T(2,128)(2,1)S(1)} fusion(bf16[1,128,2048]{2,1,0:T(8,128)(2,1)} %upstream.1), kind=kLoop, calls=%fused_computation.3 | loop fusion | bytes 16384 | tf_op jit(solution)/shard_map/squeeze | solution.py:610
  11.6 1.0 %slice_bitcast_fusion = (bf16[2,6144]{1,0:T(2,128)(2,1)S(1)}, bf16[2,6144]{1,0:T(2,128)(2,1)S(1)}) fusion(bf16[1,128,6144]{2,1,0:T(8,128)(2,1)} %features.1), kind=kLoop, calls=%fused_computation.1 | loop fusion | bytes 98304 | tf_op jit(solution)/shard_map/squeeze | solution.py:610
  12.6 1.3 %collective-permute-start.1 = (bf16[2,8192]{1,0:T(2,128)(2,1)S(1)}, bf16[2,8192]{1,0:T(2,128)(2,1)S(1)}, u32[]{:S(2)}, u32[]{:S(2)}) collective-permute-start(bf16[2,8192]{1,0:T(2,128)(2,1)S(1)} %pad_maximum_fusion), channel_id=1, source_target_pairs={{1,0},{2,1},{3,2},{4,3},{5,4},{6,5},{7,6},{9,8},{10,9},{11,10},{12... | collective-permute-start | bytes 98312 | tf_op jit(solution)/shard_map/ppermute | solution.py:22
  13.9 4.6 %collective-permute-start = (bf16[2,6144]{1,0:T(2,128)(2,1)S(1)}, bf16[2,6144]{1,0:T(2,128)(2,1)S(1)}, u32[]{:S(2)}, u32[]{:S(2)}) collective-permute-start(bf16[2,6144]{1,0:T(2,128)(2,1)S(1)} %get-tuple-element.39), channel_id=1, source_target_pairs={{0,1},{1,2},{2,3},{3,4},{4,5},{5,6},{6,7},{8,9},{9,10},{10,11},{11... | collective-permute-start | bytes 73736 | tf_op jit(solution)/shard_map/ppermute | solution.py:22
  18.5 1.5 %collective-permute-done.left = bf16[2,6144]{1,0:T(2,128)(2,1)S(1)} collective-permute-done((bf16[2,6144]{1,0:T(2,128)(2,1)S(1)}, bf16[2,6144]{1,0:T(2,128)(2,1)S(1)}, u32[]{:S(2)}, u32[]{:S(2)}) %collective-permute-start) | collective-permute-done | bytes 24608 | tf_op jit(solution)/shard_map/ppermute | solution.py:22
  20.0 0.0 collective-permute-done.1.right
  20.0 0.8 %all-to-all-done.params = f32[8,66,128]{2,1,0:T(8,128)S(1)} async-done(((f32[8,66,128]{2,1,0:T(8,128)}), f32[8,66,128]{2,1,0:T(8,128)S(1)}, u32[]{:S(2)}, u32[]{:S(2)}) %all-to-all-start) | async-done | bytes 270368 | tf_op jit(solution)/shard_map/all_to_all | solution.py:555
  20.8 0.0 copy-done
  20.8 6.9 %ends.1 = (bf16[8,2,128,128]{3,2,1,0:T(8,128)(2,1)}, f32[2,3168,128]{2,1,0:T(8,128)}, f32[2,1040,128]{2,1,0:T(8,128)}, f32[2,1040,128]{2,1,0:T(8,128)}, f32[2,10...) custom-call(s32[1,8]{1,0:T(1,128)} %far_lengths.5, bf16[1,128,6144]{2,1,0:T(8,128)(2,1)} %features.1, ...), custom_call_target="tpu_custom_call" | custom-call | tf_op jit(solution)/shard_map/ends/pallas_call | solution.py:599
  27.7 6.9 %all-to-all-start.1 = ((bf16[8,2,128,128]{3,2,1,0:T(8,128)(2,1)}), bf16[8,2,128,128]{3,2,1,0:T(8,128)(2,1)S(1)}, u32[]{:S(2)}, u32[]{:S(2)}) async-start(bf16[8,2,128,128]{3,2,1,0:T(8,128)(2,1)} %get-tuple-element.21), calls=%async_computation.1 | async-start | bytes 1048576 | tf_op jit(solution)/shard_map/all_to_all | solution.py:555
  34.7 11.7 %local.1 = (f32[2,1040,128]{2,1,0:T(8,128)}, f32[2,1040,128]{2,1,0:T(8,128)}, f32[2,1040,128]{2,1,0:T(8,128)}, f32[2,1040,128]{2,1,0:T(8,128)}, f32[2,136,128]{2,1,0:T(8,128)}) custom-call(s32[1,8]{1,0:T(1,128)} %far_lengths.5, f32[2,3168,128]{2,1,0:T(8,128)} %get-tuple-element.23.feat_in, f32[2,1040,128]{2,1,0:T(8,128)} %get-tuple-element.24.mixed_in, ...), custom_call_target="tpu_custom_call" | custom-call | tf_op jit(solution)/shard_map/local/pallas_call | solution.py:599
  46.4 0.8 %all-to-all-done.1.arrived = bf16[8,2,128,128]{3,2,1,0:T(8,128)(2,1)S(1)} async-done(((bf16[8,2,128,128]{3,2,1,0:T(8,128)(2,1)}), bf16[8,2,128,128]{3,2,1,0:T(8,128)(2,1)S(1)}, u32[]{:S(2)}, u32[]{:S(2)}) %all-to-all-start.1) | async-done | bytes 524320 | tf_op jit(solution)/shard_map/all_to_all | solution.py:555
  47.2 7.6 %finish.1 = (bf16[1,128,6144]{2,1,0:T(8,128)(2,1)}, bf16[8,192,128]{2,1,0:T(8,128)(2,1)S(1)}) custom-call(s32[1,8]{1,0:T(1,128)} %far_lengths.5, bf16[8,2,128,128]{3,2,1,0:T(8,128)(2,1)S(1)} %all-to-all-done.1.arrived, f32[2,264,128]{2,1,0:T(8,128)} %get-tuple-element.22.par_in, f32[2,136,128]{2,1,0:T(8,128)} %get-tuple-element.27.partial_in, ...), custom_call_target="tpu_custom_call" | custom-call | tf_op jit(solution)/shard_map/finish/pallas_call | solution.py:599
  54.8 14.2 %all_to_all.15.parts = bf16[8,192,128]{2,1,0:T(8,128)(2,1)S(1)} all-to-all(bf16[8,192,128]{2,1,0:T(8,128)(2,1)S(1)} %get-tuple-element.34), channel_id=1, replica_groups=mesh['dp'=4,'ctx'=8] {'ctx'}, dimensions={0} | all-to-all | bytes 786432 | tf_op jit(solution)/shard_map/all_to_all | solution.py:555
  69.0 0.1 share.1
  69.0 6.2 %all-gather = bf16[768,128]{1,0:T(8,128)(2,1)S(1)} all-gather(bf16[192,128]{1,0:T(8,128)(2,1)S(1)} %share.1), channel_id=2, replica_groups=mesh['dp'=4,'ctx'=8] {'dp'}, dimensions={0}, use_global_device_ids=true | all-gather | bytes 245760 | tf_op jit(solution)/shard_map/all_gather | solution.py:687
  75.3 0.7 emit.1
  (1 shorter events, 0.0 us)
Async XLA Ops:
  0.6 20.2 %copy-start = (f32[3,6144]{1,0:T(4,128)S(1)}, f32[3,6144]{1,0:T(4,128)}, u32[]{:S(2)}) copy-start(f32[3,6144]{1,0:T(4,128)} %taps.1) | copy-start | bytes 221188
  0.6 0.8 copy-start.1
  1.4 0.7 copy-start.2
  2.1 0.7 copy-start.3
  3.5 17.3 %all-to-all-start = ((f32[8,66,128]{2,1,0:T(8,128)}), f32[8,66,128]{2,1,0:T(8,128)S(1)}, u32[]{:S(2)}, u32[]{:S(2)}) async-start(f32[8,66,128]{2,1,0:T(8,128)} %pack.1), calls=%async_computation | async-start | bytes 589824 | tf_op jit(solution)/shard_map/all_to_all | solution.py:555
  12.6 7.4 %collective-permute-start.1 = (bf16[2,8192]{1,0:T(2,128)(2,1)S(1)}, bf16[2,8192]{1,0:T(2,128)(2,1)S(1)}, u32[]{:S(2)}, u32[]{:S(2)}) collective-permute-start(bf16[2,8192]{1,0:T(2,128)(2,1)S(1)} %pad_maximum_fusion), channel_id=1, source_target_pairs={{1,0},{2,1},{3,2},{4,3},{5,4},{6,5},{7,6},{9,8},{10,9},{11,10},{12... | collective-permute-start | bytes 98312 | tf_op jit(solution)/shard_map/ppermute | solution.py:22
  13.9 6.1 %collective-permute-start = (bf16[2,6144]{1,0:T(2,128)(2,1)S(1)}, bf16[2,6144]{1,0:T(2,128)(2,1)S(1)}, u32[]{:S(2)}, u32[]{:S(2)}) collective-permute-start(bf16[2,6144]{1,0:T(2,128)(2,1)S(1)} %get-tuple-element.39), channel_id=1, source_target_pairs={{0,1},{1,2},{2,3},{3,4},{4,5},{5,6},{6,7},{8,9},{9,10},{10,11},{11... | collective-permute-start | bytes 73736 | tf_op jit(solution)/shard_map/ppermute | solution.py:22
  27.7 19.5 %all-to-all-start.1 = ((bf16[8,2,128,128]{3,2,1,0:T(8,128)(2,1)}), bf16[8,2,128,128]{3,2,1,0:T(8,128)(2,1)S(1)}, u32[]{:S(2)}, u32[]{:S(2)}) async-start(bf16[8,2,128,128]{3,2,1,0:T(8,128)(2,1)} %get-tuple-element.21), calls=%async_computation.1 | async-start | bytes 1048576 | tf_op jit(solution)/shard_map/all_to_all | solution.py:555

commit v7 on v6

--- a/solution.py
+++ b/solution.py
@@ -46,33 +46,74 @@
     lax.fori_loop(0, row_count // 16, step, 0)
 
 
-def pack_kernel(log_rate, residues, skip_gain, out, slab):
-    poles, width = log_rate.shape
-    per = max(1, width // LANES)
+def tiles_of(width):
+    return max(1, width // LANES)
+
+
+def start_kernel(
+    log_rate, residues, skip_gain, features, upstream, out, edge, head,
+    rates, coeffs, gains, low, high, high_up, slab, sems,
+):
+    rows = features.shape[1]
+    copies = [
+        pltpu.make_async_copy(source, target, sems.at[i])
+        for i, (source, target) in enumerate(
+            [
+                (log_rate, rates),
+                (residues, coeffs),
+                (skip_gain, gains),
+                (features.at[0, pl.ds(0, 16), :], low),
+                (features.at[0, pl.ds(rows - 16, 16), :], high),
+                (upstream.at[0, pl.ds(0, 16), :], high_up),
+            ]
+        )
+    ]
+    start_all(copies)
+    poles, width = rates.shape
+    per = tiles_of(width)
+    slab[...] = jnp.zeros(slab.shape, F32)
+    wait_all(copies[:3])
     for j in range(per):
         lanes = slice(j * LANES, min(width, (j + 1) * LANES))
-        slab[pl.ds(j, poles, stride=per), :] = log_rate[:, lanes]
-        slab[pl.ds(poles * per + j, poles, stride=per), :] = residues[:, lanes]
-        slab[pl.ds(2 * poles * per + j, 1), :] = skip_gain[:, lanes]
+        rate, gain = rates[:, lanes], gains[:, lanes]
+        slab[pl.ds(j, poles, stride=per), :] = rounded(rate)
+        slab[pl.ds(poles * per + j, poles, stride=per), :] = rate - rounded(rate)
+        slab[pl.ds(2 * poles * per + j, poles, stride=per), :] = coeffs[:, lanes]
+        slab[pl.ds(3 * poles * per + j, 1), :] = rounded(gain)
+        slab[pl.ds((3 * poles + 1) * per + j, 1), :] = gain - rounded(gain)
+    packed = slab[...].astype(BF16)
     for e in range(out.shape[0]):
-        out[e] = slab[...]
-
-
-def spread_params(dst, par, half, groups, rows):
+        out[e] = packed
+    wait_all(copies[3:])
+    span = features.shape[2]
+    for at in range(0, span, GROUP):
+        lanes = slice(at, at + GROUP)
+        head[:, lanes] = low[:, lanes].astype(F32)[:HALO].astype(BF16)
+        edge[:, lanes] = high[:, lanes].astype(F32)[16 - HALO :].astype(BF16)
+    for at in range(0, upstream.shape[2], GROUP):
+        lanes = slice(at, at + GROUP)
+        head[:, span + at : span + at + GROUP] = high_up[:, lanes].astype(F32)[:HALO].astype(BF16)
+
+
+def spread_params(dst, par, slab, half, groups, poles):
     pieces, height, width = par.shape
     many = pieces // groups
     base = half * many
-    if width == LANES:
-        per = height // rows
-        for k in range(many):
-            for j in range(per):
-                value = par[base + k, pl.ds(j, rows, stride=per), :]
-                dst[pl.ds(k * per + j, rows, stride=SUB), :] = value
-    else:
-        per = LANES // width
-        for j in range(SUB):
-            parts = [par[base + j * per + i] for i in range(per)]
-            dst[pl.ds(j, rows, stride=SUB), :] = jnp.concatenate(parts, axis=1)
+    joined = LANES // width
+    per = (height - 16) // (3 * poles)
+    for k in range(many // joined):
+        parts = [par[base + k * joined + i].astype(F32) for i in range(joined)]
+        slab[...] = parts[0] if joined == 1 else jnp.concatenate(parts, axis=1)
+        for j in range(per):
+            to = k * per + j
+
+            def rows_of(piece, count=poles):
+                return slab[pl.ds(piece * per + j, count, stride=per), :]
+
+            dst[pl.ds(to, poles, stride=SUB), :] = rows_of(0) + rows_of(poles)
+            dst[pl.ds(poles * SUB + to, poles, stride=SUB), :] = rows_of(2 * poles)
+            gain = rows_of(3 * poles, 1) + rows_of(3 * poles + 1, 1)
+            dst[pl.ds(2 * poles * SUB + to, 1), :] = gain
 
 
 def segment_starts(lengths):
@@ -154,7 +195,7 @@
 def ends_kernel(
     rows, groups, far_lengths, features, upstream, left, right, taps, params,
     payload, feat_out, up_out, mixed_out, gout_out, par_out, tap_out,
-    lengths, raw, raw_up, feat, up, mixed, gout, par, tap, stack, zero_scr, keep,
+    lengths, raw, raw_up, feat, up, mixed, gout, par, tap, stack, slab, zero_scr, keep,
     length_sem, in_sems, out_sems,
 ):
     me = lax.axis_index("ctx")
@@ -186,7 +227,7 @@
     zeros = [zero_scr[...]] * poles
 
     def prepare(half):
-        spread_params(par.at[half], params, half, groups, 2 * poles + 1)
+        spread_params(par.at[half], params, slab, half, groups, poles)
         for third in range(3):
             column = (third * groups + half) * GROUP
             spread(feat.at[half], third * padded, left, column, HALO)
@@ -606,21 +647,33 @@
             name=name,
         )(*ins)
 
-    edge = features[0, rows - HALO :, :]
-    head = jnp.concatenate([features[0, :HALO, :], upstream[0, :HALO, :]], axis=1)
+    block = (3 * poles * tiles_of(per_shard) + 16, min(per_shard, LANES))
+    span = features.shape[2]
+    params, edge, head = call(
+        start_kernel,
+        "start",
+        [log_rate, residues, skip_gain[None], features, upstream],
+        [hbm] * 5,
+        [
+            jax.ShapeDtypeStruct((ctx_count,) + block, BF16),
+            jax.ShapeDtypeStruct((HALO, span), BF16),
+            jax.ShapeDtypeStruct((HALO, span + channels), BF16),
+        ],
+        [vmem] * 3,
+        [
+            pltpu.VMEM((poles, per_shard), F32),
+            pltpu.VMEM((poles, per_shard), F32),
+            pltpu.VMEM((1, per_shard), F32),
+            pltpu.VMEM((16, span), BF16),
+            pltpu.VMEM((16, span), BF16),
+            pltpu.VMEM((16, channels), BF16),
+            pltpu.VMEM(block, F32),
+            sems(6),
+        ],
+    )
+    params = swap(params, "ctx")
     left = shifted(edge, "ctx", 1)
     right = shifted(head, "ctx", -1)
-    slab = ((2 * poles + 1) * max(1, per_shard // LANES), min(per_shard, LANES))
-    params = call(
-        pack_kernel,
-        "pack",
-        [log_rate, residues, skip_gain[None]],
-        [vmem] * 3,
-        jax.ShapeDtypeStruct((ctx_count,) + slab, F32),
-        vmem,
-        [pltpu.VMEM(slab, F32)],
-    )
-    params = swap(params, "ctx")
 
     payload, feat, up, mixed, gout, par, tap = call(
         functools.partial(ends_kernel, rows, groups),
@@ -636,7 +689,8 @@
             pltpu.VMEM((groups, rows, GROUP), BF16),
         ]
         + near(3 * padded, extended, extended, extended, 2 * poles + 1, 9)
-        + [pltpu.VMEM((2, state_rows, LANES), BF16), scratch(1), keep]
+        + [pltpu.VMEM((2, state_rows, LANES), BF16)]
+        + [pltpu.VMEM((block[0], LANES), F32), scratch(1), keep]
         + [sems(), sems(groups, 4), sems(groups, 6)],
     )
     arrived = swap(payload, "ctx")

time: 76.3 us -> 73.8 us (0.967)
  local copies, waits for them, and re-layouts: 3.89 us -> 0.01 us
  blocking collectives: 20.5 us -> 21.4 us
    unnamed x8 -> x2, local copies, waits for them, and re-layouts: 2.14 us -> 0.01 us
    squeeze x2 -> x0, local copies, waits for them, and re-layouts: 1.75 us -> none  [the longest x1 0.98 us: per_device(): features[0, :HALO, :]]
    all_to_all x1, blocking collectives: 14.2 us -> 15.8 us  [swap(): return lax.all_to_all(block, axes, split_axis=0, concat_axis=0, tiled=True)]
  transfers between devices with their start and end apart: 4 -> 4, of which waited for: 3 -> 3; matrix products, arithmetic and copies ran while one was open for 2% -> 0% of each run, Pallas kernels for 15% -> 16%
where the time goes in v7:
time: 73.8 us; the launch traced here: 73.4 us
  Pallas kernels  28.2 us (38%)
  blocking collectives  21.4 us (29%)
  starting transfers between devices  19.7 us (27%)
  waiting for transfers between devices  3.49 us (5%)
    pallas_call x6, Pallas kernels, call(): pl.pallas_call(kernel, out_shape=outs, in_specs=in_specs, out_specs=out_s...  28.2 us
    all_to_all x1, blocking collectives, swap(): return lax.all_to_all(block, axes, split_axis=0, concat_axis=0, tiled=True)  15.8 us
    all_to_all x2, starting transfers between devices, swap(): return lax.all_to_all(block, axes, split_axis=0, concat_axis=0, tiled=True)  13.9 us
    ppermute x2, starting transfers between devices, shifted(): return lax.ppermute(block, axis, route)  5.83 us
    all_gather x1, blocking collectives, per_device(): lax.all_gather(mine, 'dp')  5.61 us
    all_to_all x2, waiting for transfers between devices, swap(): return lax.all_to_all(block, axes, split_axis=0, concat_axis=0, tiled=True)  1.99 us
    ppermute x2, waiting for transfers between devices, shifted(): return lax.ppermute(block, axis, route)  1.5 us
  transfers between devices with their start and end apart: 4, of which 3 were waited for; matrix products, arithmetic and copies ran while one was open for 0% of the time, Pallas kernels for 16%

profile of v7, /device:TPU:0, one launch (start us, length us, event | category | flops | bytes accessed | tf_op | source)
XLA Modules:
  0.0 73.4 jit_solution(3976327078573334988)
XLA Ops:
  0.6 0.0 copy-start
  0.6 1.9 %start.1 = (bf16[8,112,128]{2,1,0:T(8,128)(2,1)}, bf16[2,6144]{1,0:T(2,128)(2,1)S(1)}, bf16[2,8192]{1,0:T(2,128)(2,1)S(1)}) custom-call(f32[16,256]{1,0:T(8,128)} %log_rate.1, f32[16,256]{1,0:T(8,128)} %residues.1, f32[1,256]{1,0:T(1,128)} %bitcast.4, bf16[1,128,6144]{2,1,0:T(8,128)(2,1)} %features.3, bf16[1,128,2048]{2,1,0:T(8,128)(2,1)} %upstream.3), custom_call_target="tpu_custom_call" | custom-call | tf_op jit(solution)/shard_map/start/pallas_call | solution.py:640
  2.5 7.3 %all-to-all-start = ((bf16[8,112,128]{2,1,0:T(8,128)(2,1)}), bf16[8,112,128]{2,1,0:T(8,128)(2,1)S(1)}, u32[]{:S(2)}, u32[]{:S(2)}) async-start(bf16[8,112,128]{2,1,0:T(8,128)(2,1)} %get-tuple-element.26), calls=%async_computation | async-start | bytes 458752 | tf_op jit(solution)/shard_map/all_to_all | solution.py:596
  9.8 1.3 %collective-permute-start.1 = (bf16[2,8192]{1,0:T(2,128)(2,1)S(1)}, bf16[2,8192]{1,0:T(2,128)(2,1)S(1)}, u32[]{:S(2)}, u32[]{:S(2)}) collective-permute-start(bf16[2,8192]{1,0:T(2,128)(2,1)S(1)} %get-tuple-element.25), channel_id=1, source_target_pairs={{1,0},{2,1},{3,2},{4,3},{5,4},{6,5},{7,6},{9,8},{10,9},{11,10},{12... | collective-permute-start | bytes 98312 | tf_op jit(solution)/shard_map/ppermute | solution.py:22
  11.1 4.6 %collective-permute-start = (bf16[2,6144]{1,0:T(2,128)(2,1)S(1)}, bf16[2,6144]{1,0:T(2,128)(2,1)S(1)}, u32[]{:S(2)}, u32[]{:S(2)}) collective-permute-start(bf16[2,6144]{1,0:T(2,128)(2,1)S(1)} %get-tuple-element.24), channel_id=1, source_target_pairs={{0,1},{1,2},{2,3},{3,4},{4,5},{5,6},{6,7},{8,9},{9,10},{10,11},{11... | collective-permute-start | bytes 73736 | tf_op jit(solution)/shard_map/ppermute | solution.py:22
  15.6 1.5 %collective-permute-done.left = bf16[2,6144]{1,0:T(2,128)(2,1)S(1)} collective-permute-done((bf16[2,6144]{1,0:T(2,128)(2,1)S(1)}, bf16[2,6144]{1,0:T(2,128)(2,1)S(1)}, u32[]{:S(2)}, u32[]{:S(2)}) %collective-permute-start) | collective-permute-done | bytes 24608 | tf_op jit(solution)/shard_map/ppermute | solution.py:22
  17.1 0.0 collective-permute-done.1.right
  17.2 1.2 %all-to-all-done.params = bf16[8,112,128]{2,1,0:T(8,128)(2,1)S(1)} async-done(((bf16[8,112,128]{2,1,0:T(8,128)(2,1)}), bf16[8,112,128]{2,1,0:T(8,128)(2,1)S(1)}, u32[]{:S(2)}, u32[]{:S(2)}) %all-to-all-start) | async-done | bytes 229408 | tf_op jit(solution)/shard_map/all_to_all | solution.py:596
  18.3 0.0 copy-done
  18.3 6.9 %ends.1 = (bf16[8,2,128,128]{3,2,1,0:T(8,128)(2,1)}, f32[2,3168,128]{2,1,0:T(8,128)}, f32[2,1040,128]{2,1,0:T(8,128)}, f32[2,1040,128]{2,1,0:T(8,128)}, f32[2,10...) custom-call(s32[1,8]{1,0:T(1,128)} %far_lengths.5, bf16[1,128,6144]{2,1,0:T(8,128)(2,1)} %features.3, ...), custom_call_target="tpu_custom_call" | custom-call | tf_op jit(solution)/shard_map/ends/pallas_call | solution.py:640
  25.3 6.6 %all-to-all-start.1 = ((bf16[8,2,128,128]{3,2,1,0:T(8,128)(2,1)}), bf16[8,2,128,128]{3,2,1,0:T(8,128)(2,1)S(1)}, u32[]{:S(2)}, u32[]{:S(2)}) async-start(bf16[8,2,128,128]{3,2,1,0:T(8,128)(2,1)} %get-tuple-element.27), calls=%async_computation.1 | async-start | bytes 1048576 | tf_op jit(solution)/shard_map/all_to_all | solution.py:596
  31.9 11.7 %local.1 = (f32[2,1040,128]{2,1,0:T(8,128)}, f32[2,1040,128]{2,1,0:T(8,128)}, f32[2,1040,128]{2,1,0:T(8,128)}, f32[2,1040,128]{2,1,0:T(8,128)}, f32[2,136,128]{2,1,0:T(8,128)}) custom-call(s32[1,8]{1,0:T(1,128)} %far_lengths.5, f32[2,3168,128]{2,1,0:T(8,128)} %get-tuple-element.29.feat_in, f32[2,1040,128]{2,1,0:T(8,128)} %get-tuple-element.30.mixed_in, ...), custom_call_target="tpu_custom_call" | custom-call | tf_op jit(solution)/shard_map/local/pallas_call | solution.py:640
  43.6 0.8 %all-to-all-done.1.arrived = bf16[8,2,128,128]{3,2,1,0:T(8,128)(2,1)S(1)} async-done(((bf16[8,2,128,128]{3,2,1,0:T(8,128)(2,1)}), bf16[8,2,128,128]{3,2,1,0:T(8,128)(2,1)S(1)}, u32[]{:S(2)}, u32[]{:S(2)}) %all-to-all-start.1) | async-done | bytes 524320 | tf_op jit(solution)/shard_map/all_to_all | solution.py:596
  44.4 6.9 %finish.1 = (bf16[1,128,6144]{2,1,0:T(8,128)(2,1)}, bf16[8,192,128]{2,1,0:T(8,128)(2,1)S(1)}) custom-call(s32[1,8]{1,0:T(1,128)} %far_lengths.5, bf16[8,2,128,128]{3,2,1,0:T(8,128)(2,1)S(1)} %all-to-all-done.1.arrived, f32[2,264,128]{2,1,0:T(8,128)} %get-tuple-element.28.par_in, f32[2,136,128]{2,1,0:T(8,128)} %get-tuple-element.33.partial_in, ...), custom_call_target="tpu_custom_call" | custom-call | tf_op jit(solution)/shard_map/finish/pallas_call | solution.py:640
  51.3 15.8 %all_to_all.15.parts = bf16[8,192,128]{2,1,0:T(8,128)(2,1)S(1)} all-to-all(bf16[8,192,128]{2,1,0:T(8,128)(2,1)S(1)} %get-tuple-element.40), channel_id=1, replica_groups=mesh['dp'=4,'ctx'=8] {'ctx'}, dimensions={0} | all-to-all | bytes 786432 | tf_op jit(solution)/shard_map/all_to_all | solution.py:596
  67.1 0.1 share.1
  67.1 5.6 %all-gather = bf16[768,128]{1,0:T(8,128)(2,1)S(1)} all-gather(bf16[192,128]{1,0:T(8,128)(2,1)S(1)} %share.1), channel_id=2, replica_groups=mesh['dp'=4,'ctx'=8] {'dp'}, dimensions={0}, use_global_device_ids=true | all-gather | bytes 245760 | tf_op jit(solution)/shard_map/all_gather | solution.py:741
  72.7 0.7 emit.1
Async XLA Ops:
  0.6 17.7 %copy-start = (f32[3,6144]{1,0:T(4,128)S(1)}, f32[3,6144]{1,0:T(4,128)}, u32[]{:S(2)}) copy-start(f32[3,6144]{1,0:T(4,128)} %taps.1) | copy-start | bytes 221188
  2.5 15.8 %all-to-all-start = ((bf16[8,112,128]{2,1,0:T(8,128)(2,1)}), bf16[8,112,128]{2,1,0:T(8,128)(2,1)S(1)}, u32[]{:S(2)}, u32[]{:S(2)}) async-start(bf16[8,112,128]{2,1,0:T(8,128)(2,1)} %get-tuple-element.26), calls=%async_computation | async-start | bytes 458752 | tf_op jit(solution)/shard_map/all_to_all | solution.py:596
  9.8 7.4 %collective-permute-start.1 = (bf16[2,8192]{1,0:T(2,128)(2,1)S(1)}, bf16[2,8192]{1,0:T(2,128)(2,1)S(1)}, u32[]{:S(2)}, u32[]{:S(2)}) collective-permute-start(bf16[2,8192]{1,0:T(2,128)(2,1)S(1)} %get-tuple-element.25), channel_id=1, source_target_pairs={{1,0},{2,1},{3,2},{4,3},{5,4},{6,5},{7,6},{9,8},{10,9},{11,10},{12... | collective-permute-start | bytes 98312 | tf_op jit(solution)/shard_map/ppermute | solution.py:22
  11.1 6.1 %collective-permute-start = (bf16[2,6144]{1,0:T(2,128)(2,1)S(1)}, bf16[2,6144]{1,0:T(2,128)(2,1)S(1)}, u32[]{:S(2)}, u32[]{:S(2)}) collective-permute-start(bf16[2,6144]{1,0:T(2,128)(2,1)S(1)} %get-tuple-element.24), channel_id=1, source_target_pairs={{0,1},{1,2},{2,3},{3,4},{4,5},{5,6},{6,7},{8,9},{9,10},{10,11},{11... | collective-permute-start | bytes 73736 | tf_op jit(solution)/shard_map/ppermute | solution.py:22
  25.3 19.1 %all-to-all-start.1 = ((bf16[8,2,128,128]{3,2,1,0:T(8,128)(2,1)}), bf16[8,2,128,128]{3,2,1,0:T(8,128)(2,1)S(1)}, u32[]{:S(2)}, u32[]{:S(2)}) async-start(bf16[8,2,128,128]{3,2,1,0:T(8,128)(2,1)} %get-tuple-element.27), calls=%async_computation.1 | async-start | bytes 1048576 | tf_op jit(solution)/shard_map/all_to_all | solution.py:596

commit v8 on v7

--- a/solution.py
+++ b/solution.py
@@ -373,11 +373,23 @@
     each_group(groups, lambda half: wait_all(group_copies(near_out, far_out, out_sems, half)))
 
 
-def finish_kernel(
-    rows, groups, far_lengths, arrived, par_in, partial_in, tap_in, conv_in, adj_in, up_in,
-    key_in, val_in, feat_in, grads, payload,
-    lengths, par, partial, tap, conv, adj, up, key, val, feat, before, after, post, ready,
-    sums, zero_scr, keep, length_sem, in_sems, out_sems,
+def posted_rows(keep, conv, adj, up, key, val):
+    def posted(p):
+        keep_one = keep[p + 1]
+        keep_two = keep_one * keep[p]
+        conv_out = rounded(vec(conv, p))
+        grad_mixed = rounded(vec(adj, p))
+        now = [vec(up, p) * conv_out, grad_mixed * vec(val, p), grad_mixed * vec(key, p)]
+        return now, [keep_one * g for g in now], [keep_two * g for g in now]
+
+    return posted
+
+
+def sums_kernel(
+    rows, groups, far_lengths, arrived, par_in, partial_in, conv_in, adj_in, up_in, key_in, val_in,
+    feat_in, conv_out, adj_out, payload,
+    lengths, par, partial, conv, adj, up, key, val, feat, before, after, sums, zero_scr, keep,
+    length_sem, in_sems, out_sems,
 ):
     me = lax.axis_index("ctx")
     base = me * rows
@@ -387,22 +399,9 @@
     padded = rows + 2 * HALO
     get_lengths = pltpu.make_async_copy(far_lengths, lengths, length_sem)
     get_lengths.start()
-    far = [par_in, partial_in, conv_in, adj_in, tap_in, up_in, key_in, val_in, feat_in]
-    near = [par, partial, conv, adj, tap, up, key, val, feat]
+    far = [par_in, partial_in, conv_in, adj_in, up_in, key_in, val_in, feat_in]
+    near = [par, partial, conv, adj, up, key, val, feat]
     each_group(groups, lambda half: start_all(group_copies(far, near, in_sems, half)))
-
-    def leaving(half):
-        return [
-            pltpu.make_async_copy(
-                ready.at[half, third],
-                grads.at[
-                    0, :, pl.ds(pl.multiple_of((third * groups + half) * GROUP, GROUP), GROUP)
-                ],
-                out_sems.at[half, third],
-            )
-            for third in range(3)
-        ]
-
     zero_scr[...] = jnp.zeros((SUB, LANES), F32)
     zero = zero_scr[...]
     get_lengths.wait()
@@ -423,8 +422,9 @@
 
     def group(half):
         incoming = group_copies(far, near, in_sems, half)
+        outgoing = group_copies([conv, adj], [conv_out, adj_out], out_sems, half)
         par_h, partial_h, conv_h, adj_h = par.at[half], partial.at[half], conv.at[half], adj.at[half]
-        up_h, key_h, val_h, feat_h = up.at[half], key.at[half], val.at[half], feat.at[half]
+        feat_h = feat.at[half]
         wait_all(incoming[:2])
         per_pass = poles // 2
         zeros = [zero] * per_pass
@@ -478,26 +478,91 @@
             return enter, leave
 
         lax.fori_loop(0, (steps + chunk - 1) // chunk, carried, (enter, leave))
+        start_all(outgoing)
         wait_all(incoming[4:])
-        taps_h = [[vec(tap.at[half], third * 3 + j) for j in range(3)] for third in range(3)]
-
-        def posted(p):
-            keep_one = keep[p + 1]
-            keep_two = keep_one * keep[p]
-            conv_out = rounded(vec(conv_h, p))
-            grad_mixed = rounded(vec(adj_h, p))
-            now = [vec(up_h, p) * conv_out, grad_mixed * vec(val_h, p), grad_mixed * vec(key_h, p)]
-            return now, [keep_one * g for g in now], [keep_two * g for g in now]
-
-        _, _, far_two = posted(extended - 1)
-        _, near_one, near_two = posted(extended - 2)
-
-        def finish(i, carry):
-            one, two, three, tap_sums, feat_now, feat_one = carry
+        posted = posted_rows(keep, conv_h, adj_h, up.at[half], key.at[half], val.at[half])
+
+        def tap_terms(i, carry):
+            tap_sums, feat_now, feat_one = carry
             p = rows - 1 - i
             now, masked_one, masked_two = posted(p)
             feat_two = [vec(feat_h, third * padded + p) for third in range(3)]
             new_sums = []
+            for third in range(3):
+                new_sums += [
+                    tap_sums[3 * third] + now[third] * feat_now[third],
+                    tap_sums[3 * third + 1] + masked_one[third] * feat_one[third],
+                    tap_sums[3 * third + 2] + masked_two[third] * feat_two[third],
+                ]
+            return new_sums, feat_one, feat_two
+
+        feat_last = [vec(feat_h, third * padded + rows + 1) for third in range(3)]
+        feat_before = [vec(feat_h, third * padded + rows) for third in range(3)]
+        tap_sums, _, _ = lax.fori_loop(
+            0, rows, tap_terms, ([zero] * 9, feat_last, feat_before), unroll=4
+        )
+        for third in range(3):
+            for j in range(3):
+                put(sums, (3 * j + third) * groups + half, tap_sums[3 * third + j])
+
+    each_group(groups, group)
+    width = groups * SUB
+    same = 9 * width
+    tap_sums = sums[0:same, :].astype(BF16)
+    columns = (payload.shape[1] - same) // 16 - 1
+    for e in range(count):
+        payload[e, 0:same, :] = tap_sums
+        first_row = same + (e * width) // count
+        for j in range(columns):
+            value = sums[pl.ds(first_row + j, 16, stride=width), :]
+            payload[e, same + 16 * j : same + 16 * (j + 1), :] = value.astype(BF16)
+        last_row = first_row + poles * width
+        payload[e, same + 16 * columns :, :] = sums[last_row : last_row + 16, :].astype(BF16)
+    each_group(
+        groups,
+        lambda half: wait_all(group_copies([conv, adj], [conv_out, adj_out], out_sems, half)),
+    )
+
+
+def grads_kernel(
+    rows, groups, far_lengths, tap_in, conv_in, adj_in, up_in, key_in, val_in, grads,
+    lengths, tap, conv, adj, up, key, val, post, ready, keep, length_sem, in_sems, out_sems,
+):
+    extended = rows + HALO
+    get_lengths = pltpu.make_async_copy(far_lengths, lengths, length_sem)
+    get_lengths.start()
+    far = [tap_in, conv_in, adj_in, up_in, key_in, val_in]
+    near = [tap, conv, adj, up, key, val]
+    each_group(groups, lambda half: start_all(group_copies(far, near, in_sems, half)))
+
+    def leaving(half):
+        return [
+            pltpu.make_async_copy(
+                ready.at[half, third],
+                grads.at[
+                    0, :, pl.ds(pl.multiple_of((third * groups + half) * GROUP, GROUP), GROUP)
+                ],
+                out_sems.at[half, third],
+            )
+            for third in range(3)
+        ]
+
+    get_lengths.wait()
+    fill_keep(keep, segment_starts(lengths), lax.axis_index("ctx") * rows, rows)
+
+    def group(half):
+        wait_all(group_copies(far, near, in_sems, half))
+        taps_h = [[vec(tap.at[half], third * 3 + j) for j in range(3)] for third in range(3)]
+        posted = posted_rows(
+            keep, conv.at[half], adj.at[half], up.at[half], key.at[half], val.at[half]
+        )
+        _, _, far_two = posted(extended - 1)
+        _, near_one, near_two = posted(extended - 2)
+
+        def transposed(i, carry):
+            one, two, three = carry
+            p = rows - 1 - i
+            now, masked_one, masked_two = posted(p)
             for third in range(3):
                 back = (
                     taps_h[third][0] * now[third]
@@ -505,51 +570,24 @@
                     + taps_h[third][2] * three[third]
                 )
                 put(post, third * rows + p, back)
-                new_sums += [
-                    tap_sums[3 * third] + now[third] * feat_now[third],
-                    tap_sums[3 * third + 1] + masked_one[third] * feat_one[third],
-                    tap_sums[3 * third + 2] + masked_two[third] * feat_two[third],
-                ]
-            return masked_one, masked_two, two, new_sums, feat_one, feat_two
-
-        feat_last = [vec(feat_h, third * padded + rows + 1) for third in range(3)]
-        feat_before = [vec(feat_h, third * padded + rows) for third in range(3)]
-        _, _, _, tap_sums, _, _ = lax.fori_loop(
-            0,
-            rows,
-            finish,
-            (near_one, near_two, far_two, [zero] * 9, feat_last, feat_before),
-            unroll=4,
-        )
-        for third in range(3):
-            for j in range(3):
-                put(sums, (3 * j + third) * groups + half, tap_sums[3 * third + j])
+            return masked_one, masked_two, two
+
+        lax.fori_loop(0, rows, transposed, (near_one, near_two, far_two), unroll=4)
 
         def write(i, carry):
             for third in range(3):
                 for j in range(SUB):
                     value = post[pl.ds((third * rows + i * 16) * SUB + j, 16, stride=SUB), :]
-                    ready[
-                        half, third, pl.ds(pl.multiple_of(i * 16, 16), 16), j * LANES : (j + 1) * LANES
-                    ] = value.astype(BF16)
+                    lanes = slice(j * LANES, (j + 1) * LANES)
+                    ready[half, third, pl.ds(pl.multiple_of(i * 16, 16), 16), lanes] = value.astype(
+                        BF16
+                    )
             return carry
 
-        lax.fori_loop(0, rows // 16, write, 0)
+        lax.fori_loop(0, rows // 16, write, 0, unroll=2)
         start_all(leaving(half))
 
     each_group(groups, group)
-    width = groups * SUB
-    same = 9 * width
-    tap_sums = sums[0:same, :].astype(BF16)
-    columns = (payload.shape[1] - same) // 16 - 1
-    for e in range(count):
-        payload[e, 0:same, :] = tap_sums
-        first = same + (e * width) // count
-        for j in range(columns):
-            value = sums[pl.ds(first + j, 16, stride=width), :]
-            payload[e, same + 16 * j : same + 16 * (j + 1), :] = value.astype(BF16)
-        last = first + poles * width
-        payload[e, same + 16 * columns :, :] = sums[last : last + 16, :].astype(BF16)
     each_group(groups, lambda half: wait_all(leaving(half)))
 
 
@@ -708,29 +746,37 @@
     )
     used = (10 + poles) * groups * SUB
     sum_rows = 9 * groups * SUB + 16 * max(1, per_shard // LANES) + 16
-    grads, sums = call(
-        functools.partial(finish_kernel, rows, groups),
-        "finish",
-        [lengths, arrived, par, partial, tap, conv, adj, up, key, val, feat],
-        [hbm, vmem] + [hbm] * 9,
-        [
-            jax.ShapeDtypeStruct(features.shape, BF16),
-            jax.ShapeDtypeStruct((ctx_count, sum_rows, LANES), BF16),
-        ],
-        [hbm, vmem],
+    conv, adj, sums = call(
+        functools.partial(sums_kernel, rows, groups),
+        "sums",
+        [lengths, arrived, par, partial, conv, adj, up, key, val, feat],
+        [hbm, vmem] + [hbm] * 8,
+        [tall(extended)] * 2 + [jax.ShapeDtypeStruct((ctx_count, sum_rows, LANES), BF16)],
+        [hbm, hbm, vmem],
         [small]
-        + near(2 * poles + 1, poles + 1, 9, extended, extended, extended, extended, extended)
+        + near(2 * poles + 1, poles + 1, extended, extended, extended, extended, extended)
         + near(3 * padded)
-        + [scratch(poles), scratch(poles), scratch(3 * rows)]
-        + [pltpu.VMEM((groups, 3, rows, GROUP), BF16)]
+        + [scratch(poles), scratch(poles)]
         + [pltpu.VMEM((used + 16, LANES), F32), scratch(1), keep]
-        + [sems(), sems(groups, 9), sems(groups, 3)],
-    )
-
+        + [sems(), sems(groups, 8), sems(groups, 2)],
+    )
+    parts = swap(sums, "ctx")
+    (grads,) = call(
+        functools.partial(grads_kernel, rows, groups),
+        "grads",
+        [lengths, tap, conv, adj, up, key, val],
+        [hbm] * 7,
+        [jax.ShapeDtypeStruct(features.shape, BF16)],
+        [hbm],
+        [small]
+        + near(9, extended, extended, extended, extended, extended)
+        + [scratch(3 * rows), pltpu.VMEM((groups, 3, rows, GROUP), BF16), keep]
+        + [sems(), sems(groups, 6), sems(groups, 3)],
+    )
     mine = call(
         share_kernel,
         "share",
-        [swap(sums, "ctx")],
+        [parts],
         [vmem],
         jax.ShapeDtypeStruct((sum_rows, LANES), BF16),
         vmem,

time: 73.8 us -> 72.1 us (0.977)
  blocking collectives: 21.4 us -> 5.79 us
  starting transfers between devices: 19.7 us -> 25 us
  waiting for transfers between devices: 3.49 us -> 7.59 us
  Pallas kernels: 28.2 us -> 32.3 us
    all_to_all x1 -> x0, blocking collectives: 15.8 us -> none  [swap(): return lax.all_to_all(block, axes, split_axis=0, concat_axis=0, tiled=True)]
    all_to_all x2 -> x3, starting transfers between devices: 13.9 us -> 19.1 us  [swap(): return lax.all_to_all(block, axes, split_axis=0, concat_axis=0, tiled=True)]
    all_to_all x2 -> x3, waiting for transfers between devices: 1.99 us -> 6.09 us  [swap(): return lax.all_to_all(block, axes, split_axis=0, concat_axis=0, tiled=True)]
    pallas_call x6 -> x7, Pallas kernels: 28.2 us -> 32.3 us  [call(): pl.pallas_call(kernel, out_shape=outs, in_specs=in_specs, out_specs=out_s...]
  transfers between devices with their start and end apart: 4 -> 5, of which waited for: 3 -> 4; matrix products, arithmetic and copies ran while one was open for 0% -> 0% of each run, Pallas kernels for 16% -> 24%
where the time goes in v8:
time: 72.1 us; the launch traced here: 71.3 us
  Pallas kernels  32.3 us (45%)
  starting transfers between devices  25 us (35%)
  waiting for transfers between devices  7.59 us (11%)
  blocking collectives  5.79 us (8%)
    pallas_call x7, Pallas kernels, call(): pl.pallas_call(kernel, out_shape=outs, in_specs=in_specs, out_specs=out_s...  32.3 us
    all_to_all x3, starting transfers between devices, swap(): return lax.all_to_all(block, axes, split_axis=0, concat_axis=0, tiled=True)  19.1 us
    all_to_all x3, waiting for transfers between devices, swap(): return lax.all_to_all(block, axes, split_axis=0, concat_axis=0, tiled=True)  6.09 us
    ppermute x2, starting transfers between devices, shifted(): return lax.ppermute(block, axis, route)  5.83 us
    all_gather x1, blocking collectives, per_device(): lax.all_gather(mine, 'dp')  5.79 us
    ppermute x2, waiting for transfers between devices, shifted(): return lax.ppermute(block, axis, route)  1.5 us
  transfers between devices with their start and end apart: 5, of which 4 were waited for; matrix products, arithmetic and copies ran while one was open for 0% of the time, Pallas kernels for 24%

profile of v8, /device:TPU:0, one launch (start us, length us, event | category | flops | bytes accessed | tf_op | source)
XLA Modules:
  0.0 71.3 jit_solution(9160386314588307275)
XLA Ops:
  0.6 0.0 copy-start
  0.6 1.9 %start.1 = (bf16[8,112,128]{2,1,0:T(8,128)(2,1)}, bf16[2,6144]{1,0:T(2,128)(2,1)S(1)}, bf16[2,8192]{1,0:T(2,128)(2,1)S(1)}) custom-call(f32[16,256]{1,0:T(8,128)} %log_rate.1, f32[16,256]{1,0:T(8,128)} %residues.1, f32[1,256]{1,0:T(1,128)} %bitcast.4, bf16[1,128,6144]{2,1,0:T(8,128)(2,1)} %features.3, bf16[1,128,2048]{2,1,0:T(8,128)(2,1)} %upstream.3), custom_call_target="tpu_custom_call" | custom-call | tf_op jit(solution)/shard_map/start/pallas_call | solution.py:678
  2.5 7.3 %all-to-all-start = ((bf16[8,112,128]{2,1,0:T(8,128)(2,1)}), bf16[8,112,128]{2,1,0:T(8,128)(2,1)S(1)}, u32[]{:S(2)}, u32[]{:S(2)}) async-start(bf16[8,112,128]{2,1,0:T(8,128)(2,1)} %get-tuple-element.27), calls=%async_computation | async-start | bytes 458752 | tf_op jit(solution)/shard_map/all_to_all | solution.py:634
  9.8 1.3 %collective-permute-start.1 = (bf16[2,8192]{1,0:T(2,128)(2,1)S(1)}, bf16[2,8192]{1,0:T(2,128)(2,1)S(1)}, u32[]{:S(2)}, u32[]{:S(2)}) collective-permute-start(bf16[2,8192]{1,0:T(2,128)(2,1)S(1)} %get-tuple-element.26), channel_id=1, source_target_pairs={{1,0},{2,1},{3,2},{4,3},{5,4},{6,5},{7,6},{9,8},{10,9},{11,10},{12... | collective-permute-start | bytes 98312 | tf_op jit(solution)/shard_map/ppermute | solution.py:22
  11.1 4.6 %collective-permute-start = (bf16[2,6144]{1,0:T(2,128)(2,1)S(1)}, bf16[2,6144]{1,0:T(2,128)(2,1)S(1)}, u32[]{:S(2)}, u32[]{:S(2)}) collective-permute-start(bf16[2,6144]{1,0:T(2,128)(2,1)S(1)} %get-tuple-element.25), channel_id=1, source_target_pairs={{0,1},{1,2},{2,3},{3,4},{4,5},{5,6},{6,7},{8,9},{9,10},{10,11},{11... | collective-permute-start | bytes 73736 | tf_op jit(solution)/shard_map/ppermute | solution.py:22
  15.6 1.5 %collective-permute-done.left = bf16[2,6144]{1,0:T(2,128)(2,1)S(1)} collective-permute-done((bf16[2,6144]{1,0:T(2,128)(2,1)S(1)}, bf16[2,6144]{1,0:T(2,128)(2,1)S(1)}, u32[]{:S(2)}, u32[]{:S(2)}) %collective-permute-start) | collective-permute-done | bytes 24608 | tf_op jit(solution)/shard_map/ppermute | solution.py:22
  17.1 0.0 collective-permute-done.1.right
  17.2 1.2 %all-to-all-done.params = bf16[8,112,128]{2,1,0:T(8,128)(2,1)S(1)} async-done(((bf16[8,112,128]{2,1,0:T(8,128)(2,1)}), bf16[8,112,128]{2,1,0:T(8,128)(2,1)S(1)}, u32[]{:S(2)}, u32[]{:S(2)}) %all-to-all-start) | async-done | bytes 229408 | tf_op jit(solution)/shard_map/all_to_all | solution.py:634
  18.3 0.0 copy-done
  18.3 6.9 %ends.1 = (bf16[8,2,128,128]{3,2,1,0:T(8,128)(2,1)}, f32[2,3168,128]{2,1,0:T(8,128)}, f32[2,1040,128]{2,1,0:T(8,128)}, f32[2,1040,128]{2,1,0:T(8,128)}, f32[2,10...) custom-call(s32[1,8]{1,0:T(1,128)} %far_lengths.7, bf16[1,128,6144]{2,1,0:T(8,128)(2,1)} %features.3, ...), custom_call_target="tpu_custom_call" | custom-call | tf_op jit(solution)/shard_map/ends/pallas_call | solution.py:678
  25.3 6.6 %all-to-all-start.1 = ((bf16[8,2,128,128]{3,2,1,0:T(8,128)(2,1)}), bf16[8,2,128,128]{3,2,1,0:T(8,128)(2,1)S(1)}, u32[]{:S(2)}, u32[]{:S(2)}) async-start(bf16[8,2,128,128]{3,2,1,0:T(8,128)(2,1)} %get-tuple-element.29), calls=%async_computation.1 | async-start | bytes 1048576 | tf_op jit(solution)/shard_map/all_to_all | solution.py:634
  31.9 11.7 %local.1 = (f32[2,1040,128]{2,1,0:T(8,128)}, f32[2,1040,128]{2,1,0:T(8,128)}, f32[2,1040,128]{2,1,0:T(8,128)}, f32[2,1040,128]{2,1,0:T(8,128)}, f32[2,136,128]{2,1,0:T(8,128)}) custom-call(s32[1,8]{1,0:T(1,128)} %far_lengths.7, f32[2,3168,128]{2,1,0:T(8,128)} %get-tuple-element.31.feat_in, f32[2,1040,128]{2,1,0:T(8,128)} %get-tuple-element.32.mixed_in, ...), custom_call_target="tpu_custom_call" | custom-call | tf_op jit(solution)/shard_map/local/pallas_call | solution.py:678
  43.6 0.8 %all-to-all-done.1.arrived = bf16[8,2,128,128]{3,2,1,0:T(8,128)(2,1)S(1)} async-done(((bf16[8,2,128,128]{3,2,1,0:T(8,128)(2,1)}), bf16[8,2,128,128]{3,2,1,0:T(8,128)(2,1)S(1)}, u32[]{:S(2)}, u32[]{:S(2)}) %all-to-all-start.1) | async-done | bytes 524320 | tf_op jit(solution)/shard_map/all_to_all | solution.py:634
  44.4 5.9 %sums.1 = (f32[2,1040,128]{2,1,0:T(8,128)}, f32[2,1040,128]{2,1,0:T(8,128)}, bf16[8,192,128]{2,1,0:T(8,128)(2,1)}) custom-call(s32[1,8]{1,0:T(1,128)} %far_lengths.7, bf16[8,2,128,128]{3,2,1,0:T(8,128)(2,1)S(1)} %all-to-all-done.1.arrived, f32[2,264,128]{2,1,0:T(8,128)} %get-tuple-element.30.par_in, f32[2,136,128]{2,1,0:T(8,128)} %get-tuple-element.34.partial_in, ...), custom_call_target="tpu_custom_call" | custom-call | tf_op jit(solution)/shard_map/sums/pallas_call | solution.py:678
  50.3 5.2 %all-to-all-start.2 = ((bf16[8,192,128]{2,1,0:T(8,128)(2,1)}), bf16[8,192,128]{2,1,0:T(8,128)(2,1)S(1)}, u32[]{:S(2)}, u32[]{:S(2)}) async-start(bf16[8,192,128]{2,1,0:T(8,128)(2,1)} %get-tuple-element.42), calls=%async_computation.2 | async-start | bytes 786432 | tf_op jit(solution)/shard_map/all_to_all | solution.py:634
  55.5 5.1 %grads.1 = bf16[1,128,6144]{2,1,0:T(8,128)(2,1)} custom-call(s32[1,8]{1,0:T(1,128)} %far_lengths.7, f32[2,72,128]{2,1,0:T(8,128)} %get-tuple-element.28.tap_in, f32[2,1040,128]{2,1,0:T(8,128)} %get-tuple-element.40.conv_in, f32[2,1040,128]{2,1,0:T(8,128)} %get-tuple-element.41.adj_in, f32[2,1040,128]{2,1,0:T(8,128)} %get-tuple-element.37.up_in, ...), custom_call_target="tpu_custom_call" | custom-call | tf_op jit(solution)/shard_map/grads/pallas_call | solution.py:678
  60.6 4.1 %all-to-all-done.2.parts = bf16[8,192,128]{2,1,0:T(8,128)(2,1)S(1)} async-done(((bf16[8,192,128]{2,1,0:T(8,128)(2,1)}), bf16[8,192,128]{2,1,0:T(8,128)(2,1)S(1)}, u32[]{:S(2)}, u32[]{:S(2)}) %all-to-all-start.2) | async-done | bytes 393248 | tf_op jit(solution)/shard_map/all_to_all | solution.py:634
  64.7 0.1 share.1
  64.8 5.8 %all-gather = bf16[768,128]{1,0:T(8,128)(2,1)S(1)} all-gather(bf16[192,128]{1,0:T(8,128)(2,1)S(1)} %share.1), channel_id=2, replica_groups=mesh['dp'=4,'ctx'=8] {'dp'}, dimensions={0}, use_global_device_ids=true | all-gather | bytes 245760 | tf_op jit(solution)/shard_map/all_gather | solution.py:787
  70.6 0.7 %emit.1 = (f32[3,6144]{1,0:T(4,128)}, f32[16,256]{1,0:T(8,128)}, f32[1,256]{1,0:T(1,128)}) custom-call(bf16[4,192,128]{2,1,0:T(8,128)(2,1)S(1)} %bitcast.3), custom_call_target="tpu_custom_call" | custom-call | tf_op jit(solution)/shard_map/emit/pallas_call | solution.py:678
Async XLA Ops:
  0.6 17.7 %copy-start = (f32[3,6144]{1,0:T(4,128)S(1)}, f32[3,6144]{1,0:T(4,128)}, u32[]{:S(2)}) copy-start(f32[3,6144]{1,0:T(4,128)} %taps.1) | copy-start | bytes 221188
  2.5 15.8 %all-to-all-start = ((bf16[8,112,128]{2,1,0:T(8,128)(2,1)}), bf16[8,112,128]{2,1,0:T(8,128)(2,1)S(1)}, u32[]{:S(2)}, u32[]{:S(2)}) async-start(bf16[8,112,128]{2,1,0:T(8,128)(2,1)} %get-tuple-element.27), calls=%async_computation | async-start | bytes 458752 | tf_op jit(solution)/shard_map/all_to_all | solution.py:634
  9.8 7.4 %collective-permute-start.1 = (bf16[2,8192]{1,0:T(2,128)(2,1)S(1)}, bf16[2,8192]{1,0:T(2,128)(2,1)S(1)}, u32[]{:S(2)}, u32[]{:S(2)}) collective-permute-start(bf16[2,8192]{1,0:T(2,128)(2,1)S(1)} %get-tuple-element.26), channel_id=1, source_target_pairs={{1,0},{2,1},{3,2},{4,3},{5,4},{6,5},{7,6},{9,8},{10,9},{11,10},{12... | collective-permute-start | bytes 98312 | tf_op jit(solution)/shard_map/ppermute | solution.py:22
  11.1 6.1 %collective-permute-start = (bf16[2,6144]{1,0:T(2,128)(2,1)S(1)}, bf16[2,6144]{1,0:T(2,128)(2,1)S(1)}, u32[]{:S(2)}, u32[]{:S(2)}) collective-permute-start(bf16[2,6144]{1,0:T(2,128)(2,1)S(1)} %get-tuple-element.25), channel_id=1, source_target_pairs={{0,1},{1,2},{2,3},{3,4},{4,5},{5,6},{6,7},{8,9},{9,10},{10,11},{11... | collective-permute-start | bytes 73736 | tf_op jit(solution)/shard_map/ppermute | solution.py:22
  25.3 19.1 %all-to-all-start.1 = ((bf16[8,2,128,128]{3,2,1,0:T(8,128)(2,1)}), bf16[8,2,128,128]{3,2,1,0:T(8,128)(2,1)S(1)}, u32[]{:S(2)}, u32[]{:S(2)}) async-start(bf16[8,2,128,128]{3,2,1,0:T(8,128)(2,1)} %get-tuple-element.29), calls=%async_computation.1 | async-start | bytes 1048576 | tf_op jit(solution)/shard_map/all_to_all | solution.py:634
  50.3 14.5 %all-to-all-start.2 = ((bf16[8,192,128]{2,1,0:T(8,128)(2,1)}), bf16[8,192,128]{2,1,0:T(8,128)(2,1)S(1)}, u32[]{:S(2)}, u32[]{:S(2)}) async-start(bf16[8,192,128]{2,1,0:T(8,128)(2,1)} %get-tuple-element.42), calls=%async_computation.2 | async-start | bytes 786432 | tf_op jit(solution)/shard_map/all_to_all | solution.py:634

commit v9 on v8

--- a/solution.py
+++ b/solution.py
@@ -69,16 +69,26 @@
         )
     ]
     start_all(copies)
-    poles, width = rates.shape
+    width = rates.shape[1]
+    members = lax.axis_size("dp")
+    poles = rates.shape[0] // members
+
+    def mine(ref, lanes):
+        value = ref[0:poles, lanes]
+        for member in range(1, members):
+            other = ref[member * poles : (member + 1) * poles, lanes]
+            value = jnp.where(lax.axis_index("dp") == member, other, value)
+        return value
+
     per = tiles_of(width)
     slab[...] = jnp.zeros(slab.shape, F32)
     wait_all(copies[:3])
     for j in range(per):
         lanes = slice(j * LANES, min(width, (j + 1) * LANES))
-        rate, gain = rates[:, lanes], gains[:, lanes]
+        rate, gain = mine(rates, lanes), gains[:, lanes]
         slab[pl.ds(j, poles, stride=per), :] = rounded(rate)
         slab[pl.ds(poles * per + j, poles, stride=per), :] = rate - rounded(rate)
-        slab[pl.ds(2 * poles * per + j, poles, stride=per), :] = coeffs[:, lanes]
+        slab[pl.ds(2 * poles * per + j, poles, stride=per), :] = mine(coeffs, lanes)
         slab[pl.ds(3 * poles * per + j, 1), :] = rounded(gain)
         slab[pl.ds((3 * poles + 1) * per + j, 1), :] = gain - rounded(gain)
     packed = slab[...].astype(BF16)
@@ -96,24 +106,30 @@
 
 
 def spread_params(dst, par, slab, half, groups, poles):
-    pieces, height, width = par.shape
+    members = lax.axis_size("dp")
+    pieces = par.shape[0] // members
+    width = par.shape[2]
+    share = poles // members
     many = pieces // groups
-    base = half * many
     joined = LANES // width
-    per = (height - 16) // (3 * poles)
-    for k in range(many // joined):
-        parts = [par[base + k * joined + i].astype(F32) for i in range(joined)]
-        slab[...] = parts[0] if joined == 1 else jnp.concatenate(parts, axis=1)
-        for j in range(per):
-            to = k * per + j
-
-            def rows_of(piece, count=poles):
-                return slab[pl.ds(piece * per + j, count, stride=per), :]
-
-            dst[pl.ds(to, poles, stride=SUB), :] = rows_of(0) + rows_of(poles)
-            dst[pl.ds(poles * SUB + to, poles, stride=SUB), :] = rows_of(2 * poles)
-            gain = rows_of(3 * poles, 1) + rows_of(3 * poles + 1, 1)
-            dst[pl.ds(2 * poles * SUB + to, 1), :] = gain
+    per = SUB * joined // many
+    for member in range(members):
+        base = member * pieces + half * many
+        for k in range(many // joined):
+            parts = [par[base + k * joined + i].astype(F32) for i in range(joined)]
+            slab[...] = parts[0] if joined == 1 else jnp.concatenate(parts, axis=1)
+            for j in range(per):
+
+                def rows_of(piece, count):
+                    return slab[pl.ds(piece * per + j, count, stride=per), :]
+
+                first = member * share * SUB + k * per + j
+                rates = rows_of(0, share) + rows_of(share, share)
+                dst[pl.ds(first, share, stride=SUB), :] = rates
+                dst[pl.ds(poles * SUB + first, share, stride=SUB), :] = rows_of(2 * share, share)
+                if member == 0:
+                    gain = rows_of(3 * share, 1) + rows_of(3 * share + 1, 1)
+                    dst[pl.ds(2 * poles * SUB + k * per + j, 1), :] = gain
 
 
 def segment_starts(lengths):
@@ -338,31 +354,34 @@
             decay = [jnp.exp(-jnp.exp(vec(par_h, m))) for m in chosen]
             coeff = [vec(par_h, poles + m) for m in chosen]
 
-            def sweep(i, carry):
+            def sweep(i, carry, inside=True):
                 state, adjoint, resid, skip = carry
                 back = extended - 1 - i
                 x = vec(mixed_h, i)
                 g = vec(gout_h, back)
-                own = vec(mixed_h, back) * flag(back < rows)
                 keep_fwd = keep[i + 1]
                 keep_bwd = keep[back + 2]
                 state = [decay[m] * (state[m] * keep_fwd) + x for m in range(per_pass)]
                 adjoint = [decay[m] * (adjoint[m] * keep_bwd) + g for m in range(per_pass)]
-                resid = [resid[m] + own * adjoint[m] for m in range(per_pass)]
                 forward = total_of(coeff[m] * state[m] for m in range(per_pass))
                 backward = total_of(coeff[m] * adjoint[m] for m in range(per_pass))
+                if inside:
+                    own = vec(mixed_h, back)
+                    resid = [resid[m] + own * adjoint[m] for m in range(per_pass)]
                 if part == 0:
                     put(conv_h, i, forward + gain * x)
                     put(adj_h, back, backward + gain * g)
-                    skip = skip + own * g
+                    if inside:
+                        skip = skip + own * g
                 else:
                     put(conv_h, i, forward + vec(conv_h, i))
                     put(adj_h, back, backward + vec(adj_h, back))
                 return state, adjoint, resid, skip
 
-            _, _, resid, skip = lax.fori_loop(
-                0, extended, sweep, (zeros, zeros, zeros, zero), unroll=unroll_of(extended)
-            )
+            carry = (zeros, zeros, zeros, zero)
+            for i in range(HALO):
+                carry = sweep(i, carry, inside=False)
+            _, _, resid, skip = lax.fori_loop(HALO, extended, sweep, carry, unroll=16)
             for i, m in enumerate(chosen):
                 put(partial.at[half], m, resid[i])
             if part == 0:
@@ -685,7 +704,8 @@
             name=name,
         )(*ins)
 
-    block = (3 * poles * tiles_of(per_shard) + 16, min(per_shard, LANES))
+    block_rows = (3 * poles // lax.axis_size("dp") + 2) * tiles_of(per_shard)
+    block = (-(-block_rows // 16) * 16, min(per_shard, LANES))
     span = features.shape[2]
     params, edge, head = call(
         start_kernel,
@@ -693,7 +713,7 @@
         [log_rate, residues, skip_gain[None], features, upstream],
         [hbm] * 5,
         [
-            jax.ShapeDtypeStruct((ctx_count,) + block, BF16),
+            jax.ShapeDtypeStruct((total,) + block, BF16),
             jax.ShapeDtypeStruct((HALO, span), BF16),
             jax.ShapeDtypeStruct((HALO, span + channels), BF16),
         ],
@@ -709,7 +729,7 @@
             sems(6),
         ],
     )
-    params = swap(params, "ctx")
+    params = swap(params, ("dp", "ctx"))
     left = shifted(edge, "ctx", 1)
     right = shifted(head, "ctx", -1)
 

time: 72.1 us -> 73.3 us (1.017)
  waiting for transfers between devices: 7.59 us -> 12.6 us
  starting transfers between devices: 25 us -> 21.8 us
    all_to_all x3, waiting for transfers between devices: 6.09 us -> 11.1 us  [swap(): return lax.all_to_all(block, axes, split_axis=0, concat_axis=0, tiled=True)]
    all_to_all x3, starting transfers between devices: 19.1 us -> 16 us  [swap(): return lax.all_to_all(block, axes, split_axis=0, concat_axis=0, tiled=True)]
  transfers between devices with their start and end apart: 5 -> 5, of which waited for: 4 -> 4; matrix products, arithmetic and copies ran while one was open for 0% -> 0% of each run, Pallas kernels for 24% -> 23%
where the time goes in v9:
time: 73.3 us; the launch traced here: 72.8 us
  Pallas kernels  32.1 us (44%)
  starting transfers between devices  21.8 us (30%)
  waiting for transfers between devices  12.6 us (17%)
  blocking collectives  5.61 us (8%)
    pallas_call x7, Pallas kernels, call(): pl.pallas_call(kernel, out_shape=outs, in_specs=in_specs, out_specs=out_s...  32.1 us
    all_to_all x3, starting transfers between devices, swap(): return lax.all_to_all(block, axes, split_axis=0, concat_axis=0, tiled=True)  16 us
    all_to_all x3, waiting for transfers between devices, swap(): return lax.all_to_all(block, axes, split_axis=0, concat_axis=0, tiled=True)  11.1 us
    ppermute x2, starting transfers between devices, shifted(): return lax.ppermute(block, axis, route)  5.84 us
    all_gather x1, blocking collectives, per_device(): lax.all_gather(mine, 'dp')  5.61 us
    ppermute x2, waiting for transfers between devices, shifted(): return lax.ppermute(block, axis, route)  1.5 us
  transfers between devices with their start and end apart: 5, of which 4 were waited for; matrix products, arithmetic and copies ran while one was open for 0% of the time, Pallas kernels for 23%

profile of v9, /device:TPU:0, one launch (start us, length us, event | category | flops | bytes accessed | tf_op | source)
XLA Modules:
  0.0 72.8 jit_solution(17893143339746409244)
XLA Ops:
  0.6 0.0 copy-start
  0.6 1.9 %start.1 = (bf16[32,32,128]{2,1,0:T(8,128)(2,1)}, bf16[2,6144]{1,0:T(2,128)(2,1)S(1)}, bf16[2,8192]{1,0:T(2,128)(2,1)S(1)}) custom-call(f32[16,256]{1,0:T(8,128)} %log_rate.1, f32[16,256]{1,0:T(8,128)} %residues.1, f32[1,256]{1,0:T(1,128)} %bitcast.4, bf16[1,128,6144]{2,1,0:T(8,128)(2,1)} %features.3, bf16[1,128,2048]{2,1,0:T(8,128)(2,1)} %upstream.3), custom_call_target="tpu_custom_call" | custom-call | tf_op jit(solution)/shard_map/start/pallas_call | solution.py:697
  2.5 7.3 %all-to-all-start = ((bf16[32,32,128]{2,1,0:T(8,128)(2,1)}), bf16[32,32,128]{2,1,0:T(8,128)(2,1)S(1)}, u32[]{:S(2)}, u32[]{:S(2)}) async-start(bf16[32,32,128]{2,1,0:T(8,128)(2,1)} %get-tuple-element.27), calls=%async_computation | async-start | bytes 524288 | tf_op jit(solution)/shard_map/all_to_all | solution.py:653
  9.8 1.3 %collective-permute-start.1 = (bf16[2,8192]{1,0:T(2,128)(2,1)S(1)}, bf16[2,8192]{1,0:T(2,128)(2,1)S(1)}, u32[]{:S(2)}, u32[]{:S(2)}) collective-permute-start(bf16[2,8192]{1,0:T(2,128)(2,1)S(1)} %get-tuple-element.26), channel_id=1, source_target_pairs={{1,0},{2,1},{3,2},{4,3},{5,4},{6,5},{7,6},{9,8},{10,9},{11,10},{12... | collective-permute-start | bytes 98312 | tf_op jit(solution)/shard_map/ppermute | solution.py:22
  11.1 4.5 %collective-permute-start = (bf16[2,6144]{1,0:T(2,128)(2,1)S(1)}, bf16[2,6144]{1,0:T(2,128)(2,1)S(1)}, u32[]{:S(2)}, u32[]{:S(2)}) collective-permute-start(bf16[2,6144]{1,0:T(2,128)(2,1)S(1)} %get-tuple-element.25), channel_id=1, source_target_pairs={{0,1},{1,2},{2,3},{3,4},{4,5},{5,6},{6,7},{8,9},{9,10},{10,11},{11... | collective-permute-start | bytes 73736 | tf_op jit(solution)/shard_map/ppermute | solution.py:22
  15.7 1.5 %collective-permute-done.left = bf16[2,6144]{1,0:T(2,128)(2,1)S(1)} collective-permute-done((bf16[2,6144]{1,0:T(2,128)(2,1)S(1)}, bf16[2,6144]{1,0:T(2,128)(2,1)S(1)}, u32[]{:S(2)}, u32[]{:S(2)}) %collective-permute-start) | collective-permute-done | bytes 24608 | tf_op jit(solution)/shard_map/ppermute | solution.py:22
  17.2 0.0 collective-permute-done.1.right
  17.2 3.3 %all-to-all-done.params = bf16[32,32,128]{2,1,0:T(8,128)(2,1)S(1)} async-done(((bf16[32,32,128]{2,1,0:T(8,128)(2,1)}), bf16[32,32,128]{2,1,0:T(8,128)(2,1)S(1)}, u32[]{:S(2)}, u32[]{:S(2)}) %all-to-all-start) | async-done | bytes 262176 | tf_op jit(solution)/shard_map/all_to_all | solution.py:653
  20.5 0.0 copy-done
  20.5 6.9 %ends.1 = (bf16[8,2,128,128]{3,2,1,0:T(8,128)(2,1)}, f32[2,3168,128]{2,1,0:T(8,128)}, f32[2,1040,128]{2,1,0:T(8,128)}, f32[2,1040,128]{2,1,0:T(8,128)}, f32[2,10...) custom-call(s32[1,8]{1,0:T(1,128)} %far_lengths.7, bf16[1,128,6144]{2,1,0:T(8,128)(2,1)} %features.3, ...), custom_call_target="tpu_custom_call" | custom-call | tf_op jit(solution)/shard_map/ends/pallas_call | solution.py:697
  27.4 4.2 %all-to-all-start.1 = ((bf16[8,2,128,128]{3,2,1,0:T(8,128)(2,1)}), bf16[8,2,128,128]{3,2,1,0:T(8,128)(2,1)S(1)}, u32[]{:S(2)}, u32[]{:S(2)}) async-start(bf16[8,2,128,128]{3,2,1,0:T(8,128)(2,1)} %get-tuple-element.29), calls=%async_computation.1 | async-start | bytes 1048576 | tf_op jit(solution)/shard_map/all_to_all | solution.py:653
  31.7 11.3 %local.1 = (f32[2,1040,128]{2,1,0:T(8,128)}, f32[2,1040,128]{2,1,0:T(8,128)}, f32[2,1040,128]{2,1,0:T(8,128)}, f32[2,1040,128]{2,1,0:T(8,128)}, f32[2,136,128]{2,1,0:T(8,128)}) custom-call(s32[1,8]{1,0:T(1,128)} %far_lengths.7, f32[2,3168,128]{2,1,0:T(8,128)} %get-tuple-element.31.feat_in, f32[2,1040,128]{2,1,0:T(8,128)} %get-tuple-element.32.mixed_in, ...), custom_call_target="tpu_custom_call" | custom-call | tf_op jit(solution)/shard_map/local/pallas_call | solution.py:697
  43.0 2.6 %all-to-all-done.1.arrived = bf16[8,2,128,128]{3,2,1,0:T(8,128)(2,1)S(1)} async-done(((bf16[8,2,128,128]{3,2,1,0:T(8,128)(2,1)}), bf16[8,2,128,128]{3,2,1,0:T(8,128)(2,1)S(1)}, u32[]{:S(2)}, u32[]{:S(2)}) %all-to-all-start.1) | async-done | bytes 524320 | tf_op jit(solution)/shard_map/all_to_all | solution.py:653
  45.6 6.1 %sums.1 = (f32[2,1040,128]{2,1,0:T(8,128)}, f32[2,1040,128]{2,1,0:T(8,128)}, bf16[8,192,128]{2,1,0:T(8,128)(2,1)}) custom-call(s32[1,8]{1,0:T(1,128)} %far_lengths.7, bf16[8,2,128,128]{3,2,1,0:T(8,128)(2,1)S(1)} %all-to-all-done.1.arrived, f32[2,264,128]{2,1,0:T(8,128)} %get-tuple-element.30.par_in, f32[2,136,128]{2,1,0:T(8,128)} %get-tuple-element.34.partial_in, ...), custom_call_target="tpu_custom_call" | custom-call | tf_op jit(solution)/shard_map/sums/pallas_call | solution.py:697
  51.7 4.4 %all-to-all-start.2 = ((bf16[8,192,128]{2,1,0:T(8,128)(2,1)}), bf16[8,192,128]{2,1,0:T(8,128)(2,1)S(1)}, u32[]{:S(2)}, u32[]{:S(2)}) async-start(bf16[8,192,128]{2,1,0:T(8,128)(2,1)} %get-tuple-element.42), calls=%async_computation.2 | async-start | bytes 786432 | tf_op jit(solution)/shard_map/all_to_all | solution.py:653
  56.1 5.1 %grads.1 = bf16[1,128,6144]{2,1,0:T(8,128)(2,1)} custom-call(s32[1,8]{1,0:T(1,128)} %far_lengths.7, f32[2,72,128]{2,1,0:T(8,128)} %get-tuple-element.28.tap_in, f32[2,1040,128]{2,1,0:T(8,128)} %get-tuple-element.40.conv_in, f32[2,1040,128]{2,1,0:T(8,128)} %get-tuple-element.41.adj_in, f32[2,1040,128]{2,1,0:T(8,128)} %get-tuple-element.37.up_in, ...), custom_call_target="tpu_custom_call" | custom-call | tf_op jit(solution)/shard_map/grads/pallas_call | solution.py:697
  61.3 5.1 %all-to-all-done.2.parts = bf16[8,192,128]{2,1,0:T(8,128)(2,1)S(1)} async-done(((bf16[8,192,128]{2,1,0:T(8,128)(2,1)}), bf16[8,192,128]{2,1,0:T(8,128)(2,1)S(1)}, u32[]{:S(2)}, u32[]{:S(2)}) %all-to-all-start.2) | async-done | bytes 393248 | tf_op jit(solution)/shard_map/all_to_all | solution.py:653
  66.4 0.1 share.1
  66.5 5.6 %all-gather = bf16[768,128]{1,0:T(8,128)(2,1)S(1)} all-gather(bf16[192,128]{1,0:T(8,128)(2,1)S(1)} %share.1), channel_id=2, replica_groups=mesh['dp'=4,'ctx'=8] {'dp'}, dimensions={0}, use_global_device_ids=true | all-gather | bytes 245760 | tf_op jit(solution)/shard_map/all_gather | solution.py:807
  72.1 0.7 emit.1
Async XLA Ops:
  0.6 19.8 %copy-start = (f32[3,6144]{1,0:T(4,128)S(1)}, f32[3,6144]{1,0:T(4,128)}, u32[]{:S(2)}) copy-start(f32[3,6144]{1,0:T(4,128)} %taps.1) | copy-start | bytes 221188
  2.5 18.0 %all-to-all-start = ((bf16[32,32,128]{2,1,0:T(8,128)(2,1)}), bf16[32,32,128]{2,1,0:T(8,128)(2,1)S(1)}, u32[]{:S(2)}, u32[]{:S(2)}) async-start(bf16[32,32,128]{2,1,0:T(8,128)(2,1)} %get-tuple-element.27), calls=%async_computation | async-start | bytes 524288 | tf_op jit(solution)/shard_map/all_to_all | solution.py:653
  9.8 7.4 %collective-permute-start.1 = (bf16[2,8192]{1,0:T(2,128)(2,1)S(1)}, bf16[2,8192]{1,0:T(2,128)(2,1)S(1)}, u32[]{:S(2)}, u32[]{:S(2)}) collective-permute-start(bf16[2,8192]{1,0:T(2,128)(2,1)S(1)} %get-tuple-element.26), channel_id=1, source_target_pairs={{1,0},{2,1},{3,2},{4,3},{5,4},{6,5},{7,6},{9,8},{10,9},{11,10},{12... | collective-permute-start | bytes 98312 | tf_op jit(solution)/shard_map/ppermute | solution.py:22
  11.1 6.1 %collective-permute-start = (bf16[2,6144]{1,0:T(2,128)(2,1)S(1)}, bf16[2,6144]{1,0:T(2,128)(2,1)S(1)}, u32[]{:S(2)}, u32[]{:S(2)}) collective-permute-start(bf16[2,6144]{1,0:T(2,128)(2,1)S(1)} %get-tuple-element.25), channel_id=1, source_target_pairs={{0,1},{1,2},{2,3},{3,4},{4,5},{5,6},{6,7},{8,9},{9,10},{10,11},{11... | collective-permute-start | bytes 73736 | tf_op jit(solution)/shard_map/ppermute | solution.py:22
  27.4 18.2 %all-to-all-start.1 = ((bf16[8,2,128,128]{3,2,1,0:T(8,128)(2,1)}), bf16[8,2,128,128]{3,2,1,0:T(8,128)(2,1)S(1)}, u32[]{:S(2)}, u32[]{:S(2)}) async-start(bf16[8,2,128,128]{3,2,1,0:T(8,128)(2,1)} %get-tuple-element.29), calls=%async_computation.1 | async-start | bytes 1048576 | tf_op jit(solution)/shard_map/all_to_all | solution.py:653
  51.7 14.7 %all-to-all-start.2 = ((bf16[8,192,128]{2,1,0:T(8,128)(2,1)}), bf16[8,192,128]{2,1,0:T(8,128)(2,1)S(1)}, u32[]{:S(2)}, u32[]{:S(2)}) async-start(bf16[8,192,128]{2,1,0:T(8,128)(2,1)} %get-tuple-element.42), calls=%async_computation.2 | async-start | bytes 786432 | tf_op jit(solution)/shard_map/all_to_all | solution.py:653

commit v10 on v9

--- a/solution.py
+++ b/solution.py
@@ -210,8 +210,8 @@
 
 def ends_kernel(
     rows, groups, far_lengths, features, upstream, left, right, taps, params,
-    payload, feat_out, up_out, mixed_out, gout_out, par_out, tap_out,
-    lengths, raw, raw_up, feat, up, mixed, gout, par, tap, stack, slab, zero_scr, keep,
+    payload, feat_out, up_out, mixed_out, gout_out, par_out, tap_out, key_out, val_out,
+    lengths, raw, raw_up, feat, up, mixed, gout, par, tap, key_scr, val_scr, stack, slab, zero_scr, keep,
     length_sem, in_sems, out_sems,
 ):
     me = lax.axis_index("ctx")
@@ -235,8 +235,8 @@
             for third in range(3)
         ] + [pltpu.make_async_copy(upstream.at[0, :, lanes[0]], raw_up.at[half], in_sems.at[half, 3])]
 
-    near = [feat, up, tap, par, mixed, gout]
-    far = [feat_out, up_out, tap_out, par_out, mixed_out, gout_out]
+    near = [feat, up, tap, par, mixed, gout, key_scr, val_scr]
+    far = [feat_out, up_out, tap_out, par_out, mixed_out, gout_out, key_out, val_out]
 
     each_group(groups, lambda half: start_all(arriving(half)))
     zero_scr[...] = jnp.zeros((SUB, LANES), F32)
@@ -282,6 +282,8 @@
             )
             put(mixed_h, p, rounded(key * val))
             put(gout_h, p, rounded(vec(up_h, p) * query))
+            put(key_scr.at[half], p, key)
+            put(val_scr.at[half], p, val)
             return carry
 
         lax.fori_loop(0, extended, product, 0, unroll=unroll_of(extended))
@@ -310,19 +312,16 @@
 
 
 def local_kernel(
-    rows, groups, far_lengths, feat_in, mixed_in, gout_in, par_in, tap_in,
-    key_out, val_out, conv_out, adj_out, partial_out,
-    lengths, mixed, gout, par, tap, feat, key, val, conv, adj, partial, zero_scr, keep,
+    rows, groups, far_lengths, mixed_in, gout_in, par_in, conv_out, adj_out, partial_out,
+    lengths, mixed, gout, par, conv, adj, partial, zero_scr, keep,
     length_sem, in_sems, out_sems,
 ):
     poles = (par.shape[1] // SUB - 1) // 2
     extended = rows + HALO
-    padded = rows + 2 * HALO
     get_lengths = pltpu.make_async_copy(far_lengths, lengths, length_sem)
     get_lengths.start()
-    far_in, near_in = [par_in, tap_in, feat_in, mixed_in, gout_in], [par, tap, feat, mixed, gout]
-    near_out = [key, val, conv, adj, partial]
-    far_out = [key_out, val_out, conv_out, adj_out, partial_out]
+    far_in, near_in = [par_in, mixed_in, gout_in], [par, mixed, gout]
+    near_out, far_out = [conv, adj, partial], [conv_out, adj_out, partial_out]
     each_group(groups, lambda half: start_all(group_copies(far_in, near_in, in_sems, half)))
     zero_scr[...] = jnp.zeros((SUB, LANES), F32)
     zero = zero_scr[...]
@@ -334,20 +333,9 @@
     def group(half):
         incoming = group_copies(far_in, near_in, in_sems, half)
         outgoing = group_copies(near_out, far_out, out_sems, half)
-        feat_h, mixed_h, gout_h, par_h = feat.at[half], mixed.at[half], gout.at[half], par.at[half]
-        conv_h, adj_h, key_h, val_h = conv.at[half], adj.at[half], key.at[half], val.at[half]
+        mixed_h, gout_h, par_h = mixed.at[half], gout.at[half], par.at[half]
+        conv_h, adj_h = conv.at[half], adj.at[half]
         wait_all(incoming)
-        taps_h = [[vec(tap.at[half], third * 3 + j) for j in range(3)] for third in range(3)]
-
-        def product(p, carry):
-            keep_one = keep[p + 1]
-            keep_two = keep_one * keep[p]
-            put(key_h, p, featured(feat_h, taps_h[1], padded + p, keep_one, keep_two))
-            put(val_h, p, featured(feat_h, taps_h[2], 2 * padded + p, keep_one, keep_two))
-            return carry
-
-        lax.fori_loop(0, extended, product, 0, unroll=unroll_of(extended))
-        start_all(outgoing[:2])
         gain = vec(par_h, 2 * poles)
         for part in range(poles // per_pass):
             chosen = list(range(part * per_pass, (part + 1) * per_pass))
@@ -381,12 +369,12 @@
             carry = (zeros, zeros, zeros, zero)
             for i in range(HALO):
                 carry = sweep(i, carry, inside=False)
-            _, _, resid, skip = lax.fori_loop(HALO, extended, sweep, carry, unroll=16)
+            _, _, resid, skip = lax.fori_loop(HALO, extended, sweep, carry, unroll=32)
             for i, m in enumerate(chosen):
                 put(partial.at[half], m, resid[i])
             if part == 0:
                 put(partial.at[half], poles, skip)
-        start_all(outgoing[2:])
+        start_all(outgoing)
 
     each_group(groups, group)
     each_group(groups, lambda half: wait_all(group_copies(near_out, far_out, out_sems, half)))
@@ -733,36 +721,36 @@
     left = shifted(edge, "ctx", 1)
     right = shifted(head, "ctx", -1)
 
-    payload, feat, up, mixed, gout, par, tap = call(
+    payload, feat, up, mixed, gout, par, tap, key, val = call(
         functools.partial(ends_kernel, rows, groups),
         "ends",
         [lengths, features, upstream, left, right, conv_taps, params],
         [hbm] * 3 + [vmem] * 4,
         [jax.ShapeDtypeStruct((ctx_count, groups, state_rows, LANES), BF16)]
-        + [tall(height) for height in [3 * padded] + [extended] * 3 + [2 * poles + 1, 9]],
-        [vmem] + [hbm] * 6,
+        + [tall(height) for height in [3 * padded] + [extended] * 3 + [2 * poles + 1, 9]]
+        + [tall(extended)] * 2,
+        [vmem] + [hbm] * 8,
         [
             small,
             pltpu.VMEM((groups, 3, rows, GROUP), BF16),
             pltpu.VMEM((groups, rows, GROUP), BF16),
         ]
-        + near(3 * padded, extended, extended, extended, 2 * poles + 1, 9)
+        + near(3 * padded, extended, extended, extended, 2 * poles + 1, 9, extended, extended)
         + [pltpu.VMEM((2, state_rows, LANES), BF16)]
         + [pltpu.VMEM((block[0], LANES), F32), scratch(1), keep]
-        + [sems(), sems(groups, 4), sems(groups, 6)],
+        + [sems(), sems(groups, 4), sems(groups, 8)],
     )
     arrived = swap(payload, "ctx")
-    key, val, conv, adj, partial = call(
+    conv, adj, partial = call(
         functools.partial(local_kernel, rows, groups),
         "local",
-        [lengths, feat, mixed, gout, par, tap],
-        [hbm] * 6,
-        [tall(extended)] * 4 + [tall(poles + 1)],
-        [hbm] * 5,
+        [lengths, mixed, gout, par],
+        [hbm] * 4,
+        [tall(extended)] * 2 + [tall(poles + 1)],
+        [hbm] * 3,
         [small]
-        + near(extended, extended, 2 * poles + 1, 9, 3 * padded)
-        + near(extended, extended, extended, extended, poles + 1)
-        + [scratch(1), keep, sems(), sems(groups, 5), sems(groups, 5)],
+        + near(extended, extended, 2 * poles + 1, extended, extended, poles + 1)
+        + [scratch(1), keep, sems(), sems(groups, 3), sems(groups, 3)],
     )
     used = (10 + poles) * groups * SUB
     sum_rows = 9 * groups * SUB + 16 * max(1, per_shard // LANES) + 16

time: 73.3 us -> 73.5 us (level)
  waiting for transfers between devices: 12.6 us -> 14.2 us
  starting transfers between devices: 21.8 us -> 20.9 us
    all_to_all x3, waiting for transfers between devices: 11.1 us -> 12.7 us  [swap(): return lax.all_to_all(block, axes, split_axis=0, concat_axis=0, tiled=True)]
    all_to_all x3, starting transfers between devices: 16 us -> 15 us  [swap(): return lax.all_to_all(block, axes, split_axis=0, concat_axis=0, tiled=True)]
  transfers between devices with their start and end apart: 5 -> 5, of which waited for: 4 -> 4; matrix products, arithmetic and copies ran while one was open for 0% -> 0% of each run, Pallas kernels for 23% -> 20%
where the time goes in v10:
time: 73.5 us; the launch traced here: 72.9 us
  Pallas kernels  31.5 us (43%)
  starting transfers between devices  20.9 us (28%)
  waiting for transfers between devices  14.2 us (19%)
  blocking collectives  5.61 us (8%)
    pallas_call x7, Pallas kernels, call(): pl.pallas_call(kernel, out_shape=outs, in_specs=in_specs, out_specs=out_s...  31.5 us
    all_to_all x3, starting transfers between devices, swap(): return lax.all_to_all(block, axes, split_axis=0, concat_axis=0, tiled=True)  15 us
    all_to_all x3, waiting for transfers between devices, swap(): return lax.all_to_all(block, axes, split_axis=0, concat_axis=0, tiled=True)  12.7 us
    ppermute x2, starting transfers between devices, shifted(): return lax.ppermute(block, axis, route)  5.84 us
    all_gather x1, blocking collectives, per_device(): lax.all_gather(mine, 'dp')  5.61 us
    ppermute x2, waiting for transfers between devices, shifted(): return lax.ppermute(block, axis, route)  1.5 us
  transfers between devices with their start and end apart: 5, of which 4 were waited for; matrix products, arithmetic and copies ran while one was open for 0% of the time, Pallas kernels for 20%

profile of v10, /device:TPU:0, one launch (start us, length us, event | category | flops | bytes accessed | tf_op | source)
XLA Modules:
  0.0 72.9 jit_solution(7427268249307537736)
XLA Ops:
  0.6 0.0 copy-start
  0.6 1.9 %start.1 = (bf16[32,32,128]{2,1,0:T(8,128)(2,1)}, bf16[2,6144]{1,0:T(2,128)(2,1)S(1)}, bf16[2,8192]{1,0:T(2,128)(2,1)S(1)}) custom-call(f32[16,256]{1,0:T(8,128)} %log_rate.1, f32[16,256]{1,0:T(8,128)} %residues.1, f32[1,256]{1,0:T(1,128)} %bitcast.4, bf16[1,128,6144]{2,1,0:T(8,128)(2,1)} %features.3, bf16[1,128,2048]{2,1,0:T(8,128)(2,1)} %upstream.3), custom_call_target="tpu_custom_call" | custom-call | tf_op jit(solution)/shard_map/start/pallas_call | solution.py:685
  2.5 7.3 %all-to-all-start = ((bf16[32,32,128]{2,1,0:T(8,128)(2,1)}), bf16[32,32,128]{2,1,0:T(8,128)(2,1)S(1)}, u32[]{:S(2)}, u32[]{:S(2)}) async-start(bf16[32,32,128]{2,1,0:T(8,128)(2,1)} %get-tuple-element.27), calls=%async_computation | async-start | bytes 524288 | tf_op jit(solution)/shard_map/all_to_all | solution.py:641
  9.8 1.3 %collective-permute-start.1 = (bf16[2,8192]{1,0:T(2,128)(2,1)S(1)}, bf16[2,8192]{1,0:T(2,128)(2,1)S(1)}, u32[]{:S(2)}, u32[]{:S(2)}) collective-permute-start(bf16[2,8192]{1,0:T(2,128)(2,1)S(1)} %get-tuple-element.26), channel_id=1, source_target_pairs={{1,0},{2,1},{3,2},{4,3},{5,4},{6,5},{7,6},{9,8},{10,9},{11,10},{12... | collective-permute-start | bytes 98312 | tf_op jit(solution)/shard_map/ppermute | solution.py:22
  11.1 4.5 %collective-permute-start = (bf16[2,6144]{1,0:T(2,128)(2,1)S(1)}, bf16[2,6144]{1,0:T(2,128)(2,1)S(1)}, u32[]{:S(2)}, u32[]{:S(2)}) collective-permute-start(bf16[2,6144]{1,0:T(2,128)(2,1)S(1)} %get-tuple-element.25), channel_id=1, source_target_pairs={{0,1},{1,2},{2,3},{3,4},{4,5},{5,6},{6,7},{8,9},{9,10},{10,11},{11... | collective-permute-start | bytes 73736 | tf_op jit(solution)/shard_map/ppermute | solution.py:22
  15.7 1.5 %collective-permute-done.left = bf16[2,6144]{1,0:T(2,128)(2,1)S(1)} collective-permute-done((bf16[2,6144]{1,0:T(2,128)(2,1)S(1)}, bf16[2,6144]{1,0:T(2,128)(2,1)S(1)}, u32[]{:S(2)}, u32[]{:S(2)}) %collective-permute-start) | collective-permute-done | bytes 24608 | tf_op jit(solution)/shard_map/ppermute | solution.py:22
  17.2 0.0 collective-permute-done.1.right
  17.2 3.3 %all-to-all-done.params = bf16[32,32,128]{2,1,0:T(8,128)(2,1)S(1)} async-done(((bf16[32,32,128]{2,1,0:T(8,128)(2,1)}), bf16[32,32,128]{2,1,0:T(8,128)(2,1)S(1)}, u32[]{:S(2)}, u32[]{:S(2)}) %all-to-all-start) | async-done | bytes 262176 | tf_op jit(solution)/shard_map/all_to_all | solution.py:641
  20.5 0.0 copy-done
  20.5 7.1 %ends.1 = (bf16[8,2,128,128]{3,2,1,0:T(8,128)(2,1)}, f32[2,3168,128]{2,1,0:T(8,128)}, f32[2,1040,128]{2,1,0:T(8,128)}, f32[2,1040,128]{2,1,0:T(8,128)}, f32[2,10...) custom-call(s32[1,8]{1,0:T(1,128)} %far_lengths.7, ...), custom_call_target="tpu_custom_call" | custom-call | tf_op jit(solution)/shard_map/ends/pallas_call | solution.py:685
  27.6 4.2 %all-to-all-start.1 = ((bf16[8,2,128,128]{3,2,1,0:T(8,128)(2,1)}), bf16[8,2,128,128]{3,2,1,0:T(8,128)(2,1)S(1)}, u32[]{:S(2)}, u32[]{:S(2)}) async-start(bf16[8,2,128,128]{3,2,1,0:T(8,128)(2,1)} %get-tuple-element.29), calls=%async_computation.1 | async-start | bytes 1048576 | tf_op jit(solution)/shard_map/all_to_all | solution.py:641
  31.8 9.8 %local.1 = (f32[2,1040,128]{2,1,0:T(8,128)}, f32[2,1040,128]{2,1,0:T(8,128)}, f32[2,136,128]{2,1,0:T(8,128)}) custom-call(s32[1,8]{1,0:T(1,128)} %far_lengths.7, f32[2,1040,128]{2,1,0:T(8,128)} %get-tuple-element.31.mixed_in, f32[2,1040,128]{2,1,0:T(8,128)} %get-tuple-element.32.gout_in, f32[2,264,128]{2,1,0:T(8,128)} %get-tuple-element.30.par_in), custom_call_target="tpu_custom_call" | custom-call | tf_op jit(solution)/shard_map/local/pallas_call | solution.py:685
  41.6 4.2 %all-to-all-done.1.arrived = bf16[8,2,128,128]{3,2,1,0:T(8,128)(2,1)S(1)} async-done(((bf16[8,2,128,128]{3,2,1,0:T(8,128)(2,1)}), bf16[8,2,128,128]{3,2,1,0:T(8,128)(2,1)S(1)}, u32[]{:S(2)}, u32[]{:S(2)}) %all-to-all-start.1) | async-done | bytes 524320 | tf_op jit(solution)/shard_map/all_to_all | solution.py:641
  45.7 6.9 %sums.1 = (f32[2,1040,128]{2,1,0:T(8,128)}, f32[2,1040,128]{2,1,0:T(8,128)}, bf16[8,192,128]{2,1,0:T(8,128)(2,1)}) custom-call(s32[1,8]{1,0:T(1,128)} %far_lengths.7, bf16[8,2,128,128]{3,2,1,0:T(8,128)(2,1)S(1)} %all-to-all-done.1.arrived, f32[2,264,128]{2,1,0:T(8,128)} %get-tuple-element.30.par_in, f32[2,136,128]{2,1,0:T(8,128)} %get-tuple-element.33.partial_in, ...), custom_call_target="tpu_custom_call" | custom-call | tf_op jit(solution)/shard_map/sums/pallas_call | solution.py:685
  52.6 3.5 %all-to-all-start.2 = ((bf16[8,192,128]{2,1,0:T(8,128)(2,1)}), bf16[8,192,128]{2,1,0:T(8,128)(2,1)S(1)}, u32[]{:S(2)}, u32[]{:S(2)}) async-start(bf16[8,192,128]{2,1,0:T(8,128)(2,1)} %get-tuple-element.42), calls=%async_computation.2 | async-start | bytes 786432 | tf_op jit(solution)/shard_map/all_to_all | solution.py:641
  56.1 5.1 %grads.1 = bf16[1,128,6144]{2,1,0:T(8,128)(2,1)} custom-call(s32[1,8]{1,0:T(1,128)} %far_lengths.7, f32[2,72,128]{2,1,0:T(8,128)} %get-tuple-element.28.tap_in, f32[2,1040,128]{2,1,0:T(8,128)} %get-tuple-element.40.conv_in, f32[2,1040,128]{2,1,0:T(8,128)} %get-tuple-element.41.adj_in, f32[2,1040,128]{2,1,0:T(8,128)} %get-tuple-element.36.up_in, ...), custom_call_target="tpu_custom_call" | custom-call | tf_op jit(solution)/shard_map/grads/pallas_call | solution.py:685
  61.2 5.3 %all-to-all-done.2.parts = bf16[8,192,128]{2,1,0:T(8,128)(2,1)S(1)} async-done(((bf16[8,192,128]{2,1,0:T(8,128)(2,1)}), bf16[8,192,128]{2,1,0:T(8,128)(2,1)S(1)}, u32[]{:S(2)}, u32[]{:S(2)}) %all-to-all-start.2) | async-done | bytes 393248 | tf_op jit(solution)/shard_map/all_to_all | solution.py:641
  66.5 0.1 share.1
  66.6 5.6 %all-gather = bf16[768,128]{1,0:T(8,128)(2,1)S(1)} all-gather(bf16[192,128]{1,0:T(8,128)(2,1)S(1)} %share.1), channel_id=2, replica_groups=mesh['dp'=4,'ctx'=8] {'dp'}, dimensions={0}, use_global_device_ids=true | all-gather | bytes 245760 | tf_op jit(solution)/shard_map/all_gather | solution.py:795
  72.2 0.7 emit.1
Async XLA Ops:
  0.6 19.8 %copy-start = (f32[3,6144]{1,0:T(4,128)S(1)}, f32[3,6144]{1,0:T(4,128)}, u32[]{:S(2)}) copy-start(f32[3,6144]{1,0:T(4,128)} %taps.1) | copy-start | bytes 221188
  2.5 18.0 %all-to-all-start = ((bf16[32,32,128]{2,1,0:T(8,128)(2,1)}), bf16[32,32,128]{2,1,0:T(8,128)(2,1)S(1)}, u32[]{:S(2)}, u32[]{:S(2)}) async-start(bf16[32,32,128]{2,1,0:T(8,128)(2,1)} %get-tuple-element.27), calls=%async_computation | async-start | bytes 524288 | tf_op jit(solution)/shard_map/all_to_all | solution.py:641
  9.8 7.4 %collective-permute-start.1 = (bf16[2,8192]{1,0:T(2,128)(2,1)S(1)}, bf16[2,8192]{1,0:T(2,128)(2,1)S(1)}, u32[]{:S(2)}, u32[]{:S(2)}) collective-permute-start(bf16[2,8192]{1,0:T(2,128)(2,1)S(1)} %get-tuple-element.26), channel_id=1, source_target_pairs={{1,0},{2,1},{3,2},{4,3},{5,4},{6,5},{7,6},{9,8},{10,9},{11,10},{12... | collective-permute-start | bytes 98312 | tf_op jit(solution)/shard_map/ppermute | solution.py:22
  11.1 6.1 %collective-permute-start = (bf16[2,6144]{1,0:T(2,128)(2,1)S(1)}, bf16[2,6144]{1,0:T(2,128)(2,1)S(1)}, u32[]{:S(2)}, u32[]{:S(2)}) collective-permute-start(bf16[2,6144]{1,0:T(2,128)(2,1)S(1)} %get-tuple-element.25), channel_id=1, source_target_pairs={{0,1},{1,2},{2,3},{3,4},{4,5},{5,6},{6,7},{8,9},{9,10},{10,11},{11... | collective-permute-start | bytes 73736 | tf_op jit(solution)/shard_map/ppermute | solution.py:22
  27.6 18.2 %all-to-all-start.1 = ((bf16[8,2,128,128]{3,2,1,0:T(8,128)(2,1)}), bf16[8,2,128,128]{3,2,1,0:T(8,128)(2,1)S(1)}, u32[]{:S(2)}, u32[]{:S(2)}) async-start(bf16[8,2,128,128]{3,2,1,0:T(8,128)(2,1)} %get-tuple-element.29), calls=%async_computation.1 | async-start | bytes 1048576 | tf_op jit(solution)/shard_map/all_to_all | solution.py:641
  52.6 13.9 %all-to-all-start.2 = ((bf16[8,192,128]{2,1,0:T(8,128)(2,1)}), bf16[8,192,128]{2,1,0:T(8,128)(2,1)S(1)}, u32[]{:S(2)}, u32[]{:S(2)}) async-start(bf16[8,192,128]{2,1,0:T(8,128)(2,1)} %get-tuple-element.42), calls=%async_computation.2 | async-start | bytes 786432 | tf_op jit(solution)/shard_map/all_to_all | solution.py:641

commit v11 on v10

--- a/solution.py
+++ b/solution.py
@@ -69,26 +69,16 @@
         )
     ]
     start_all(copies)
-    width = rates.shape[1]
-    members = lax.axis_size("dp")
-    poles = rates.shape[0] // members
-
-    def mine(ref, lanes):
-        value = ref[0:poles, lanes]
-        for member in range(1, members):
-            other = ref[member * poles : (member + 1) * poles, lanes]
-            value = jnp.where(lax.axis_index("dp") == member, other, value)
-        return value
-
+    poles, width = rates.shape
     per = tiles_of(width)
     slab[...] = jnp.zeros(slab.shape, F32)
     wait_all(copies[:3])
     for j in range(per):
         lanes = slice(j * LANES, min(width, (j + 1) * LANES))
-        rate, gain = mine(rates, lanes), gains[:, lanes]
+        rate, gain = rates[:, lanes], gains[:, lanes]
         slab[pl.ds(j, poles, stride=per), :] = rounded(rate)
         slab[pl.ds(poles * per + j, poles, stride=per), :] = rate - rounded(rate)
-        slab[pl.ds(2 * poles * per + j, poles, stride=per), :] = mine(coeffs, lanes)
+        slab[pl.ds(2 * poles * per + j, poles, stride=per), :] = coeffs[:, lanes]
         slab[pl.ds(3 * poles * per + j, 1), :] = rounded(gain)
         slab[pl.ds((3 * poles + 1) * per + j, 1), :] = gain - rounded(gain)
     packed = slab[...].astype(BF16)
@@ -106,30 +96,24 @@
 
 
 def spread_params(dst, par, slab, half, groups, poles):
-    members = lax.axis_size("dp")
-    pieces = par.shape[0] // members
-    width = par.shape[2]
-    share = poles // members
+    pieces, height, width = par.shape
     many = pieces // groups
+    base = half * many
     joined = LANES // width
-    per = SUB * joined // many
-    for member in range(members):
-        base = member * pieces + half * many
-        for k in range(many // joined):
-            parts = [par[base + k * joined + i].astype(F32) for i in range(joined)]
-            slab[...] = parts[0] if joined == 1 else jnp.concatenate(parts, axis=1)
-            for j in range(per):
-
-                def rows_of(piece, count):
-                    return slab[pl.ds(piece * per + j, count, stride=per), :]
-
-                first = member * share * SUB + k * per + j
-                rates = rows_of(0, share) + rows_of(share, share)
-                dst[pl.ds(first, share, stride=SUB), :] = rates
-                dst[pl.ds(poles * SUB + first, share, stride=SUB), :] = rows_of(2 * share, share)
-                if member == 0:
-                    gain = rows_of(3 * share, 1) + rows_of(3 * share + 1, 1)
-                    dst[pl.ds(2 * poles * SUB + k * per + j, 1), :] = gain
+    per = height // (3 * poles)
+    for k in range(many // joined):
+        parts = [par[base + k * joined + i].astype(F32) for i in range(joined)]
+        slab[...] = parts[0] if joined == 1 else jnp.concatenate(parts, axis=1)
+        for j in range(per):
+            to = k * per + j
+
+            def rows_of(piece, count=poles):
+                return slab[pl.ds(piece * per + j, count, stride=per), :]
+
+            dst[pl.ds(to, poles, stride=SUB), :] = rows_of(0) + rows_of(poles)
+            dst[pl.ds(poles * SUB + to, poles, stride=SUB), :] = rows_of(2 * poles)
+            gain = rows_of(3 * poles, 1) + rows_of(3 * poles + 1, 1)
+            dst[pl.ds(2 * poles * SUB + to, 1), :] = gain
 
 
 def segment_starts(lengths):
@@ -516,7 +500,7 @@
     width = groups * SUB
     same = 9 * width
     tap_sums = sums[0:same, :].astype(BF16)
-    columns = (payload.shape[1] - same) // 16 - 1
+    columns = (payload.shape[1] - same) // 16
     for e in range(count):
         payload[e, 0:same, :] = tap_sums
         first_row = same + (e * width) // count
@@ -524,7 +508,7 @@
             value = sums[pl.ds(first_row + j, 16, stride=width), :]
             payload[e, same + 16 * j : same + 16 * (j + 1), :] = value.astype(BF16)
         last_row = first_row + poles * width
-        payload[e, same + 16 * columns :, :] = sums[last_row : last_row + 16, :].astype(BF16)
+        payload[e, same + 16 * columns :, :] = sums[last_row : last_row + SUB, :].astype(BF16)
     each_group(
         groups,
         lambda half: wait_all(group_copies([conv, adj], [conv_out, adj_out], out_sems, half)),
@@ -616,7 +600,7 @@
     for k in range(3 * width):
         grad_taps[:, k * LANES : (k + 1) * LANES] = whole[pl.ds(k, 3, stride=3 * width), :]
     first = 9 * width
-    columns = (whole.shape[0] - first) // 16 - 1
+    columns = (whole.shape[0] - first) // 16
     last = first + 16 * columns
     if per_shard >= LANES:
         for j in range(columns):
@@ -692,8 +676,8 @@
             name=name,
         )(*ins)
 
-    block_rows = (3 * poles // lax.axis_size("dp") + 2) * tiles_of(per_shard)
-    block = (-(-block_rows // 16) * 16, min(per_shard, LANES))
+    block_rows = (3 * poles + 2) * tiles_of(per_shard)
+    block = (-(-block_rows // SUB) * SUB, min(per_shard, LANES))
     span = features.shape[2]
     params, edge, head = call(
         start_kernel,
@@ -701,7 +685,7 @@
         [log_rate, residues, skip_gain[None], features, upstream],
         [hbm] * 5,
         [
-            jax.ShapeDtypeStruct((total,) + block, BF16),
+            jax.ShapeDtypeStruct((ctx_count,) + block, BF16),
             jax.ShapeDtypeStruct((HALO, span), BF16),
             jax.ShapeDtypeStruct((HALO, span + channels), BF16),
         ],
@@ -717,7 +701,7 @@
             sems(6),
         ],
     )
-    params = swap(params, ("dp", "ctx"))
+    params = swap(params, "ctx")
     left = shifted(edge, "ctx", 1)
     right = shifted(head, "ctx", -1)
 
@@ -753,7 +737,7 @@
         + [scratch(1), keep, sems(), sems(groups, 3), sems(groups, 3)],
     )
     used = (10 + poles) * groups * SUB
-    sum_rows = 9 * groups * SUB + 16 * max(1, per_shard // LANES) + 16
+    sum_rows = 9 * groups * SUB + 16 * tiles_of(per_shard) + SUB
     conv, adj, sums = call(
         functools.partial(sums_kernel, rows, groups),
         "sums",

time: 73.5 us -> 71.4 us (0.971)
  waiting for transfers between devices: 14.2 us -> 9.57 us
  starting transfers between devices: 20.9 us -> 23.5 us
    all_to_all x3, waiting for transfers between devices: 12.7 us -> 8.06 us  [swap(): return lax.all_to_all(block, axes, split_axis=0, concat_axis=0, tiled=True)]
    all_to_all x3, starting transfers between devices: 15 us -> 17.7 us  [swap(): return lax.all_to_all(block, axes, split_axis=0, concat_axis=0, tiled=True)]
  transfers between devices with their start and end apart: 5 -> 5, of which waited for: 4 -> 4; matrix products, arithmetic and copies ran while one was open for 0% -> 0% of each run, Pallas kernels for 20% -> 21%
where the time goes in v11:
time: 71.4 us; the launch traced here: 70.8 us
  Pallas kernels  31.5 us (44%)
  starting transfers between devices  23.5 us (33%)
  waiting for transfers between devices  9.57 us (13%)
  blocking collectives  5.58 us (8%)
    pallas_call x7, Pallas kernels, call(): pl.pallas_call(kernel, out_shape=outs, in_specs=in_specs, out_specs=out_s...  31.5 us
    all_to_all x3, starting transfers between devices, swap(): return lax.all_to_all(block, axes, split_axis=0, concat_axis=0, tiled=True)  17.7 us
    all_to_all x3, waiting for transfers between devices, swap(): return lax.all_to_all(block, axes, split_axis=0, concat_axis=0, tiled=True)  8.06 us
    ppermute x2, starting transfers between devices, shifted(): return lax.ppermute(block, axis, route)  5.83 us
    all_gather x1, blocking collectives, per_device(): lax.all_gather(mine, 'dp')  5.58 us
    ppermute x2, waiting for transfers between devices, shifted(): return lax.ppermute(block, axis, route)  1.5 us
  transfers between devices with their start and end apart: 5, of which 4 were waited for; matrix products, arithmetic and copies ran while one was open for 0% of the time, Pallas kernels for 21%

profile of v11, /device:TPU:0, one launch (start us, length us, event | category | flops | bytes accessed | tf_op | source)
XLA Modules:
  0.0 70.8 jit_solution(5958345878119790549)
XLA Ops:
  0.6 0.0 copy-start
  0.6 1.8 %start.1 = (bf16[8,104,128]{2,1,0:T(8,128)(2,1)}, bf16[2,6144]{1,0:T(2,128)(2,1)S(1)}, bf16[2,8192]{1,0:T(2,128)(2,1)S(1)}) custom-call(f32[16,256]{1,0:T(8,128)} %log_rate.1, f32[16,256]{1,0:T(8,128)} %residues.1, f32[1,256]{1,0:T(1,128)} %bitcast.4, bf16[1,128,6144]{2,1,0:T(8,128)(2,1)} %features.3, bf16[1,128,2048]{2,1,0:T(8,128)(2,1)} %upstream.3), custom_call_target="tpu_custom_call" | custom-call | tf_op jit(solution)/shard_map/start/pallas_call | solution.py:669
  2.5 7.3 %all-to-all-start = ((bf16[8,104,128]{2,1,0:T(8,128)(2,1)}), bf16[8,104,128]{2,1,0:T(8,128)(2,1)S(1)}, u32[]{:S(2)}, u32[]{:S(2)}) async-start(bf16[8,104,128]{2,1,0:T(8,128)(2,1)} %get-tuple-element.27), calls=%async_computation | async-start | bytes 425984 | tf_op jit(solution)/shard_map/all_to_all | solution.py:625
  9.8 1.3 %collective-permute-start.1 = (bf16[2,8192]{1,0:T(2,128)(2,1)S(1)}, bf16[2,8192]{1,0:T(2,128)(2,1)S(1)}, u32[]{:S(2)}, u32[]{:S(2)}) collective-permute-start(bf16[2,8192]{1,0:T(2,128)(2,1)S(1)} %get-tuple-element.26), channel_id=1, source_target_pairs={{1,0},{2,1},{3,2},{4,3},{5,4},{6,5},{7,6},{9,8},{10,9},{11,10},{12... | collective-permute-start | bytes 98312 | tf_op jit(solution)/shard_map/ppermute | solution.py:22
  11.1 4.6 %collective-permute-start = (bf16[2,6144]{1,0:T(2,128)(2,1)S(1)}, bf16[2,6144]{1,0:T(2,128)(2,1)S(1)}, u32[]{:S(2)}, u32[]{:S(2)}) collective-permute-start(bf16[2,6144]{1,0:T(2,128)(2,1)S(1)} %get-tuple-element.25), channel_id=1, source_target_pairs={{0,1},{1,2},{2,3},{3,4},{4,5},{5,6},{6,7},{8,9},{9,10},{10,11},{11... | collective-permute-start | bytes 73736 | tf_op jit(solution)/shard_map/ppermute | solution.py:22
  15.6 1.5 %collective-permute-done.left = bf16[2,6144]{1,0:T(2,128)(2,1)S(1)} collective-permute-done((bf16[2,6144]{1,0:T(2,128)(2,1)S(1)}, bf16[2,6144]{1,0:T(2,128)(2,1)S(1)}, u32[]{:S(2)}, u32[]{:S(2)}) %collective-permute-start) | collective-permute-done | bytes 24608 | tf_op jit(solution)/shard_map/ppermute | solution.py:22
  17.1 0.0 collective-permute-done.1.right
  17.1 0.9 %all-to-all-done.params = bf16[8,104,128]{2,1,0:T(8,128)(2,1)S(1)} async-done(((bf16[8,104,128]{2,1,0:T(8,128)(2,1)}), bf16[8,104,128]{2,1,0:T(8,128)(2,1)S(1)}, u32[]{:S(2)}, u32[]{:S(2)}) %all-to-all-start) | async-done | bytes 213024 | tf_op jit(solution)/shard_map/all_to_all | solution.py:625
  18.0 0.0 copy-done
  18.0 7.1 %ends.1 = (bf16[8,2,128,128]{3,2,1,0:T(8,128)(2,1)}, f32[2,3168,128]{2,1,0:T(8,128)}, f32[2,1040,128]{2,1,0:T(8,128)}, f32[2,1040,128]{2,1,0:T(8,128)}, f32[2,10...) custom-call(s32[1,8]{1,0:T(1,128)} %far_lengths.7, ...), custom_call_target="tpu_custom_call" | custom-call | tf_op jit(solution)/shard_map/ends/pallas_call | solution.py:669
  25.1 6.9 %all-to-all-start.1 = ((bf16[8,2,128,128]{3,2,1,0:T(8,128)(2,1)}), bf16[8,2,128,128]{3,2,1,0:T(8,128)(2,1)S(1)}, u32[]{:S(2)}, u32[]{:S(2)}) async-start(bf16[8,2,128,128]{3,2,1,0:T(8,128)(2,1)} %get-tuple-element.29), calls=%async_computation.1 | async-start | bytes 1048576 | tf_op jit(solution)/shard_map/all_to_all | solution.py:625
  32.0 9.8 %local.1 = (f32[2,1040,128]{2,1,0:T(8,128)}, f32[2,1040,128]{2,1,0:T(8,128)}, f32[2,136,128]{2,1,0:T(8,128)}) custom-call(s32[1,8]{1,0:T(1,128)} %far_lengths.7, f32[2,1040,128]{2,1,0:T(8,128)} %get-tuple-element.31.mixed_in, f32[2,1040,128]{2,1,0:T(8,128)} %get-tuple-element.32.gout_in, f32[2,264,128]{2,1,0:T(8,128)} %get-tuple-element.30.par_in), custom_call_target="tpu_custom_call" | custom-call | tf_op jit(solution)/shard_map/local/pallas_call | solution.py:669
  41.8 2.7 %all-to-all-done.1.arrived = bf16[8,2,128,128]{3,2,1,0:T(8,128)(2,1)S(1)} async-done(((bf16[8,2,128,128]{3,2,1,0:T(8,128)(2,1)}), bf16[8,2,128,128]{3,2,1,0:T(8,128)(2,1)S(1)}, u32[]{:S(2)}, u32[]{:S(2)}) %all-to-all-start.1) | async-done | bytes 524320 | tf_op jit(solution)/shard_map/all_to_all | solution.py:625
  44.5 6.9 %sums.1 = (f32[2,1040,128]{2,1,0:T(8,128)}, f32[2,1040,128]{2,1,0:T(8,128)}, bf16[8,184,128]{2,1,0:T(8,128)(2,1)}) custom-call(s32[1,8]{1,0:T(1,128)} %far_lengths.7, bf16[8,2,128,128]{3,2,1,0:T(8,128)(2,1)S(1)} %all-to-all-done.1.arrived, f32[2,264,128]{2,1,0:T(8,128)} %get-tuple-element.30.par_in, f32[2,136,128]{2,1,0:T(8,128)} %get-tuple-element.33.partial_in, ...), custom_call_target="tpu_custom_call" | custom-call | tf_op jit(solution)/shard_map/sums/pallas_call | solution.py:669
  51.4 3.5 %all-to-all-start.2 = ((bf16[8,184,128]{2,1,0:T(8,128)(2,1)}), bf16[8,184,128]{2,1,0:T(8,128)(2,1)S(1)}, u32[]{:S(2)}, u32[]{:S(2)}) async-start(bf16[8,184,128]{2,1,0:T(8,128)(2,1)} %get-tuple-element.42), calls=%async_computation.2 | async-start | bytes 753664 | tf_op jit(solution)/shard_map/all_to_all | solution.py:625
  54.9 5.1 %grads.1 = bf16[1,128,6144]{2,1,0:T(8,128)(2,1)} custom-call(s32[1,8]{1,0:T(1,128)} %far_lengths.7, f32[2,72,128]{2,1,0:T(8,128)} %get-tuple-element.28.tap_in, f32[2,1040,128]{2,1,0:T(8,128)} %get-tuple-element.40.conv_in, f32[2,1040,128]{2,1,0:T(8,128)} %get-tuple-element.41.adj_in, f32[2,1040,128]{2,1,0:T(8,128)} %get-tuple-element.36.up_in, ...), custom_call_target="tpu_custom_call" | custom-call | tf_op jit(solution)/shard_map/grads/pallas_call | solution.py:669
  60.0 4.5 %all-to-all-done.2.parts = bf16[8,184,128]{2,1,0:T(8,128)(2,1)S(1)} async-done(((bf16[8,184,128]{2,1,0:T(8,128)(2,1)}), bf16[8,184,128]{2,1,0:T(8,128)(2,1)S(1)}, u32[]{:S(2)}, u32[]{:S(2)}) %all-to-all-start.2) | async-done | bytes 376864 | tf_op jit(solution)/shard_map/all_to_all | solution.py:625
  64.5 0.1 share.1
  64.5 5.6 %all-gather = bf16[736,128]{1,0:T(8,128)(2,1)S(1)} all-gather(bf16[184,128]{1,0:T(8,128)(2,1)S(1)} %share.1), channel_id=2, replica_groups=mesh['dp'=4,'ctx'=8] {'dp'}, dimensions={0}, use_global_device_ids=true | all-gather | bytes 235520 | tf_op jit(solution)/shard_map/all_gather | solution.py:779
  70.1 0.7 %emit.1 = (f32[3,6144]{1,0:T(4,128)}, f32[16,256]{1,0:T(8,128)}, f32[1,256]{1,0:T(1,128)}) custom-call(bf16[4,184,128]{2,1,0:T(8,128)(2,1)S(1)} %bitcast.3), custom_call_target="tpu_custom_call" | custom-call | tf_op jit(solution)/shard_map/emit/pallas_call | solution.py:669
Async XLA Ops:
  0.6 17.4 %copy-start = (f32[3,6144]{1,0:T(4,128)S(1)}, f32[3,6144]{1,0:T(4,128)}, u32[]{:S(2)}) copy-start(f32[3,6144]{1,0:T(4,128)} %taps.1) | copy-start | bytes 221188
  2.5 15.5 %all-to-all-start = ((bf16[8,104,128]{2,1,0:T(8,128)(2,1)}), bf16[8,104,128]{2,1,0:T(8,128)(2,1)S(1)}, u32[]{:S(2)}, u32[]{:S(2)}) async-start(bf16[8,104,128]{2,1,0:T(8,128)(2,1)} %get-tuple-element.27), calls=%async_computation | async-start | bytes 425984 | tf_op jit(solution)/shard_map/all_to_all | solution.py:625
  9.8 7.4 %collective-permute-start.1 = (bf16[2,8192]{1,0:T(2,128)(2,1)S(1)}, bf16[2,8192]{1,0:T(2,128)(2,1)S(1)}, u32[]{:S(2)}, u32[]{:S(2)}) collective-permute-start(bf16[2,8192]{1,0:T(2,128)(2,1)S(1)} %get-tuple-element.26), channel_id=1, source_target_pairs={{1,0},{2,1},{3,2},{4,3},{5,4},{6,5},{7,6},{9,8},{10,9},{11,10},{12... | collective-permute-start | bytes 98312 | tf_op jit(solution)/shard_map/ppermute | solution.py:22
  11.1 6.1 %collective-permute-start = (bf16[2,6144]{1,0:T(2,128)(2,1)S(1)}, bf16[2,6144]{1,0:T(2,128)(2,1)S(1)}, u32[]{:S(2)}, u32[]{:S(2)}) collective-permute-start(bf16[2,6144]{1,0:T(2,128)(2,1)S(1)} %get-tuple-element.25), channel_id=1, source_target_pairs={{0,1},{1,2},{2,3},{3,4},{4,5},{5,6},{6,7},{8,9},{9,10},{10,11},{11... | collective-permute-start | bytes 73736 | tf_op jit(solution)/shard_map/ppermute | solution.py:22
  25.1 19.4 %all-to-all-start.1 = ((bf16[8,2,128,128]{3,2,1,0:T(8,128)(2,1)}), bf16[8,2,128,128]{3,2,1,0:T(8,128)(2,1)S(1)}, u32[]{:S(2)}, u32[]{:S(2)}) async-start(bf16[8,2,128,128]{3,2,1,0:T(8,128)(2,1)} %get-tuple-element.29), calls=%async_computation.1 | async-start | bytes 1048576 | tf_op jit(solution)/shard_map/all_to_all | solution.py:625
  51.4 13.1 %all-to-all-start.2 = ((bf16[8,184,128]{2,1,0:T(8,128)(2,1)}), bf16[8,184,128]{2,1,0:T(8,128)(2,1)S(1)}, u32[]{:S(2)}, u32[]{:S(2)}) async-start(bf16[8,184,128]{2,1,0:T(8,128)(2,1)} %get-tuple-element.42), calls=%async_computation.2 | async-start | bytes 753664 | tf_op jit(solution)/shard_map/all_to_all | solution.py:625

commit v12 on v11

--- a/solution.py
+++ b/solution.py
@@ -192,16 +192,12 @@
         copy.wait()
 
 
-def ends_kernel(
-    rows, groups, far_lengths, features, upstream, left, right, taps, params,
-    payload, feat_out, up_out, mixed_out, gout_out, par_out, tap_out, key_out, val_out,
-    lengths, raw, raw_up, feat, up, mixed, gout, par, tap, key_scr, val_scr, stack, slab, zero_scr, keep,
+def features_kernel(
+    rows, groups, far_lengths, features, upstream, left, right, taps,
+    mixed, gout, feat_out, up_out, mixed_out, gout_out, tap_out, key_out, val_out,
+    lengths, raw, raw_up, feat, up, tap, key_scr, val_scr, keep,
     length_sem, in_sems, out_sems,
 ):
-    me = lax.axis_index("ctx")
-    base = me * rows
-    count = payload.shape[0]
-    poles = (par.shape[1] // SUB - 1) // 2
     extended = rows + HALO
     padded = rows + 2 * HALO
     get_lengths = pltpu.make_async_copy(far_lengths, lengths, length_sem)
@@ -219,15 +215,12 @@
             for third in range(3)
         ] + [pltpu.make_async_copy(upstream.at[0, :, lanes[0]], raw_up.at[half], in_sems.at[half, 3])]
 
-    near = [feat, up, tap, par, mixed, gout, key_scr, val_scr]
-    far = [feat_out, up_out, tap_out, par_out, mixed_out, gout_out, key_out, val_out]
+    near = [feat, up, tap, mixed, gout, key_scr, val_scr]
+    far = [feat_out, up_out, tap_out, mixed_out, gout_out, key_out, val_out]
 
     each_group(groups, lambda half: start_all(arriving(half)))
-    zero_scr[...] = jnp.zeros((SUB, LANES), F32)
-    zeros = [zero_scr[...]] * poles
 
     def prepare(half):
-        spread_params(par.at[half], params, slab, half, groups, poles)
         for third in range(3):
             column = (third * groups + half) * GROUP
             spread(feat.at[half], third * padded, left, column, HALO)
@@ -237,13 +230,7 @@
 
     each_group(groups, prepare)
     get_lengths.wait()
-    starts = segment_starts(lengths)
-    fill_keep(keep, starts, base, rows)
-    low, high = jnp.int32(0), jnp.int32(extended)
-    for start in starts:
-        at = start - base
-        low = jnp.where(at < rows, jnp.maximum(low, at), low)
-        high = jnp.where(at > HALO, jnp.minimum(high, at), high)
+    fill_keep(keep, segment_starts(lengths), lax.axis_index("ctx") * rows, rows)
 
     def group(half):
         incoming = arriving(half)
@@ -254,7 +241,7 @@
             spread_rows(feat_h, third * padded + HALO, raw.at[half, third], rows)
         incoming[3].wait()
         spread_rows(up_h, 0, raw_up.at[half], rows)
-        start_all(outgoing[:4])
+        start_all(outgoing[:3])
         taps_h = [[vec(tap.at[half], third * 3 + j) for j in range(3)] for third in range(3)]
 
         def product(p, carry):
@@ -271,7 +258,40 @@
             return carry
 
         lax.fori_loop(0, extended, product, 0, unroll=unroll_of(extended))
-        start_all(outgoing[4:])
+        start_all(outgoing[3:])
+
+    each_group(groups, group)
+    each_group(groups, lambda half: wait_all(group_copies(near, far, out_sems, half)))
+
+
+def ends_kernel(
+    rows, groups, far_lengths, params, mixed, gout, payload, par_out,
+    lengths, par, stack, slab, zero_scr, length_sem, out_sems,
+):
+    me = lax.axis_index("ctx")
+    base = me * rows
+    count = payload.shape[0]
+    poles = (par.shape[1] // SUB - 1) // 2
+    extended = rows + HALO
+    get_lengths = pltpu.make_async_copy(far_lengths, lengths, length_sem)
+    get_lengths.start()
+    zero_scr[...] = jnp.zeros((SUB, LANES), F32)
+    zeros = [zero_scr[...]] * poles
+
+    def prepare(half):
+        spread_params(par.at[half], params, slab, half, groups, poles)
+        start_all(group_copies([par], [par_out], out_sems, half))
+
+    each_group(groups, prepare)
+    get_lengths.wait()
+    low, high = jnp.int32(0), jnp.int32(extended)
+    for start in segment_starts(lengths):
+        at = start - base
+        low = jnp.where(at < rows, jnp.maximum(low, at), low)
+        high = jnp.where(at > HALO, jnp.minimum(high, at), high)
+
+    def group(half):
+        mixed_h, gout_h = mixed.at[half], gout.at[half]
         decay = [jnp.exp(-jnp.exp(vec(par.at[half], m))) for m in range(poles)]
 
         def sweep(i, carry):
@@ -292,7 +312,7 @@
             payload[e, half] = stack[jnp.where(e >= me, 0, 1)]
 
     each_group(groups, group)
-    each_group(groups, lambda half: wait_all(group_copies(near, far, out_sems, half)))
+    each_group(groups, lambda half: wait_all(group_copies([par], [par_out], out_sems, half)))
 
 
 def local_kernel(
@@ -656,7 +676,7 @@
     keep = pltpu.SMEM((rows + 8,), F32)
     small = pltpu.SMEM(lengths.shape, jnp.int32)
 
-    def call(kernel, name, ins, in_specs, outs, out_specs, scratch_shapes=()):
+    def call(kernel, name, ins, in_specs, outs, out_specs, scratch_shapes=(), cost=None):
         ins = [
             pltpu.with_memory_space_constraint(x, pltpu.HBM) if spec is hbm else x
             for x, spec in zip(ins, in_specs)
@@ -673,6 +693,7 @@
             out_specs=out_specs,
             scratch_shapes=list(scratch_shapes),
             compiler_params=limits,
+            cost_estimate=cost,
             name=name,
         )(*ins)
 
@@ -705,24 +726,42 @@
     left = shifted(edge, "ctx", 1)
     right = shifted(head, "ctx", -1)
 
-    payload, feat, up, mixed, gout, par, tap, key, val = call(
-        functools.partial(ends_kernel, rows, groups),
-        "ends",
-        [lengths, features, upstream, left, right, conv_taps, params],
-        [hbm] * 3 + [vmem] * 4,
-        [jax.ShapeDtypeStruct((ctx_count, groups, state_rows, LANES), BF16)]
-        + [tall(height) for height in [3 * padded] + [extended] * 3 + [2 * poles + 1, 9]]
+    near_mixed, near_gout, feat, up, mixed, gout, tap, key, val = call(
+        functools.partial(features_kernel, rows, groups),
+        "features",
+        [lengths, features, upstream, left, right, conv_taps],
+        [hbm] * 3 + [vmem] * 3,
+        [tall(extended)] * 2
+        + [tall(3 * padded)]
+        + [tall(extended)] * 3
+        + [tall(9)]
         + [tall(extended)] * 2,
-        [vmem] + [hbm] * 8,
+        [vmem] * 2 + [hbm] * 7,
         [
             small,
             pltpu.VMEM((groups, 3, rows, GROUP), BF16),
             pltpu.VMEM((groups, rows, GROUP), BF16),
         ]
-        + near(3 * padded, extended, extended, extended, 2 * poles + 1, 9, extended, extended)
+        + near(3 * padded, extended, 9, extended, extended)
+        + [keep, sems(), sems(groups, 4), sems(groups, 7)],
+        pl.CostEstimate(flops=5 * 10**9, bytes_accessed=4 * 10**7, transcendentals=0),
+    )
+    state_rows = poles * SUB
+    payload, par = call(
+        functools.partial(ends_kernel, rows, groups),
+        "ends",
+        [lengths, params, near_mixed, near_gout],
+        [hbm] + [vmem] * 3,
+        [
+            jax.ShapeDtypeStruct((ctx_count, groups, state_rows, LANES), BF16),
+            tall(2 * poles + 1),
+        ],
+        [vmem, hbm],
+        [small]
+        + near(2 * poles + 1)
         + [pltpu.VMEM((2, state_rows, LANES), BF16)]
-        + [pltpu.VMEM((block[0], LANES), F32), scratch(1), keep]
-        + [sems(), sems(groups, 4), sems(groups, 8)],
+        + [pltpu.VMEM((block[0], LANES), F32), scratch(1)]
+        + [sems(), sems(groups, 1)],
     )
     arrived = swap(payload, "ctx")
     conv, adj, partial = call(

time: 71.4 us -> 71.8 us (level)
  starting transfers between devices: 23.5 us -> 20.2 us
  Pallas kernels: 31.5 us -> 33.7 us
  waiting for transfers between devices: 9.57 us -> 10.5 us
    all_to_all x3, starting transfers between devices: 17.7 us -> 13.4 us  [swap(): return lax.all_to_all(block, axes, split_axis=0, concat_axis=0, tiled=True)]
    all_to_all x3, waiting for transfers between devices: 8.06 us -> 10.5 us  [swap(): return lax.all_to_all(block, axes, split_axis=0, concat_axis=0, tiled=True)]
    pallas_call x7 -> x8, Pallas kernels: 31.5 us -> 33.7 us  [call(): pl.pallas_call(kernel, out_shape=outs, in_specs=in_specs, out_specs=out_s...]
    ppermute x2, waiting for transfers between devices: 1.5 us -> 0.01 us  [shifted(): return lax.ppermute(block, axis, route)]
    ppermute x2, starting transfers between devices: 5.83 us -> 6.79 us  [shifted(): return lax.ppermute(block, axis, route)]
  transfers between devices with their start and end apart: 5 -> 5, of which waited for: 4 -> 3; matrix products, arithmetic and copies ran while one was open for 0% -> 0% of each run, Pallas kernels for 21% -> 28%
where the time goes in v12:
time: 71.8 us; the launch traced here: 70.8 us
  Pallas kernels  33.7 us (47%)
  starting transfers between devices  20.2 us (28%)
  waiting for transfers between devices  10.5 us (15%)
  blocking collectives  5.58 us (8%)
  between operations  0.74 us (1%)
    pallas_call x8, Pallas kernels, call(): pl.pallas_call(kernel, out_shape=outs, in_specs=in_specs, out_specs=out_s...  33.7 us
    all_to_all x3, starting transfers between devices, swap(): return lax.all_to_all(block, axes, split_axis=0, concat_axis=0, tiled=True)  13.4 us
    all_to_all x3, waiting for transfers between devices, swap(): return lax.all_to_all(block, axes, split_axis=0, concat_axis=0, tiled=True)  10.5 us
    ppermute x2, starting transfers between devices, shifted(): return lax.ppermute(block, axis, route)  6.79 us
    all_gather x1, blocking collectives, per_device(): lax.all_gather(mine, 'dp')  5.58 us
  transfers between devices with their start and end apart: 5, of which 3 were waited for; matrix products, arithmetic and copies ran while one was open for 0% of the time, Pallas kernels for 28%

profile of v12, /device:TPU:0, one launch (start us, length us, event | category | flops | bytes accessed | tf_op | source)
XLA Modules:
  0.0 70.8 jit_solution(12361804772027516228)
XLA Ops:
  0.6 0.0 copy-start
  0.6 1.8 %start.1 = (bf16[8,104,128]{2,1,0:T(8,128)(2,1)}, bf16[2,6144]{1,0:T(2,128)(2,1)S(1)}, bf16[2,8192]{1,0:T(2,128)(2,1)S(1)}) custom-call(f32[16,256]{1,0:T(8,128)} %log_rate.1, f32[16,256]{1,0:T(8,128)} %residues.1, f32[1,256]{1,0:T(1,128)} %bitcast.4, bf16[1,128,6144]{2,1,0:T(8,128)(2,1)} %features.5, bf16[1,128,2048]{2,1,0:T(8,128)(2,1)} %upstream.3), custom_call_target="tpu_custom_call" | custom-call | tf_op jit(solution)/shard_map/start/pallas_call | solution.py:689
  2.5 1.3 %collective-permute-start.1 = (bf16[2,8192]{1,0:T(2,128)(2,1)S(1)}, bf16[2,8192]{1,0:T(2,128)(2,1)S(1)}, u32[]{:S(2)}, u32[]{:S(2)}) collective-permute-start(bf16[2,8192]{1,0:T(2,128)(2,1)S(1)} %get-tuple-element.28), channel_id=1, source_target_pairs={{1,0},{2,1},{3,2},{4,3},{5,4},{6,5},{7,6},{9,8},{10,9},{11,10},{12... | collective-permute-start | bytes 98312 | tf_op jit(solution)/shard_map/ppermute | solution.py:22
  3.8 5.5 %collective-permute-start = (bf16[2,6144]{1,0:T(2,128)(2,1)S(1)}, bf16[2,6144]{1,0:T(2,128)(2,1)S(1)}, u32[]{:S(2)}, u32[]{:S(2)}) collective-permute-start(bf16[2,6144]{1,0:T(2,128)(2,1)S(1)} %get-tuple-element.27), channel_id=1, source_target_pairs={{0,1},{1,2},{2,3},{3,4},{4,5},{5,6},{6,7},{8,9},{9,10},{10,11},{11... | collective-permute-start | bytes 73736 | tf_op jit(solution)/shard_map/ppermute | solution.py:22
  9.3 6.2 %all-to-all-start = ((bf16[8,104,128]{2,1,0:T(8,128)(2,1)}), bf16[8,104,128]{2,1,0:T(8,128)(2,1)S(1)}, u32[]{:S(2)}, u32[]{:S(2)}) async-start(bf16[8,104,128]{2,1,0:T(8,128)(2,1)} %get-tuple-element.30), calls=%async_computation | async-start | bytes 425984 | tf_op jit(solution)/shard_map/all_to_all | solution.py:645
  15.5 0.0 collective-permute-done.left
  15.5 0.0 collective-permute-done.1.right
  15.5 0.0 copy-done
  15.5 5.1 %features.4 = (f32[2,1040,128]{2,1,0:T(8,128)S(1)}, f32[2,1040,128]{2,1,0:T(8,128)S(1)}, f32[2,3168,128]{2,1,0:T(8,128)}, f32[2,1040,128]{2,1,0:T(8,128)}, f32[2...) custom-call(s32[1,8]{1,0:T(1,128)} %far_lengths.9, ...), custom_call_target="tpu_custom_call" | custom-call | flops 5000000000 | bytes 40000000 | tf_op jit(solution)/shard_map/features/pallas_call | solution.py:689
  20.6 2.8 %all-to-all-done.params = bf16[8,104,128]{2,1,0:T(8,128)(2,1)S(1)} async-done(((bf16[8,104,128]{2,1,0:T(8,128)(2,1)}), bf16[8,104,128]{2,1,0:T(8,128)(2,1)S(1)}, u32[]{:S(2)}, u32[]{:S(2)}) %all-to-all-start) | async-done | bytes 213024 | tf_op jit(solution)/shard_map/all_to_all | solution.py:645
  23.4 4.3 %ends.1 = (bf16[8,2,128,128]{3,2,1,0:T(8,128)(2,1)}, f32[2,264,128]{2,1,0:T(8,128)}) custom-call(s32[1,8]{1,0:T(1,128)} %far_lengths.9, bf16[8,104,128]{2,1,0:T(8,128)(2,1)S(1)} %all-to-all-done.params, f32[2,1040,128]{2,1,0:T(8,128)S(1)} %get-tuple-element.31.mixed, f32[2,1040,128]{2,1,0:T(8,128)S(1)} %get-tuple-element.32.gout), custom_call_target="tpu_custom_call" | custom-call | tf_op jit(solution)/shard_map/ends/pallas_call | solution.py:689
  27.7 3.5 %all-to-all-start.1 = ((bf16[8,2,128,128]{3,2,1,0:T(8,128)(2,1)}), bf16[8,2,128,128]{3,2,1,0:T(8,128)(2,1)S(1)}, u32[]{:S(2)}, u32[]{:S(2)}) async-start(bf16[8,2,128,128]{3,2,1,0:T(8,128)(2,1)} %get-tuple-element.33), calls=%async_computation.1 | async-start | bytes 1048576 | tf_op jit(solution)/shard_map/all_to_all | solution.py:645
  31.2 9.8 %local.1 = (f32[2,1040,128]{2,1,0:T(8,128)}, f32[2,1040,128]{2,1,0:T(8,128)}, f32[2,136,128]{2,1,0:T(8,128)}) custom-call(s32[1,8]{1,0:T(1,128)} %far_lengths.9, f32[2,1040,128]{2,1,0:T(8,128)} %get-tuple-element.35.mixed_in, f32[2,1040,128]{2,1,0:T(8,128)} %get-tuple-element.36.gout_in, f32[2,264,128]{2,1,0:T(8,128)} %get-tuple-element.34.par_in), custom_call_target="tpu_custom_call" | custom-call | tf_op jit(solution)/shard_map/local/pallas_call | solution.py:689
  41.0 3.3 %all-to-all-done.1.arrived = bf16[8,2,128,128]{3,2,1,0:T(8,128)(2,1)S(1)} async-done(((bf16[8,2,128,128]{3,2,1,0:T(8,128)(2,1)}), bf16[8,2,128,128]{3,2,1,0:T(8,128)(2,1)S(1)}, u32[]{:S(2)}, u32[]{:S(2)}) %all-to-all-start.1) | async-done | bytes 524320 | tf_op jit(solution)/shard_map/all_to_all | solution.py:645
  44.3 6.9 %sums.1 = (f32[2,1040,128]{2,1,0:T(8,128)}, f32[2,1040,128]{2,1,0:T(8,128)}, bf16[8,184,128]{2,1,0:T(8,128)(2,1)}) custom-call(s32[1,8]{1,0:T(1,128)} %far_lengths.9, bf16[8,2,128,128]{3,2,1,0:T(8,128)(2,1)S(1)} %all-to-all-done.1.arrived, f32[2,264,128]{2,1,0:T(8,128)} %get-tuple-element.34.par_in, f32[2,136,128]{2,1,0:T(8,128)} %get-tuple-element.37.partial_in, ...), custom_call_target="tpu_custom_call" | custom-call | tf_op jit(solution)/shard_map/sums/pallas_call | solution.py:689
  51.2 3.7 %all-to-all-start.2 = ((bf16[8,184,128]{2,1,0:T(8,128)(2,1)}), bf16[8,184,128]{2,1,0:T(8,128)(2,1)S(1)}, u32[]{:S(2)}, u32[]{:S(2)}) async-start(bf16[8,184,128]{2,1,0:T(8,128)(2,1)} %get-tuple-element.46), calls=%async_computation.2 | async-start | bytes 753664 | tf_op jit(solution)/shard_map/all_to_all | solution.py:645
  54.9 5.1 %grads.1 = bf16[1,128,6144]{2,1,0:T(8,128)(2,1)} custom-call(s32[1,8]{1,0:T(1,128)} %far_lengths.9, f32[2,72,128]{2,1,0:T(8,128)} %get-tuple-element.29.tap_in, f32[2,1040,128]{2,1,0:T(8,128)} %get-tuple-element.44.conv_in, f32[2,1040,128]{2,1,0:T(8,128)} %get-tuple-element.45.adj_in, f32[2,1040,128]{2,1,0:T(8,128)} %get-tuple-element.40.up_in, ...), custom_call_target="tpu_custom_call" | custom-call | tf_op jit(solution)/shard_map/grads/pallas_call | solution.py:689
  60.0 4.4 %all-to-all-done.2.parts = bf16[8,184,128]{2,1,0:T(8,128)(2,1)S(1)} async-done(((bf16[8,184,128]{2,1,0:T(8,128)(2,1)}), bf16[8,184,128]{2,1,0:T(8,128)(2,1)S(1)}, u32[]{:S(2)}, u32[]{:S(2)}) %all-to-all-start.2) | async-done | bytes 376864 | tf_op jit(solution)/shard_map/all_to_all | solution.py:645
  64.4 0.1 share.1
  64.5 5.6 %all-gather = bf16[736,128]{1,0:T(8,128)(2,1)S(1)} all-gather(bf16[184,128]{1,0:T(8,128)(2,1)S(1)} %share.1), channel_id=2, replica_groups=mesh['dp'=4,'ctx'=8] {'dp'}, dimensions={0}, use_global_device_ids=true | all-gather | bytes 235520 | tf_op jit(solution)/shard_map/all_gather | solution.py:818
  70.1 0.7 %emit.1 = (f32[3,6144]{1,0:T(4,128)}, f32[16,256]{1,0:T(8,128)}, f32[1,256]{1,0:T(1,128)}) custom-call(bf16[4,184,128]{2,1,0:T(8,128)(2,1)S(1)} %bitcast.3), custom_call_target="tpu_custom_call" | custom-call | tf_op jit(solution)/shard_map/emit/pallas_call | solution.py:689
Async XLA Ops:
  0.6 14.9 %copy-start = (f32[3,6144]{1,0:T(4,128)S(1)}, f32[3,6144]{1,0:T(4,128)}, u32[]{:S(2)}) copy-start(f32[3,6144]{1,0:T(4,128)} %taps.1) | copy-start | bytes 221188
  2.5 13.0 %collective-permute-start.1 = (bf16[2,8192]{1,0:T(2,128)(2,1)S(1)}, bf16[2,8192]{1,0:T(2,128)(2,1)S(1)}, u32[]{:S(2)}, u32[]{:S(2)}) collective-permute-start(bf16[2,8192]{1,0:T(2,128)(2,1)S(1)} %get-tuple-element.28), channel_id=1, source_target_pairs={{1,0},{2,1},{3,2},{4,3},{5,4},{6,5},{7,6},{9,8},{10,9},{11,10},{12... | collective-permute-start | bytes 98312 | tf_op jit(solution)/shard_map/ppermute | solution.py:22
  3.8 11.7 %collective-permute-start = (bf16[2,6144]{1,0:T(2,128)(2,1)S(1)}, bf16[2,6144]{1,0:T(2,128)(2,1)S(1)}, u32[]{:S(2)}, u32[]{:S(2)}) collective-permute-start(bf16[2,6144]{1,0:T(2,128)(2,1)S(1)} %get-tuple-element.27), channel_id=1, source_target_pairs={{0,1},{1,2},{2,3},{3,4},{4,5},{5,6},{6,7},{8,9},{9,10},{10,11},{11... | collective-permute-start | bytes 73736 | tf_op jit(solution)/shard_map/ppermute | solution.py:22
  9.3 14.1 %all-to-all-start = ((bf16[8,104,128]{2,1,0:T(8,128)(2,1)}), bf16[8,104,128]{2,1,0:T(8,128)(2,1)S(1)}, u32[]{:S(2)}, u32[]{:S(2)}) async-start(bf16[8,104,128]{2,1,0:T(8,128)(2,1)} %get-tuple-element.30), calls=%async_computation | async-start | bytes 425984 | tf_op jit(solution)/shard_map/all_to_all | solution.py:645
  27.7 16.6 %all-to-all-start.1 = ((bf16[8,2,128,128]{3,2,1,0:T(8,128)(2,1)}), bf16[8,2,128,128]{3,2,1,0:T(8,128)(2,1)S(1)}, u32[]{:S(2)}, u32[]{:S(2)}) async-start(bf16[8,2,128,128]{3,2,1,0:T(8,128)(2,1)} %get-tuple-element.33), calls=%async_computation.1 | async-start | bytes 1048576 | tf_op jit(solution)/shard_map/all_to_all | solution.py:645
  51.2 13.3 %all-to-all-start.2 = ((bf16[8,184,128]{2,1,0:T(8,128)(2,1)}), bf16[8,184,128]{2,1,0:T(8,128)(2,1)S(1)}, u32[]{:S(2)}, u32[]{:S(2)}) async-start(bf16[8,184,128]{2,1,0:T(8,128)(2,1)} %get-tuple-element.46), calls=%async_computation.2 | async-start | bytes 753664 | tf_op jit(solution)/shard_map/all_to_all | solution.py:645

commit v13 on v12

--- a/solution.py
+++ b/solution.py
@@ -194,8 +194,8 @@
 
 def features_kernel(
     rows, groups, far_lengths, features, upstream, left, right, taps,
-    mixed, gout, feat_out, up_out, mixed_out, gout_out, tap_out, key_out, val_out,
-    lengths, raw, raw_up, feat, up, tap, key_scr, val_scr, keep,
+    last_mixed, first_gout, feat_out, up_out, mixed_out, gout_out, tap_out, key_out, val_out,
+    lengths, raw, raw_up, feat, up, mixed, gout, tap, key_scr, val_scr, keep,
     length_sem, in_sems, out_sems,
 ):
     extended = rows + HALO
@@ -230,7 +230,14 @@
 
     each_group(groups, prepare)
     get_lengths.wait()
-    fill_keep(keep, segment_starts(lengths), lax.axis_index("ctx") * rows, rows)
+    base = lax.axis_index("ctx") * rows
+    starts = segment_starts(lengths)
+    fill_keep(keep, starts, base, rows)
+    low, high = jnp.int32(0), jnp.int32(extended)
+    for start in starts:
+        at = start - base
+        low = jnp.where(at < rows, jnp.maximum(low, at), low)
+        high = jnp.where(at > HALO, jnp.minimum(high, at), high)
 
     def group(half):
         incoming = arriving(half)
@@ -251,8 +258,12 @@
                 featured(feat_h, taps_h[third], third * padded + p, keep_one, keep_two)
                 for third in range(3)
             )
-            put(mixed_h, p, rounded(key * val))
-            put(gout_h, p, rounded(vec(up_h, p) * query))
+            x = rounded(key * val)
+            g = rounded(vec(up_h, p) * query)
+            put(mixed_h, p, x)
+            put(gout_h, p, g)
+            put(last_mixed.at[half], p, x * flag(p >= low))
+            put(first_gout.at[half], p, g * flag(p < high))
             put(key_scr.at[half], p, key)
             put(val_scr.at[half], p, val)
             return carry
@@ -265,16 +276,12 @@
 
 
 def ends_kernel(
-    rows, groups, far_lengths, params, mixed, gout, payload, par_out,
-    lengths, par, stack, slab, zero_scr, length_sem, out_sems,
+    rows, groups, params, mixed, gout, payload, par_out, par, stack, slab, zero_scr, out_sems
 ):
     me = lax.axis_index("ctx")
-    base = me * rows
     count = payload.shape[0]
     poles = (par.shape[1] // SUB - 1) // 2
     extended = rows + HALO
-    get_lengths = pltpu.make_async_copy(far_lengths, lengths, length_sem)
-    get_lengths.start()
     zero_scr[...] = jnp.zeros((SUB, LANES), F32)
     zeros = [zero_scr[...]] * poles
 
@@ -283,12 +290,6 @@
         start_all(group_copies([par], [par_out], out_sems, half))
 
     each_group(groups, prepare)
-    get_lengths.wait()
-    low, high = jnp.int32(0), jnp.int32(extended)
-    for start in segment_starts(lengths):
-        at = start - base
-        low = jnp.where(at < rows, jnp.maximum(low, at), low)
-        high = jnp.where(at > HALO, jnp.minimum(high, at), high)
 
     def group(half):
         mixed_h, gout_h = mixed.at[half], gout.at[half]
@@ -297,8 +298,8 @@
         def sweep(i, carry):
             state, adjoint = carry
             back = extended - 1 - i
-            x = vec(mixed_h, i) * flag(i >= low)
-            g = vec(gout_h, back) * flag(back < high)
+            x = vec(mixed_h, i)
+            g = vec(gout_h, back)
             state = [decay[m] * state[m] + x for m in range(poles)]
             adjoint = [decay[m] * adjoint[m] + g for m in range(poles)]
             return state, adjoint
@@ -742,7 +743,7 @@
             pltpu.VMEM((groups, 3, rows, GROUP), BF16),
             pltpu.VMEM((groups, rows, GROUP), BF16),
         ]
-        + near(3 * padded, extended, 9, extended, extended)
+        + near(3 * padded, extended, extended, extended, 9, extended, extended)
         + [keep, sems(), sems(groups, 4), sems(groups, 7)],
         pl.CostEstimate(flops=5 * 10**9, bytes_accessed=4 * 10**7, transcendentals=0),
     )
@@ -750,18 +751,17 @@
     payload, par = call(
         functools.partial(ends_kernel, rows, groups),
         "ends",
-        [lengths, params, near_mixed, near_gout],
-        [hbm] + [vmem] * 3,
+        [params, near_mixed, near_gout],
+        [vmem] * 3,
         [
             jax.ShapeDtypeStruct((ctx_count, groups, state_rows, LANES), BF16),
             tall(2 * poles + 1),
         ],
         [vmem, hbm],
-        [small]
-        + near(2 * poles + 1)
+        near(2 * poles + 1)
         + [pltpu.VMEM((2, state_rows, LANES), BF16)]
         + [pltpu.VMEM((block[0], LANES), F32), scratch(1)]
-        + [sems(), sems(groups, 1)],
+        + [sems(groups, 1)],
     )
     arrived = swap(payload, "ctx")
     conv, adj, partial = call(

time: 71.8 us -> 71.3 us (level)
  Pallas kernels: 33.7 us -> 32 us
  waiting for transfers between devices: 10.5 us -> 11.5 us
    pallas_call x8, Pallas kernels: 33.7 us -> 32 us  [call(): pl.pallas_call(kernel, out_shape=outs, in_specs=in_specs, out_specs=out_s...]
    all_to_all x3, waiting for transfers between devices: 10.5 us -> 11.5 us  [swap(): return lax.all_to_all(block, axes, split_axis=0, concat_axis=0, tiled=True)]
where the time goes in v13:
time: 71.3 us; the launch traced here: 70.6 us
  Pallas kernels  32 us (45%)
  starting transfers between devices  20.2 us (28%)
  waiting for transfers between devices  11.5 us (16%)
  blocking collectives  6.17 us (9%)
  between operations  0.74 us (1%)
    pallas_call x8, Pallas kernels, call(): pl.pallas_call(kernel, out_shape=outs, in_specs=in_specs, out_specs=out_s...  32 us
    all_to_all x3, starting transfers between devices, swap(): return lax.all_to_all(block, axes, split_axis=0, concat_axis=0, tiled=True)  13.4 us
    all_to_all x3, waiting for transfers between devices, swap(): return lax.all_to_all(block, axes, split_axis=0, concat_axis=0, tiled=True)  11.5 us
    ppermute x2, starting transfers between devices, shifted(): return lax.ppermute(block, axis, route)  6.79 us
    all_gather x1, blocking collectives, per_device(): lax.all_gather(mine, 'dp')  6.17 us
  transfers between devices with their start and end apart: 5, of which 3 were waited for; matrix products, arithmetic and copies ran while one was open for 0% of the time, Pallas kernels for 28%

profile of v13, /device:TPU:0, one launch (start us, length us, event | category | flops | bytes accessed | tf_op | source)
XLA Modules:
  0.0 70.6 jit_solution(3397511197281288482)
XLA Ops:
  0.6 0.0 copy-start
  0.6 1.8 %start.1 = (bf16[8,104,128]{2,1,0:T(8,128)(2,1)}, bf16[2,6144]{1,0:T(2,128)(2,1)S(1)}, bf16[2,8192]{1,0:T(2,128)(2,1)S(1)}) custom-call(f32[16,256]{1,0:T(8,128)} %log_rate.1, f32[16,256]{1,0:T(8,128)} %residues.1, f32[1,256]{1,0:T(1,128)} %bitcast.4, bf16[1,128,6144]{2,1,0:T(8,128)(2,1)} %features.5, bf16[1,128,2048]{2,1,0:T(8,128)(2,1)} %upstream.3), custom_call_target="tpu_custom_call" | custom-call | tf_op jit(solution)/shard_map/start/pallas_call | solution.py:690
  2.5 1.3 %collective-permute-start.1 = (bf16[2,8192]{1,0:T(2,128)(2,1)S(1)}, bf16[2,8192]{1,0:T(2,128)(2,1)S(1)}, u32[]{:S(2)}, u32[]{:S(2)}) collective-permute-start(bf16[2,8192]{1,0:T(2,128)(2,1)S(1)} %get-tuple-element.28), channel_id=1, source_target_pairs={{1,0},{2,1},{3,2},{4,3},{5,4},{6,5},{7,6},{9,8},{10,9},{11,10},{12... | collective-permute-start | bytes 98312 | tf_op jit(solution)/shard_map/ppermute | solution.py:22
  3.8 5.5 %collective-permute-start = (bf16[2,6144]{1,0:T(2,128)(2,1)S(1)}, bf16[2,6144]{1,0:T(2,128)(2,1)S(1)}, u32[]{:S(2)}, u32[]{:S(2)}) collective-permute-start(bf16[2,6144]{1,0:T(2,128)(2,1)S(1)} %get-tuple-element.27), channel_id=1, source_target_pairs={{0,1},{1,2},{2,3},{3,4},{4,5},{5,6},{6,7},{8,9},{9,10},{10,11},{11... | collective-permute-start | bytes 73736 | tf_op jit(solution)/shard_map/ppermute | solution.py:22
  9.3 6.2 %all-to-all-start = ((bf16[8,104,128]{2,1,0:T(8,128)(2,1)}), bf16[8,104,128]{2,1,0:T(8,128)(2,1)S(1)}, u32[]{:S(2)}, u32[]{:S(2)}) async-start(bf16[8,104,128]{2,1,0:T(8,128)(2,1)} %get-tuple-element.30), calls=%async_computation | async-start | bytes 425984 | tf_op jit(solution)/shard_map/all_to_all | solution.py:646
  15.5 0.0 collective-permute-done.left
  15.5 0.0 collective-permute-done.1.right
  15.5 0.0 copy-done
  15.5 5.1 %features.4 = (f32[2,1040,128]{2,1,0:T(8,128)S(1)}, f32[2,1040,128]{2,1,0:T(8,128)S(1)}, f32[2,3168,128]{2,1,0:T(8,128)}, f32[2,1040,128]{2,1,0:T(8,128)}, f32[2...) custom-call(s32[1,8]{1,0:T(1,128)} %far_lengths.7, ...), custom_call_target="tpu_custom_call" | custom-call | flops 5000000000 | bytes 40000000 | tf_op jit(solution)/shard_map/features/pallas_call | solution.py:690
  20.6 2.8 %all-to-all-done.params = bf16[8,104,128]{2,1,0:T(8,128)(2,1)S(1)} async-done(((bf16[8,104,128]{2,1,0:T(8,128)(2,1)}), bf16[8,104,128]{2,1,0:T(8,128)(2,1)S(1)}, u32[]{:S(2)}, u32[]{:S(2)}) %all-to-all-start) | async-done | bytes 213024 | tf_op jit(solution)/shard_map/all_to_all | solution.py:646
  23.4 3.5 %ends.1 = (bf16[8,2,128,128]{3,2,1,0:T(8,128)(2,1)}, f32[2,264,128]{2,1,0:T(8,128)}) custom-call(bf16[8,104,128]{2,1,0:T(8,128)(2,1)S(1)} %all-to-all-done.params, f32[2,1040,128]{2,1,0:T(8,128)S(1)} %get-tuple-element.31.mixed, f32[2,1040,128]{2,1,0:T(8,128)S(1)} %get-tuple-element.32.gout), custom_call_target="tpu_custom_call" | custom-call | tf_op jit(solution)/shard_map/ends/pallas_call | solution.py:690
  26.9 3.5 %all-to-all-start.1 = ((bf16[8,2,128,128]{3,2,1,0:T(8,128)(2,1)}), bf16[8,2,128,128]{3,2,1,0:T(8,128)(2,1)S(1)}, u32[]{:S(2)}, u32[]{:S(2)}) async-start(bf16[8,2,128,128]{3,2,1,0:T(8,128)(2,1)} %get-tuple-element.33), calls=%async_computation.1 | async-start | bytes 1048576 | tf_op jit(solution)/shard_map/all_to_all | solution.py:646
  30.4 9.8 %local.1 = (f32[2,1040,128]{2,1,0:T(8,128)}, f32[2,1040,128]{2,1,0:T(8,128)}, f32[2,136,128]{2,1,0:T(8,128)}) custom-call(s32[1,8]{1,0:T(1,128)} %far_lengths.7, f32[2,1040,128]{2,1,0:T(8,128)} %get-tuple-element.35.mixed_in, f32[2,1040,128]{2,1,0:T(8,128)} %get-tuple-element.36.gout_in, f32[2,264,128]{2,1,0:T(8,128)} %get-tuple-element.34.par_in), custom_call_target="tpu_custom_call" | custom-call | tf_op jit(solution)/shard_map/local/pallas_call | solution.py:690
  40.2 3.3 %all-to-all-done.1.arrived = bf16[8,2,128,128]{3,2,1,0:T(8,128)(2,1)S(1)} async-done(((bf16[8,2,128,128]{3,2,1,0:T(8,128)(2,1)}), bf16[8,2,128,128]{3,2,1,0:T(8,128)(2,1)S(1)}, u32[]{:S(2)}, u32[]{:S(2)}) %all-to-all-start.1) | async-done | bytes 524320 | tf_op jit(solution)/shard_map/all_to_all | solution.py:646
  43.5 5.9 %sums.1 = (f32[2,1040,128]{2,1,0:T(8,128)}, f32[2,1040,128]{2,1,0:T(8,128)}, bf16[8,184,128]{2,1,0:T(8,128)(2,1)}) custom-call(s32[1,8]{1,0:T(1,128)} %far_lengths.7, bf16[8,2,128,128]{3,2,1,0:T(8,128)(2,1)S(1)} %all-to-all-done.1.arrived, f32[2,264,128]{2,1,0:T(8,128)} %get-tuple-element.34.par_in, f32[2,136,128]{2,1,0:T(8,128)} %get-tuple-element.37.partial_in, ...), custom_call_target="tpu_custom_call" | custom-call | tf_op jit(solution)/shard_map/sums/pallas_call | solution.py:690
  49.4 3.7 %all-to-all-start.2 = ((bf16[8,184,128]{2,1,0:T(8,128)(2,1)}), bf16[8,184,128]{2,1,0:T(8,128)(2,1)S(1)}, u32[]{:S(2)}, u32[]{:S(2)}) async-start(bf16[8,184,128]{2,1,0:T(8,128)(2,1)} %get-tuple-element.46), calls=%async_computation.2 | async-start | bytes 753664 | tf_op jit(solution)/shard_map/all_to_all | solution.py:646
  53.1 5.1 %grads.1 = bf16[1,128,6144]{2,1,0:T(8,128)(2,1)} custom-call(s32[1,8]{1,0:T(1,128)} %far_lengths.7, f32[2,72,128]{2,1,0:T(8,128)} %get-tuple-element.29.tap_in, f32[2,1040,128]{2,1,0:T(8,128)} %get-tuple-element.44.conv_in, f32[2,1040,128]{2,1,0:T(8,128)} %get-tuple-element.45.adj_in, f32[2,1040,128]{2,1,0:T(8,128)} %get-tuple-element.40.up_in, ...), custom_call_target="tpu_custom_call" | custom-call | tf_op jit(solution)/shard_map/grads/pallas_call | solution.py:690
  58.2 5.4 %all-to-all-done.2.parts = bf16[8,184,128]{2,1,0:T(8,128)(2,1)S(1)} async-done(((bf16[8,184,128]{2,1,0:T(8,128)(2,1)}), bf16[8,184,128]{2,1,0:T(8,128)(2,1)S(1)}, u32[]{:S(2)}, u32[]{:S(2)}) %all-to-all-start.2) | async-done | bytes 376864 | tf_op jit(solution)/shard_map/all_to_all | solution.py:646
  63.7 0.1 share.1
  63.7 6.2 %all-gather = bf16[736,128]{1,0:T(8,128)(2,1)S(1)} all-gather(bf16[184,128]{1,0:T(8,128)(2,1)S(1)} %share.1), channel_id=2, replica_groups=mesh['dp'=4,'ctx'=8] {'dp'}, dimensions={0}, use_global_device_ids=true | all-gather | bytes 235520 | tf_op jit(solution)/shard_map/all_gather | solution.py:818
  69.9 0.7 %emit.1 = (f32[3,6144]{1,0:T(4,128)}, f32[16,256]{1,0:T(8,128)}, f32[1,256]{1,0:T(1,128)}) custom-call(bf16[4,184,128]{2,1,0:T(8,128)(2,1)S(1)} %bitcast.3), custom_call_target="tpu_custom_call" | custom-call | tf_op jit(solution)/shard_map/emit/pallas_call | solution.py:690
Async XLA Ops:
  0.6 14.9 %copy-start = (f32[3,6144]{1,0:T(4,128)S(1)}, f32[3,6144]{1,0:T(4,128)}, u32[]{:S(2)}) copy-start(f32[3,6144]{1,0:T(4,128)} %taps.1) | copy-start | bytes 221188
  2.5 13.0 %collective-permute-start.1 = (bf16[2,8192]{1,0:T(2,128)(2,1)S(1)}, bf16[2,8192]{1,0:T(2,128)(2,1)S(1)}, u32[]{:S(2)}, u32[]{:S(2)}) collective-permute-start(bf16[2,8192]{1,0:T(2,128)(2,1)S(1)} %get-tuple-element.28), channel_id=1, source_target_pairs={{1,0},{2,1},{3,2},{4,3},{5,4},{6,5},{7,6},{9,8},{10,9},{11,10},{12... | collective-permute-start | bytes 98312 | tf_op jit(solution)/shard_map/ppermute | solution.py:22
  3.8 11.7 %collective-permute-start = (bf16[2,6144]{1,0:T(2,128)(2,1)S(1)}, bf16[2,6144]{1,0:T(2,128)(2,1)S(1)}, u32[]{:S(2)}, u32[]{:S(2)}) collective-permute-start(bf16[2,6144]{1,0:T(2,128)(2,1)S(1)} %get-tuple-element.27), channel_id=1, source_target_pairs={{0,1},{1,2},{2,3},{3,4},{4,5},{5,6},{6,7},{8,9},{9,10},{10,11},{11... | collective-permute-start | bytes 73736 | tf_op jit(solution)/shard_map/ppermute | solution.py:22
  9.3 14.1 %all-to-all-start = ((bf16[8,104,128]{2,1,0:T(8,128)(2,1)}), bf16[8,104,128]{2,1,0:T(8,128)(2,1)S(1)}, u32[]{:S(2)}, u32[]{:S(2)}) async-start(bf16[8,104,128]{2,1,0:T(8,128)(2,1)} %get-tuple-element.30), calls=%async_computation | async-start | bytes 425984 | tf_op jit(solution)/shard_map/all_to_all | solution.py:646
  26.9 16.6 %all-to-all-start.1 = ((bf16[8,2,128,128]{3,2,1,0:T(8,128)(2,1)}), bf16[8,2,128,128]{3,2,1,0:T(8,128)(2,1)S(1)}, u32[]{:S(2)}, u32[]{:S(2)}) async-start(bf16[8,2,128,128]{3,2,1,0:T(8,128)(2,1)} %get-tuple-element.33), calls=%async_computation.1 | async-start | bytes 1048576 | tf_op jit(solution)/shard_map/all_to_all | solution.py:646
  49.4 14.3 %all-to-all-start.2 = ((bf16[8,184,128]{2,1,0:T(8,128)(2,1)}), bf16[8,184,128]{2,1,0:T(8,128)(2,1)S(1)}, u32[]{:S(2)}, u32[]{:S(2)}) async-start(bf16[8,184,128]{2,1,0:T(8,128)(2,1)} %get-tuple-element.46), calls=%async_computation.2 | async-start | bytes 753664 | tf_op jit(solution)/shard_map/all_to_all | solution.py:646
